TPU v7x, 32 devices: a whole 2x2x4 slice. The times are simulated.
32 devices in a mesh: band: 32 (over z, y, x, core).
Axes of the slice: x: 2, y: 2, z: 4, core: 2. Of those that a mesh axis runs over, the one named last changes fastest.
Arguments:
- orbitals: float32 [32, 64, 4096], P('band'), may hold values from -6 to 6
- kernel_values: float32 [32], replicated, may hold values from 0.2 to 4
- shell_index: int32 [64, 4096], replicated, may hold values from 0 to 31, as said below
Outputs:
- exchange_term: float32 [32, 64, 4096], P('band')
- margin: float32 [32, 32], P('band')
Inputs may be any that keep to these rules, and one draw needn't show every extreme that they name: `shell_index`: the class of a wave vector is unchanged when any one of its indices a is replaced by (64 - a) mod 64.
All inputs are finite; a program needn't handle non-finite values.
Results may differ from a plain program's by a relative error of at most 0.0003.
Values sent between devices are 32-bit elements; how exact they have to be, the bound alone decides.
No kernel may reach another device: no remote copies, remote signals or barrier semaphores. Data moves between devices by JAX's collectives and lax.ppermute only.
A program may use at most 64 MiB of HBM per device.

v0:
```python
import functools

import jax
import jax.numpy as jnp
import ml_dtypes
import numpy as np
from jax import lax
from jax.experimental import pallas as pl
from jax.experimental.pallas import tpu as pltpu
from jax.sharding import PartitionSpec as P

CHUNKS = 2
LANES = 128
SUBLANES = 8
f32, bf16 = jnp.float32, jnp.bfloat16
VMEM = pl.BlockSpec(memory_space=pltpu.VMEM)


def tables(g):
    index = np.arange(g)
    angle = 2.0 * np.pi / g * (np.outer(index, index) % g)
    cas = np.cos(angle) + np.sin(angle)
    hi = cas.astype(np.float32).astype(ml_dtypes.bfloat16)
    lo = (cas - hi.astype(np.float64)).astype(np.float32).astype(ml_dtypes.bfloat16)
    rows = np.concatenate([hi, hi, lo], axis=1)
    eye = np.eye(LANES // g, dtype=np.float32)
    wide_hi = np.kron(eye, hi.astype(np.float32)).astype(ml_dtypes.bfloat16)
    wide_lo = np.kron(eye, lo.astype(np.float32)).astype(ml_dtypes.bfloat16)
    lanes = np.block([[wide_hi, wide_lo], [wide_hi, np.zeros_like(wide_lo)]])
    return jnp.asarray(rows), jnp.asarray(lanes)


def split(value):
    hi = value.astype(bf16)
    lo = (value - hi.astype(f32)).astype(bf16)
    return hi, lo


def rows_pass(table, value):
    hi, lo = split(value)
    stacked = jnp.concatenate([hi, lo, hi], axis=0)
    return jnp.dot(table, stacked, preferred_element_type=f32)


def lanes_pass(value, table):
    hi, lo = split(value)
    both = jnp.concatenate([hi, lo], axis=1)
    result = jnp.dot(both, table, preferred_element_type=f32)
    return result[:, :LANES] + result[:, LANES:]


def exchange_halves(value, g):
    half = g // 2
    low = lax.broadcasted_iota(jnp.int32, (half, LANES), 1) < g
    parts = []
    for start in range(0, value.shape[0], g):
        first = value[start : start + half]
        second = value[start + half : start + g]
        parts.append(jnp.where(low, first, pltpu.roll(second, g, 1)))
        parts.append(jnp.where(low, pltpu.roll(first, g, 1), second))
    return jnp.concatenate(parts, axis=0)


def pair_kernel(g, n_right, n_other, has_acc, tiled, *refs):
    refs = list(refs)
    left = refs.pop(0)
    right_refs = [refs.pop(0) for _ in range(n_right)]
    other_refs = [refs.pop(0) for _ in range(n_other)]
    flag = refs.pop(0) if n_other else None
    acc = refs.pop(0) if has_acc else None
    kern, rows_table, lanes_table = refs[:3]
    out = refs[3]
    tiles = refs[4] if tiled else None
    work = refs[-1]
    half = g // 2
    width = 2 * LANES
    table = rows_table[...]
    wide = lanes_table[...]

    def load(parts, cols):
        return jnp.concatenate([part[:, cols] for part in parts], axis=0)

    def right_block(cols):
        value = load(right_refs, cols)
        if n_other:
            value = jnp.where(flag[0] > 0, value, load(other_refs, cols))
        return value

    for step in range(g * g // width):
        cols = slice(step * width, (step + 1) * width)
        first = rows_pass(table, left[:, cols] * right_block(cols))
        first = jnp.concatenate([first[:, :LANES], first[:, LANES:]], axis=0)
        second = exchange_halves(lanes_pass(first, wide), g)
        work[step * 2 * g : (step + 1) * 2 * g, :] = second

    for step in range(half // 2):
        plane = 2 * step
        value = jnp.concatenate(
            [work[pl.ds(plane + k, g, stride=half), :] for k in range(2)], axis=1
        )
        scale = kern[plane * g : (plane + 2) * g, :]
        scale = jnp.concatenate([scale[:g], scale[g:]], axis=1)
        value = rows_pass(table, rows_pass(table, value) * scale)
        for k in range(2):
            work[pl.ds(plane + k, g, stride=half), :] = value[:, k * LANES : (k + 1) * LANES]

    for step in range(g * g // width):
        cols = slice(step * width, (step + 1) * width)
        value = exchange_halves(lanes_pass(work[step * 2 * g : (step + 1) * 2 * g, :], wide), g)
        value = rows_pass(table, jnp.concatenate([value[:g], value[g:]], axis=1))
        value = value * right_block(cols)
        if has_acc:
            value = acc[:, cols] + value
        out[:, cols] = value
        if tiled:
            tiles[2 * step * g : (2 * step + 1) * g, :] = value[:, :LANES]
            tiles[(2 * step + 1) * g : (2 * step + 2) * g, :] = value[:, LANES:]


def pair(left, right, acc, kern, consts, other=(), flag=None, tiled=False):
    g = left.shape[0]
    operands = [left, *right, *other]
    specs = [VMEM] * len(operands)
    if other:
        operands.append(flag)
        specs.append(pl.BlockSpec(memory_space=pltpu.SMEM))
    if acc is not None:
        operands.append(acc)
        specs.append(VMEM)
    operands += [kern, *consts]
    specs += [VMEM] * 3
    shapes = [jax.ShapeDtypeStruct(left.shape, f32)]
    if tiled:
        shapes.append(jax.ShapeDtypeStruct((g * g * g // LANES, LANES), f32))
    points = g**3
    result = pl.pallas_call(
        functools.partial(pair_kernel, g, len(right), len(other), acc is not None, tiled),
        out_shape=shapes,
        in_specs=specs,
        out_specs=[VMEM] * len(shapes),
        scratch_shapes=[pltpu.VMEM((points // LANES, LANES), f32)],
        compiler_params=pltpu.CompilerParams(vmem_limit_bytes=32 * 2**20),
        cost_estimate=pl.CostEstimate(
            flops=12 * points * LANES * 6, bytes_accessed=16 * points, transcendentals=0
        ),
    )(*operands)
    return result if tiled else result[0]


def lookup_kernel(scale, values, index, out):
    rows = values[...]
    size = index.shape[0] // 16
    for step in range(16):
        part = index[step * size : (step + 1) * size, :]
        table = jnp.broadcast_to(rows, part.shape)
        out[step * size : (step + 1) * size, :] = jnp.take_along_axis(table, part, axis=1) * scale


def lookup(kernel_values, shell_index):
    g = shell_index.shape[0]
    classes = kernel_values.shape[0]
    index = shell_index.reshape(2, g // 2, g, g).transpose(1, 2, 0, 3).reshape(-1, LANES)
    padded = jnp.pad(kernel_values, (0, LANES - classes)).reshape(1, LANES)
    return pl.pallas_call(
        functools.partial(lookup_kernel, -1.0 / g**3),
        out_shape=jax.ShapeDtypeStruct(index.shape, f32),
        in_specs=[VMEM] * 2,
        out_specs=VMEM,
    )(padded, index)


def margin_kernel(scale, orbitals, terms, out):
    count = orbitals.shape[0]
    lefts, rights = [], []
    for step in range(orbitals.shape[1] // SUBLANES):
        rows = slice(step * SUBLANES, (step + 1) * SUBLANES)
        a_hi, a_lo = split(orbitals[:, rows, :].reshape(count * SUBLANES, LANES))
        b_hi, b_lo = split(terms[:, rows, :].reshape(count * SUBLANES, LANES))
        lefts += [a_hi, a_lo, a_hi]
        rights += [b_hi, b_hi, b_lo]
    products = lax.dot_general(
        jnp.concatenate(lefts, axis=1),
        jnp.concatenate(rights, axis=1),
        (((1,), (1,)), ((), ())),
        preferred_element_type=f32,
    )
    size = count * SUBLANES
    row = lax.broadcasted_iota(jnp.int32, (size, size), 0) % SUBLANES
    col = lax.broadcasted_iota(jnp.int32, (size, size), 1) % SUBLANES
    kept = jnp.where(row == col, products, 0.0)
    summed = jnp.sum(kept.reshape(count, SUBLANES, size), axis=1)
    pick_row = lax.broadcasted_iota(jnp.int32, (size, count), 0) // SUBLANES
    pick_col = lax.broadcasted_iota(jnp.int32, (size, count), 1)
    pick = (pick_row == pick_col).astype(f32)
    out[...] = scale * jnp.dot(
        summed, pick, precision=lax.Precision.HIGHEST, preferred_element_type=f32
    )


def partial_margin(orbitals, terms, points):
    count = orbitals.shape[0]
    return pl.pallas_call(
        functools.partial(margin_kernel, 1.0 / points),
        out_shape=jax.ShapeDtypeStruct((count, count), f32),
        in_specs=[VMEM] * 2,
        out_specs=VMEM,
        compiler_params=pltpu.CompilerParams(vmem_limit_bytes=48 * 2**20),
    )(orbitals, terms)


def permute(value, target, count):
    return lax.ppermute(value, "band", [(source, target(source) % count) for source in range(count)])


def far_target(source):
    return source - 4 if (source // 2) % 2 else source + 4


def local(orbitals, kernel_values, shell_index):
    count = lax.axis_size("band")
    me = lax.axis_index("band")
    g = shell_index.shape[0]
    points = g**3
    consts = tables(g)
    own = orbitals.reshape(g, g * g)

    size = g // CHUNKS
    near = [permute(own[k * size : (k + 1) * size], lambda d: d ^ 2, count) for k in range(CHUNKS)]
    peer = permute(own, lambda d: d ^ 1, count)
    far = [permute(part, far_target, count) for part in near]
    near_cross = [permute(part, lambda d: d ^ 1, count) for part in near]
    far_cross = [permute(part, lambda d: d ^ 1, count) for part in far]
    use_near = (((me + 1) // 2) % 2).astype(jnp.int32).reshape(1)

    kern = lookup(kernel_values, shell_index)
    by_tile = own.reshape(g, g * g // LANES, LANES).transpose(1, 0, 2).reshape(count, -1, LANES)
    spread_orbitals = lax.all_to_all(by_tile, "band", split_axis=0, concat_axis=0, tiled=True)

    term = pair(own, [own], None, kern, consts)
    term = pair(own, [peer], term, kern, consts)
    term = pair(own, near, term, kern, consts)
    term = pair(own, far, term, kern, consts)
    term, tiles = pair(own, near_cross, term, kern, consts, far_cross, use_near, tiled=True)

    spread_terms = lax.all_to_all(
        tiles.reshape(count, -1, LANES), "band", split_axis=0, concat_axis=0, tiled=True
    )
    rows = partial_margin(spread_orbitals, spread_terms, points)
    rows = lax.all_to_all(rows, "band", split_axis=0, concat_axis=0, tiled=True)
    margin = jnp.sum(rows, axis=0, keepdims=True)
    return term.reshape(orbitals.shape), margin


def solution(mesh):
    return jax.shard_map(
        local,
        mesh=mesh,
        in_specs=(P("band", None, None), P(), P()),
        out_specs=(P("band", None, None), P("band", None)),
        check_vma=False,
    )
```

profile of v0, /device:TPU:0, one launch (start us, length us, event | category | flops | bytes accessed | tf_op | source)
XLA Modules:
  0.0 139.1 jit_solution(8015689401742571324)
XLA Ops:
  0.6 1.4 %copy.13 = f32[8,8,32,128]{3,2,1,0:T(8,128)S(1)} copy(f32[8,8,32,128]{3,1,2,0:T(8,128)} %bitcast.23) | data formatting | bytes 2097152
  2.0 0.0 copy-start
  2.1 1.6 %copy.17 = f32[64,32,128]{2,0,1:T(8,128)} copy(f32[64,32,128]{2,1,0:T(8,128)S(1)} %bitcast.34) | data formatting | bytes 2097152 | tf_op jit(solution)/shard_map/reshape;reshape | solution.py:236
  3.6 7.3 %all-to-all-start = ((f32[32,64,128]{2,1,0:T(8,128)}), f32[32,64,128]{2,1,0:T(8,128)S(1)}, u32[]{:S(2)}, u32[]{:S(2)}) async-start(f32[32,64,128]{2,1,0:T(8,128)} %bitcast.22), calls=%async_computation | async-start | bytes 2097152 | tf_op jit(solution)/shard_map/all_to_all | solution.py:237
  10.9 0.0 copy-done
  11.0 0.1 slice_bitcast_fusion
  11.0 1.8 %collective-permute-start = (f32[32,4096]{1,0:T(8,128)S(1)}, f32[32,4096]{1,0:T(8,128)}, u32[]{:S(2)}, u32[]{:S(2)}) collective-permute-start(f32[32,4096]{1,0:T(8,128)S(1)} %get-tuple-element.7), channel_id=1, source_target_pairs={{0,2},{1,3},{2,0},{3,1},{4,6},{5,7},{6,4},{7,5},{8,10},{9,11},{10,... | collective-permute-start | bytes 1572872 | tf_op jit(solution)/shard_map/ppermute | solution.py:212
  12.9 0.3 collective-permute-start.2
  13.1 0.0 collective-permute-start.8
  13.1 23.7 %collective-permute-done.refs_1_ = f32[32,4096]{1,0:T(8,128)} collective-permute-done((f32[32,4096]{1,0:T(8,128)S(1)}, f32[32,4096]{1,0:T(8,128)}, u32[]{:S(2)}, u32[]{:S(2)}) %collective-permute-start) | collective-permute-done | bytes 524320 | tf_op jit(solution)/shard_map/ppermute | solution.py:212
  36.9 1.5 %collective-permute-start.4 = (f32[32,4096]{1,0:T(8,128)}, f32[32,4096]{1,0:T(8,128)}, u32[]{:S(2)}, u32[]{:S(2)}) collective-permute-start(f32[32,4096]{1,0:T(8,128)} %collective-permute-done.refs_1_), channel_id=1, source_target_pairs={{0,4},{1,5},{2,30},{3,31},{4,8},{5,9},{6,2},{7,3},{8,12},{9,13},{1... | collective-permute-start | bytes 1572872 | tf_op jit(solution)/shard_map/ppermute | solution.py:212
  38.3 9.3 %collective-permute-done.2.refs_2_ = f32[32,4096]{1,0:T(8,128)} collective-permute-done((f32[32,4096]{1,0:T(8,128)S(1)}, f32[32,4096]{1,0:T(8,128)}, u32[]{:S(2)}, u32[]{:S(2)}) %collective-permute-start.2) | collective-permute-done | bytes 524320 | tf_op jit(solution)/shard_map/ppermute | solution.py:212
  47.6 1.5 %collective-permute-start.6 = (f32[32,4096]{1,0:T(8,128)}, f32[32,4096]{1,0:T(8,128)}, u32[]{:S(2)}, u32[]{:S(2)}) collective-permute-start(f32[32,4096]{1,0:T(8,128)} %collective-permute-done.2.refs_2_), channel_id=1, source_target_pairs={{0,4},{1,5},{2,30},{3,31},{4,8},{5,9},{6,2},{7,3},{8,12},{9,13},{1... | collective-permute-start | bytes 1572872 | tf_op jit(solution)/shard_map/ppermute | solution.py:212
  49.1 3.1 %reshape.32 = s32[2,32,64,64]{3,2,1,0:T(8,128)} reshape(s32[64,4096]{1,0:T(8,128)} %param.7) | data formatting | bytes 2097152 | tf_op jit(solution)/shard_map/reshape | solution.py:162
  52.2 4.6 %copy.16 = s32[2,32,64,64]{3,0,2,1:T(2,128)} copy(s32[2,32,64,64]{3,2,1,0:T(8,128)} %reshape.32) | data formatting | bytes 2097152 | tf_op jit(solution)/shard_map/reshape | solution.py:162
  56.8 0.0 copy-start.4
  56.8 0.0 copy-start.2
  56.8 0.0 copy-start.3
  56.8 3.4 %reshape.33.index = s32[2048,128]{1,0:T(8,128)} reshape(s32[32,64,2,64]{3,2,1,0:T(2,128)} %bitcast.33) | data formatting | bytes 2097152 | tf_op jit(solution)/shard_map/reshape | solution.py:162
  60.1 0.0 copy-done.4
  60.1 0.5 pad_bitcast_fusion.values
  60.7 3.0 %shard_map.68.refs_2_.refs_3_.refs_4_.refs_7_ = f32[2048,128]{1,0:T(8,128)} custom-call(f32[1,128]{1,0:T(1,128)} %pad_bitcast_fusion.values, s32[2048,128]{1,0:T(8,128)} %reshape.33.index), custom_call_target="tpu_custom_call" | custom-call | tf_op jit(solution)/shard_map/pallas_call | solution.py:164
  63.7 0.0 copy-done.2
  63.7 0.0 copy-done.3
  63.7 0.0 copy-start.1
  63.7 1.2 copy-done.1
  64.9 5.5 %shard_map.69.refs_2_ = f32[64,4096]{1,0:T(8,128)S(1)} custom-call(f32[64,4096]{1,0:T(8,128)S(1)} %bitcast.25, f32[64,4096]{1,0:T(8,128)S(1)} %bitcast.26, f32[2048,128]{1,0:T(8,128)S(1)} %copy-done.1, bf16[64,192]{1,0:T(8,128)(2,1)S(1)} %copy-done.3, bf16[256,256]{1,0:T(8,128)(2,1)S(1)} %copy-done.2), custom_call_target="tpu_custom_call" | custom-call | flops 2415919104 | bytes 4194304 | tf_op jit(solution)/shard_map/pallas_call | solution.py:136
  70.4 0.1 collective-permute-start.1
  70.5 0.5 collective-permute-start.3
  71.0 0.0 collective-permute-done.4.refs_1_
  71.0 0.1 collective-permute-start.5
  71.1 0.0 collective-permute-done.6.refs_2_
  71.1 0.4 collective-permute-start.7
  71.5 0.0 collective-permute-done.8.refs_1_
  71.5 5.5 %shard_map.70.refs_3_ = f32[64,4096]{1,0:T(8,128)S(1)} custom-call(f32[64,4096]{1,0:T(8,128)S(1)} %bitcast.27, f32[64,4096]{1,0:T(8,128)S(1)} %collective-permute-done.8.refs_1_, f32[64,4096]{1,0:T(8,128)S(1)} %shard_map.69.refs_2_, f32[2048,128]{1,0:T(8,128)S(1)} %copy-done.1, bf16[64,192]{1,0:T(8,128)(2,1)S(1)} %copy-done.3, bf16[256,256]{1,0:T(8,128)(2,1)S(1)} %copy-done.2), custom_call_target="tpu_custom_call" | custom-call | flops 2415919104 | bytes 4194304 | tf_op jit(solution)/shard_map/pallas_call | solution.py:136
  77.1 6.9 %shard_map.71.refs_3_ = f32[64,4096]{1,0:T(8,128)S(1)} custom-call(f32[64,4096]{1,0:T(8,128)S(1)} %bitcast.28, f32[32,4096]{1,0:T(8,128)} %collective-permute-done.refs_1_, f32[32,4096]{1,0:T(8,128)} %collective-permute-done.2.refs_2_, f32[64,4096]{1,0:T(8,128)S(1)} %shard_map.70.refs_3_, f32[2048,128]{1,0:T(8,128)S(1)} %copy-done.1, ...), custom_call_target="tpu_custom_call" | custom-call | flops 2415919104 | bytes 4194304 | tf_op jit(solution)/shard_map/pallas_call | solution.py:136
  84.0 6.7 %shard_map.72.refs_6_ = f32[64,4096]{1,0:T(8,128)S(1)} custom-call(f32[64,4096]{1,0:T(8,128)S(1)} %bitcast.29, f32[32,4096]{1,0:T(8,128)} %collective-permute-done.4.refs_1_, f32[32,4096]{1,0:T(8,128)} %collective-permute-done.6.refs_2_, f32[64,4096]{1,0:T(8,128)S(1)} %shard_map.71.refs_3_, f32[2048,128]{1,0:T(8,128)S(1)} %copy-done.1, ...), custom_call_target="tpu_custom_call" | custom-call | flops 2415919104 | bytes 4194304 | tf_op jit(solution)/shard_map/pallas_call | solution.py:136
  90.7 0.0 collective-permute-done.1.refs_1_
  90.7 0.0 collective-permute-done.3.refs_2_
  90.7 0.0 collective-permute-done.5.refs_3_
  90.8 0.0 collective-permute-done.7.refs_4_
  90.8 6.5 %shard_map.73 = (f32[64,4096]{1,0:T(8,128)}, f32[2048,128]{1,0:T(8,128)S(1)}) custom-call(f32[64,4096]{1,0:T(8,128)S(1)} %bitcast.30, f32[32,4096]{1,0:T(8,128)S(1)} %collective-permute-done.1.refs_1_, f32[32,4096]{1,0:T(8,128)S(1)} %collective-permute-done.3.refs_2_, f32[32,4096]{1,0:T(8,128)S(1)} %collective-permute-done.5.refs_3_, ...), custom_call_target="tpu_custom_call" | custom-call | flops 2415919104 | bytes 4194304 | tf_op jit(solution)/shard_map/pallas_call | solution.py:136
  97.3 0.0 all-to-all-done.orbitals
  97.3 29.7 %all_to_all.19.terms = f32[32,64,128]{2,1,0:T(8,128)S(1)} all-to-all(f32[32,64,128]{2,1,0:T(8,128)S(1)} %bitcast.31), channel_id=1, replica_groups=mesh['band'=32] {'band'}, dimensions={0} | all-to-all | bytes 2097152 | tf_op jit(solution)/shard_map/all_to_all | solution.py:245
  127.0 0.9 shard_map.74
  127.9 10.6 %all_to_all.20 = f32[32,1,32]{2,1,0:T(1,128)S(1)} all-to-all(f32[32,1,32]{2,1,0:T(1,128)S(1)} %bitcast.32), channel_id=1, replica_groups=mesh['band'=32] {'band'}, dimensions={0} | all-to-all | bytes 8192 | tf_op jit(solution)/shard_map/all_to_all | solution.py:249
  138.5 0.6 reduce_sum.9
Async XLA Ops:
  2.0 8.9 %copy-start = (f32[1,64,4096]{2,1,0:T(8,128)S(1)}, f32[1,64,4096]{2,1,0:T(8,128)}, u32[]{:S(2)}) copy-start(f32[1,64,4096]{2,1,0:T(8,128)} %param.5) | copy-start | bytes 3145732
  3.6 93.6 %all-to-all-start = ((f32[32,64,128]{2,1,0:T(8,128)}), f32[32,64,128]{2,1,0:T(8,128)S(1)}, u32[]{:S(2)}, u32[]{:S(2)}) async-start(f32[32,64,128]{2,1,0:T(8,128)} %bitcast.22), calls=%async_computation | async-start | bytes 2097152 | tf_op jit(solution)/shard_map/all_to_all | solution.py:237
  11.0 25.8 %collective-permute-start = (f32[32,4096]{1,0:T(8,128)S(1)}, f32[32,4096]{1,0:T(8,128)}, u32[]{:S(2)}, u32[]{:S(2)}) collective-permute-start(f32[32,4096]{1,0:T(8,128)S(1)} %get-tuple-element.7), channel_id=1, source_target_pairs={{0,2},{1,3},{2,0},{3,1},{4,6},{5,7},{6,4},{7,5},{8,10},{9,11},{10,... | collective-permute-start | bytes 1572872 | tf_op jit(solution)/shard_map/ppermute | solution.py:212
  12.9 34.8 %collective-permute-start.2 = (f32[32,4096]{1,0:T(8,128)S(1)}, f32[32,4096]{1,0:T(8,128)}, u32[]{:S(2)}, u32[]{:S(2)}) collective-permute-start(f32[32,4096]{1,0:T(8,128)S(1)} %get-tuple-element.6), channel_id=1, source_target_pairs={{0,2},{1,3},{2,0},{3,1},{4,6},{5,7},{6,4},{7,5},{8,10},{9,11},{10,... | collective-permute-start | bytes 1572872 | tf_op jit(solution)/shard_map/ppermute | solution.py:212
  13.1 58.4 %collective-permute-start.8 = (f32[64,4096]{1,0:T(8,128)S(1)}, f32[64,4096]{1,0:T(8,128)S(1)}, u32[]{:S(2)}, u32[]{:S(2)}) collective-permute-start(f32[64,4096]{1,0:T(8,128)S(1)} %bitcast.24), channel_id=1, source_target_pairs={{0,1},{1,0},{2,3},{3,2},{4,5},{5,4},{6,7},{7,6},{8,9},{9,8},{10,11... | collective-permute-start | bytes 3145736 | tf_op jit(solution)/shard_map/ppermute | solution.py:212
  36.9 34.1 %collective-permute-start.4 = (f32[32,4096]{1,0:T(8,128)}, f32[32,4096]{1,0:T(8,128)}, u32[]{:S(2)}, u32[]{:S(2)}) collective-permute-start(f32[32,4096]{1,0:T(8,128)} %collective-permute-done.refs_1_), channel_id=1, source_target_pairs={{0,4},{1,5},{2,30},{3,31},{4,8},{5,9},{6,2},{7,3},{8,12},{9,13},{1... | collective-permute-start | bytes 1572872 | tf_op jit(solution)/shard_map/ppermute | solution.py:212
  47.6 23.5 %collective-permute-start.6 = (f32[32,4096]{1,0:T(8,128)}, f32[32,4096]{1,0:T(8,128)}, u32[]{:S(2)}, u32[]{:S(2)}) collective-permute-start(f32[32,4096]{1,0:T(8,128)} %collective-permute-done.2.refs_2_), channel_id=1, source_target_pairs={{0,4},{1,5},{2,30},{3,31},{4,8},{5,9},{6,2},{7,3},{8,12},{9,13},{1... | collective-permute-start | bytes 1572872 | tf_op jit(solution)/shard_map/ppermute | solution.py:212
  56.8 3.4 %copy-start.4 = (f32[32]{0:T(128)S(1)}, f32[32]{0:T(128)}, u32[]{:S(2)}) copy-start(f32[32]{0:T(128)} %param.6) | copy-start | bytes 388
  56.8 6.9 %copy-start.2 = (bf16[256,256]{1,0:T(8,128)(2,1)S(1)}, bf16[256,256]{1,0:T(8,128)(2,1)}, u32[]{:S(2)}) copy-start(bf16[256,256]{1,0:T(8,128)(2,1)} %constant.38.clone.refs_4_.refs_5_.refs_6_.refs_9_) | copy-start | bytes 393220
  56.8 6.9 %copy-start.3 = (bf16[64,192]{1,0:T(8,128)(2,1)S(1)}, bf16[64,192]{1,0:T(8,128)(2,1)}, u32[]{:S(2)}) copy-start(bf16[64,192]{1,0:T(8,128)(2,1)} %constant.37.clone.refs_3_.refs_4_.refs_5_.refs_8_) | copy-start | bytes 73732
  63.7 1.2 copy-start.1
  70.4 20.3 %collective-permute-start.1 = (f32[32,4096]{1,0:T(8,128)}, f32[32,4096]{1,0:T(8,128)S(1)}, u32[]{:S(2)}, u32[]{:S(2)}) collective-permute-start(f32[32,4096]{1,0:T(8,128)} %collective-permute-done.refs_1_), channel_id=1, source_target_pairs={{0,1},{1,0},{2,3},{3,2},{4,5},{5,4},{6,7},{7,6},{8,9},{9,8},{10,11... | collective-permute-start | bytes 1572872 | tf_op jit(solution)/shard_map/ppermute | solution.py:212
  70.5 20.2 %collective-permute-start.3 = (f32[32,4096]{1,0:T(8,128)}, f32[32,4096]{1,0:T(8,128)S(1)}, u32[]{:S(2)}, u32[]{:S(2)}) collective-permute-start(f32[32,4096]{1,0:T(8,128)} %collective-permute-done.2.refs_2_), channel_id=1, source_target_pairs={{0,1},{1,0},{2,3},{3,2},{4,5},{5,4},{6,7},{7,6},{8,9},{9,8},{10,11... | collective-permute-start | bytes 1572872 | tf_op jit(solution)/shard_map/ppermute | solution.py:212
  71.0 19.7 %collective-permute-start.5 = (f32[32,4096]{1,0:T(8,128)}, f32[32,4096]{1,0:T(8,128)S(1)}, u32[]{:S(2)}, u32[]{:S(2)}) collective-permute-start(f32[32,4096]{1,0:T(8,128)} %collective-permute-done.4.refs_1_), channel_id=1, source_target_pairs={{0,1},{1,0},{2,3},{3,2},{4,5},{5,4},{6,7},{7,6},{8,9},{9,8},{10,11... | collective-permute-start | bytes 1572872 | tf_op jit(solution)/shard_map/ppermute | solution.py:212
  71.1 19.7 %collective-permute-start.7 = (f32[32,4096]{1,0:T(8,128)}, f32[32,4096]{1,0:T(8,128)S(1)}, u32[]{:S(2)}, u32[]{:S(2)}) collective-permute-start(f32[32,4096]{1,0:T(8,128)} %collective-permute-done.6.refs_2_), channel_id=1, source_target_pairs={{0,1},{1,0},{2,3},{3,2},{4,5},{5,4},{6,7},{7,6},{8,9},{9,8},{10,11... | collective-permute-start | bytes 1572872 | tf_op jit(solution)/shard_map/ppermute | solution.py:212
where the time goes:
time: 140 us; the launch traced here: 139 us
  blocking collectives  40.3 us (29%)
  Pallas kernels  35.1 us (25%)
  waiting for transfers between devices  33 us (24%)
  local copies, waits for them, and re-layouts  15.9 us (11%)
  starting transfers between devices  13.4 us (10%)
    ppermute x9, waiting for transfers between devices, permute(): lax.ppermute(value, 'band', [(source, target(source) % count) for source...  33 us
    pallas_call x5, Pallas kernels, pair(): pl.pallas_call(functools.partial(pair_kernel, g, len(right), len(other),...  31.2 us
    all_to_all x1, blocking collectives, local(): lax.all_to_all(tiles.reshape(count, -1, LANES), 'band', split_axis=0, con...  29.7 us
    reshape x3, local copies, waits for them, and re-layouts, lookup(): shell_index.reshape(2, g // 2, g, g).transpose(1, 2, 0, 3)  11.1 us
    all_to_all x1, blocking collectives, local(): rows = lax.all_to_all(rows, 'band', split_axis=0, concat_axis=0, tiled=True)  10.6 us
    all_to_all x1, starting transfers between devices, local(): lax.all_to_all(by_tile, 'band', split_axis=0, concat_axis=0, tiled=True)  7.3 us
    ppermute x9, starting transfers between devices, permute(): lax.ppermute(value, 'band', [(source, target(source) % count) for source...  6.1 us
    pallas_call x1, Pallas kernels, lookup(): pl.pallas_call(functools.partial(lookup_kernel, -1.0 / g ** 3), out_shape...  2.99 us
  transfers between devices with their start and end apart: 10, of which 2 were waited for; matrix products, arithmetic and copies ran while one was open for 8% of the time, Pallas kernels for 25%

commit v1 on v0

v1 whole, which is shorter than its diff:
```python
import functools

import jax
import jax.numpy as jnp
import ml_dtypes
import numpy as np
from jax import lax
from jax.experimental import pallas as pl
from jax.experimental.pallas import tpu as pltpu
from jax.sharding import PartitionSpec as P

CHUNKS = (32, 32)
LAYER = 8
LANES = 128
SUBLANES = 8
f32, bf16 = jnp.float32, jnp.bfloat16
VMEM = pl.BlockSpec(memory_space=pltpu.VMEM)


def tables(g):
    index = np.arange(g)
    angle = 2.0 * np.pi / g * (np.outer(index, index) % g)
    cas = np.cos(angle) + np.sin(angle)
    hi = cas.astype(np.float32).astype(ml_dtypes.bfloat16)
    lo = (cas - hi.astype(np.float64)).astype(np.float32).astype(ml_dtypes.bfloat16)
    rows = np.concatenate([hi, hi, lo], axis=1)
    eye = np.eye(LANES // g, dtype=np.float32)
    wide_hi = np.kron(eye, hi.astype(np.float32)).astype(ml_dtypes.bfloat16)
    wide_lo = np.kron(eye, lo.astype(np.float32)).astype(ml_dtypes.bfloat16)
    lanes = np.block([[wide_hi, wide_lo], [wide_hi, np.zeros_like(wide_lo)]])
    return jnp.asarray(rows), jnp.asarray(lanes)


def split(value):
    hi = value.astype(bf16)
    lo = (value - hi.astype(f32)).astype(bf16)
    return hi, lo


def rows_pass(table, value):
    hi, lo = split(value)
    stacked = jnp.concatenate([hi, lo, hi], axis=0)
    return jnp.dot(table, stacked, preferred_element_type=f32)


def lanes_pass(value, table):
    hi, lo = split(value)
    both = jnp.concatenate([hi, lo], axis=1)
    result = jnp.dot(both, table, preferred_element_type=f32)
    return result[:, :LANES] + result[:, LANES:]


def exchange_halves(value, g):
    half = g // 2
    low = lax.broadcasted_iota(jnp.int32, (half, LANES), 1) < g
    parts = []
    for start in range(0, value.shape[0], g):
        first = value[start : start + half]
        second = value[start + half : start + g]
        parts.append(jnp.where(low, first, pltpu.roll(second, g, 1)))
        parts.append(jnp.where(low, pltpu.roll(first, g, 1), second))
    return jnp.concatenate(parts, axis=0)


def side_by_side(value, count):
    rows = value.shape[0] // count
    return jnp.concatenate([value[k * rows : (k + 1) * rows] for k in range(count)], axis=1)


def stacked(value):
    count = value.shape[1] // LANES
    return jnp.concatenate([value[:, k * LANES : (k + 1) * LANES] for k in range(count)], axis=0)


def pair_kernel(g, n_right, n_other, has_acc, tiles, *refs):
    refs = list(refs)
    left = refs.pop(0)
    parts = [refs.pop(0) for _ in range(n_right + n_other)]
    flag = refs.pop(0) if n_other else None
    acc, _ = (refs.pop(0), refs.pop(0)) if has_acc else (None, None)
    kern, rows_table, lanes_table, out, token, work, right, other, sems = refs
    half = g // 2
    count = g * g // LANES
    table = rows_table[...]
    wide = lanes_table[...]

    copies = []
    filled = 0
    for k, part in enumerate(parts):
        filled = 0 if k == n_right else filled
        place = pl.ds(filled, part.shape[0])
        whole = right if k < n_right else other
        copies.append(pltpu.make_async_copy(part, whole.at[place, :], sems.at[k]))
        filled += part.shape[0]
    for copy in copies:
        copy.start()
    for copy in copies:
        copy.wait()

    def right_block():
        if not parts:
            return left[...]
        if n_other:
            return jnp.where(flag[0] > 0, right[...], other[...])
        return right[...]

    value = stacked(rows_pass(table, left[...] * right_block()))
    work[...] = exchange_halves(lanes_pass(value, wide), g)

    value = jnp.concatenate([work[pl.ds(k, g, stride=half), :] for k in range(half)], axis=1)
    value = rows_pass(table, value) * side_by_side(kern[...], half)
    value = rows_pass(table, value)
    for k in range(half):
        work[pl.ds(k, g, stride=half), :] = value[:, k * LANES : (k + 1) * LANES]

    value = exchange_halves(lanes_pass(work[...], wide), g)
    value = rows_pass(table, side_by_side(value, count)) * right_block()
    if has_acc:
        value = acc[...] + value
    out[...] = stacked(value) if tiles else value
    token[...] = value[:SUBLANES, :LANES]


def pair(left, right, acc, kern, consts, other=(), flag=None, tiles=False):
    g = left.shape[0]
    points = g**3
    operands = [left, *right, *other]
    specs = [VMEM] + [pl.BlockSpec(memory_space=pl.ANY)] * (len(right) + len(other))
    if other:
        operands.append(flag)
        specs.append(pl.BlockSpec(memory_space=pltpu.SMEM))
    if acc is not None:
        operands += acc
        specs += [VMEM, pl.BlockSpec(memory_space=pl.ANY)]
    operands += [kern, *consts]
    specs += [VMEM] * 3
    shape = (points // LANES, LANES) if tiles else left.shape
    return pl.pallas_call(
        functools.partial(pair_kernel, g, len(right), len(other), acc is not None, tiles),
        out_shape=[
            jax.ShapeDtypeStruct(shape, f32),
            jax.ShapeDtypeStruct((SUBLANES, LANES), f32),
        ],
        in_specs=specs,
        out_specs=[VMEM] * 2,
        scratch_shapes=[
            pltpu.VMEM((points // LANES, LANES), f32),
            pltpu.VMEM(left.shape if right else (SUBLANES, LANES), f32),
            pltpu.VMEM(left.shape if other else (SUBLANES, LANES), f32),
            pltpu.SemaphoreType.DMA((max(1, len(right) + len(other)),)),
        ],
        compiler_params=pltpu.CompilerParams(vmem_limit_bytes=10 * 2**20),
        cost_estimate=pl.CostEstimate(flops=points, bytes_accessed=points, transcendentals=0),
    )(*operands)


def lookup_kernel(scale, values, index, out):
    g = index.shape[0]
    half = g // 2
    table = jnp.broadcast_to(values[...], (g, LANES))
    for step in range(g * g // LANES):
        cols = slice(step * LANES, (step + 1) * LANES)
        found = jnp.take_along_axis(table, index[:, cols], axis=1) * scale
        found = exchange_halves(found, g)
        for k in range(2):
            out[pl.ds(2 * step + k, half, stride=g), :] = found[k * half : (k + 1) * half]


def lookup(kernel_values, shell_index):
    g = shell_index.shape[0]
    classes = kernel_values.shape[0]
    padded = jnp.pad(kernel_values, (0, LANES - classes)).reshape(1, LANES)
    return pl.pallas_call(
        functools.partial(lookup_kernel, -1.0 / g**3),
        out_shape=jax.ShapeDtypeStruct((g**3 // LANES, LANES), f32),
        in_specs=[VMEM] * 2,
        out_specs=VMEM,
        compiler_params=pltpu.CompilerParams(vmem_limit_bytes=8 * 2**20),
    )(padded, shell_index)


def tile_kernel(own, tiles):
    tiles[...] = stacked(own[...])


def tiled(own):
    return pl.pallas_call(
        tile_kernel,
        out_shape=jax.ShapeDtypeStruct((own.size // LANES, LANES), f32),
        in_specs=[VMEM],
        out_specs=VMEM,
        compiler_params=pltpu.CompilerParams(vmem_limit_bytes=8 * 2**20),
    )(own)


def regroup_kernel(place, columns, done, *outs):
    rows = outs[0].shape[1]
    for k, out in enumerate(outs):
        first = pl.multiple_of(jnp.bitwise_xor(place[0], k) * rows, rows)
        out[...] = columns[:, pl.ds(first, rows), :]


def regroup(columns, place, done):
    layers, rows = columns.shape[0], columns.shape[1] // LAYER
    return pl.pallas_call(
        regroup_kernel,
        out_shape=[jax.ShapeDtypeStruct((layers, rows, LANES), f32)] * LAYER,
        in_specs=[pl.BlockSpec(memory_space=pltpu.SMEM), VMEM, pl.BlockSpec(memory_space=pl.ANY)],
        out_specs=[VMEM] * LAYER,
        compiler_params=pltpu.CompilerParams(vmem_limit_bytes=8 * 2**20),
    )(place, columns, done)


def margin_kernel(scale, place, terms, *refs):
    orbitals, out = refs[:-1], refs[-1]
    count = terms.shape[0]
    lefts, rights = [], []
    for step in range(terms.shape[1] // SUBLANES):
        rows = slice(step * SUBLANES, (step + 1) * SUBLANES)
        part = [column[k, rows, :] for k in range(count // LAYER) for column in orbitals]
        a_hi, a_lo = split(jnp.concatenate(part, axis=0))
        b_hi, b_lo = split(terms[:, rows, :].reshape(count * SUBLANES, LANES))
        lefts += [a_hi, a_lo, a_hi]
        rights += [b_hi, b_hi, b_lo]
    products = lax.dot_general(
        jnp.concatenate(lefts, axis=1),
        jnp.concatenate(rights, axis=1),
        (((1,), (1,)), ((), ())),
        preferred_element_type=f32,
    )
    size = count * SUBLANES
    row = lax.broadcasted_iota(jnp.int32, (size, size), 0) % SUBLANES
    col = lax.broadcasted_iota(jnp.int32, (size, size), 1) % SUBLANES
    kept = jnp.where(row == col, products, 0.0)
    summed = jnp.sum(kept.reshape(count, SUBLANES, size), axis=1)
    pick_row = lax.broadcasted_iota(jnp.int32, (size, count), 0) // SUBLANES
    pick_col = lax.broadcasted_iota(jnp.int32, (size, count), 1)
    pick = (pick_row == pick_col).astype(f32)
    highest = lax.Precision.HIGHEST
    by_distance = jnp.dot(summed, pick, precision=highest, preferred_element_type=f32)
    row = lax.broadcasted_iota(jnp.int32, (count, count), 0)
    col = lax.broadcasted_iota(jnp.int32, (count, count), 1)
    order = (jnp.bitwise_xor(row, place[0]) == col).astype(f32)
    out[...] = scale * jnp.dot(order, by_distance, precision=highest, preferred_element_type=f32)


def partial_margin(orbitals, terms, place, points):
    count = terms.shape[0]
    return pl.pallas_call(
        functools.partial(margin_kernel, 1.0 / points),
        out_shape=jax.ShapeDtypeStruct((count, count), f32),
        in_specs=[pl.BlockSpec(memory_space=pltpu.SMEM)] + [VMEM] * (1 + len(orbitals)),
        out_specs=VMEM,
        compiler_params=pltpu.CompilerParams(
            vmem_limit_bytes=8 * 2**20 + 12 * (count * SUBLANES) ** 2
        ),
    )(place, terms, *orbitals)


def permute(value, target, count):
    return lax.ppermute(value, "band", [(source, target(source) % count) for source in range(count)])


def far_target(source):
    return source - 4 if (source // 2) % 2 else source + 4


def after(*values):
    return lax.optimization_barrier(values)


def exchange(value, groups=None):
    return lax.all_to_all(
        value, "band", split_axis=0, concat_axis=0, tiled=True, axis_index_groups=groups
    )


def local(orbitals, kernel_values, shell_index):
    count = lax.axis_size("band")
    me = lax.axis_index("band")
    g = shell_index.shape[0]
    points = g**3
    consts = tables(g)
    own = orbitals.reshape(g, g * g)
    layers = count // LAYER
    along = [[layer * LAYER + k for layer in range(layers)] for k in range(LAYER)]

    def swap(value, distance=1):
        return permute(value, lambda d: d ^ distance, count)

    starts = [sum(CHUNKS[:k]) for k in range(len(CHUNKS))]
    near = [swap(own[start : start + size], 2) for start, size in zip(starts, CHUNKS)]
    peer = swap(own)
    by_tile, kernel_values = after(tiled(own), kernel_values)
    columns = exchange(by_tile.reshape(layers, -1, LANES), along)

    kern = lookup(kernel_values, shell_index)
    far = [None] * 2
    term, done = pair(own, [], None, kern, consts)
    near[0], done = after(near[0], done)
    far[0] = permute(near[0], far_target, count)
    term, done = pair(own, [peer], (term, done), kern, consts)
    near[1], done = after(near[1], done)
    far[1] = permute(near[1], far_target, count)
    near_cross = [swap(part) for part in near]
    use_near = (((me + 1) // 2) % 2).astype(jnp.int32).reshape(1)
    term, done = pair(own, near, (term, done), kern, consts)
    far[1], done = after(far[1], done)
    far_cross = [swap(part) for part in far]
    term, done = pair(own, far, (term, done), kern, consts)
    tiles, done = pair(own, near_cross, (term, done), kern, consts, far_cross, use_near, tiles=True)
    place = (me % LAYER).astype(jnp.int32).reshape(1)
    columns = list(regroup(columns, place, done))
    columns = [columns[0]] + [swap(columns[k], k) for k in range(1, LAYER)]
    spread_terms = exchange(tiles.reshape(count, -1, LANES))
    term = tiles.reshape(g * g // LANES, g, LANES).transpose(1, 0, 2).reshape(orbitals.shape)
    rows = partial_margin(columns, spread_terms, place, points)
    margin = jnp.sum(exchange(rows), axis=0, keepdims=True)
    return term, margin


def solution(mesh):
    return jax.shard_map(
        local,
        mesh=mesh,
        in_specs=(P("band", None, None), P(), P()),
        out_specs=(P("band", None, None), P("band", None)),
        check_vma=False,
    )
```

time: 140 us -> 116 us (0.83)
  blocking collectives: 40.3 us -> 0 us
  starting transfers between devices: 13.4 us -> 30.7 us
  waiting for transfers between devices: 33 us -> 46.5 us
  local copies, waits for them, and re-layouts: 15.9 us -> 8.4 us
  Pallas kernels: 35.1 us -> 28.1 us
    all_to_all x2 -> x0, blocking collectives: 40.3 us -> none  [the longest x1 29.7 us: local(): lax.all_to_all(tiles.reshape(count, -1, LANES), 'band', split_axis=0, con...]
    reshape x3 -> x1, local copies, waits for them, and re-layouts: 11.1 us -> 1.16 us  [local(): tiles.reshape(g * g // LANES, g, LANES).transpose(1, 0, 2)]
    ppermute x9 -> x16, starting transfers between devices: 6.1 us -> 15 us  [permute(): lax.ppermute(value, 'band', [(source, target(source) % count) for source...]
    pallas_call x5, Pallas kernels: 31.2 us -> 22.5 us  [pair(): pl.pallas_call(functools.partial(pair_kernel, g, len(right), len(other),...]
    all_to_all x1 -> x3, starting transfers between devices: 7.3 us -> 15.7 us  [exchange(): lax.all_to_all(value, 'band', split_axis=0, concat_axis=0, tiled=True, ax...]
    ppermute x9 -> x16, waiting for transfers between devices: 33 us -> 41 us  [permute(): lax.ppermute(value, 'band', [(source, target(source) % count) for source...]
    all_to_all x1 -> x3, waiting for transfers between devices: 0.01 us -> 5.55 us  [exchange(): lax.all_to_all(value, 'band', split_axis=0, concat_axis=0, tiled=True, ax...]
    slice x1, local copies, waits for them, and re-layouts: 0.07 us -> 2.23 us  [local(): own[start:start + size]]
  transfers between devices with their start and end apart: 10 -> 19, of which waited for: 2 -> 9; matrix products, arithmetic and copies ran while one was open for 8% -> 3% of each run, Pallas kernels for 25% -> 23%
where the time goes in v1:
time: 116 us; the launch traced here: 115 us
  waiting for transfers between devices  46.5 us (40%)
  starting transfers between devices  30.7 us (26%)
  Pallas kernels  28.1 us (24%)
  local copies, waits for them, and re-layouts  8.4 us (7%)
    ppermute x16, waiting for transfers between devices, permute(): lax.ppermute(value, 'band', [(source, target(source) % count) for source...  41 us
    pallas_call x5, Pallas kernels, pair(): pl.pallas_call(functools.partial(pair_kernel, g, len(right), len(other),...  22.5 us
    all_to_all x3, starting transfers between devices, exchange(): lax.all_to_all(value, 'band', split_axis=0, concat_axis=0, tiled=True, ax...  15.7 us
    ppermute x16, starting transfers between devices, permute(): lax.ppermute(value, 'band', [(source, target(source) % count) for source...  15 us
    all_to_all x3, waiting for transfers between devices, exchange(): lax.all_to_all(value, 'band', split_axis=0, concat_axis=0, tiled=True, ax...  5.55 us
    unnamed x18, local copies, waits for them, and re-layouts  4.39 us
    pallas_call x1, Pallas kernels, lookup(): pl.pallas_call(functools.partial(lookup_kernel, -1.0 / g ** 3), out_shape...  2.82 us
  transfers between devices with their start and end apart: 19, of which 9 were waited for; matrix products, arithmetic and copies ran while one was open for 3% of the time, Pallas kernels for 23%

profile of v1, /device:TPU:0, one launch (start us, length us, event | category | flops | bytes accessed | tf_op | source)
XLA Modules:
  0.0 115.2 jit_solution(12603204156304777487)
XLA Ops:
  0.6 0.0 copy-start
  0.6 0.5 collective-permute-start.3
  1.2 2.2 %slice_bitcast_fusion = (f32[32,4096]{1,0:T(8,128)}, f32[32,4096]{1,0:T(8,128)}) fusion(f32[1,64,4096]{2,1,0:T(8,128)} %param.5), kind=kLoop, calls=%fused_computation | loop fusion | bytes 2097152 | tf_op jit(solution)/shard_map/slice | solution.py:292
  3.4 2.6 %collective-permute-start = (f32[32,4096]{1,0:T(8,128)}, f32[32,4096]{1,0:T(8,128)}, u32[]{:S(2)}, u32[]{:S(2)}) collective-permute-start(f32[32,4096]{1,0:T(8,128)} %get-tuple-element.55), channel_id=1, source_target_pairs={{0,2},{1,3},{2,0},{3,1},{4,6},{5,7},{6,4},{7,5},{8,10},{9,11},{10,... | collective-permute-start | bytes 1572872 | tf_op jit(solution)/shard_map/ppermute | solution.py:261
  6.0 0.0 collective-permute-start.2
  6.0 0.0 copy-done
  6.0 1.0 shard_map.68
  7.1 5.5 %all-to-all-start.1 = ((f32[4,512,128]{2,1,0:T(8,128)}), f32[4,512,128]{2,1,0:T(8,128)S(1)}, u32[]{:S(2)}, u32[]{:S(2)}) async-start(f32[4,512,128]{2,1,0:T(8,128)} %bitcast.8), calls=%async_computation.1 | async-start | bytes 2097152 | tf_op jit(solution)/shard_map/all_to_all | solution.py:273
  12.6 0.0 copy-done.8
  12.6 0.0 copy-start.6
  12.6 1.2 %copy-done.6 = s32[64,4096]{1,0:T(8,128)S(1)} copy-done((s32[64,4096]{1,0:T(8,128)S(1)}, s32[64,4096]{1,0:T(8,128)}, u32[]{:S(2)}) %copy-start.6) | copy-done | bytes 1048600
  13.8 2.8 %shard_map.69.refs_1_.refs_4_.refs_5_.refs_8_ = f32[2048,128]{1,0:T(8,128)S(1)} custom-call(f32[1,128]{1,0:T(1,128)S(1)} %pad_bitcast_fusion.values, s32[64,4096]{1,0:T(8,128)S(1)} %copy-done.6), custom_call_target="tpu_custom_call" | custom-call | tf_op jit(solution)/shard_map/pallas_call | solution.py:173
  16.6 0.0 copy-done.3
  16.6 0.0 copy-done.7
  16.6 3.4 %shard_map.70 = (f32[64,4096]{1,0:T(8,128)S(1)}, f32[8,128]{1,0:T(8,128)S(1)}) custom-call(f32[64,4096]{1,0:T(8,128)S(1)} %bitcast.19, f32[2048,128]{1,0:T(8,128)S(1)} %shard_map.69.refs_1_.refs_4_.refs_5_.refs_8_, bf16[64,192]{1,0:T(8,128)(2,1)S(1)} %copy-done.7, bf16[256,256]{1,0:T(8,128)(2,1)S(1)} %copy-done.3), custom_call_target="tpu_custom_call" | custom-call | flops 262144 | bytes 262144 | tf_op jit(solution)/shard_map/pallas_call | solution.py:138
  20.1 0.0 collective-permute-done.refs_1_
  20.1 1.6 %collective-permute-start.5 = (f32[32,4096]{1,0:T(8,128)}, f32[32,4096]{1,0:T(8,128)}, u32[]{:S(2)}, u32[]{:S(2)}) collective-permute-start(f32[32,4096]{1,0:T(8,128)} %collective-permute-done.refs_1_), channel_id=1, source_target_pairs={{0,4},{1,5},{2,30},{3,31},{4,8},{5,9},{6,2},{7,3},{8,12},{9,13},{1... | collective-permute-start | bytes 1572872 | tf_op jit(solution)/shard_map/ppermute | solution.py:261
  21.7 0.0 collective-permute-done.3.refs_1_
  21.7 4.7 %shard_map.71 = (f32[64,4096]{1,0:T(8,128)S(1)}, f32[8,128]{1,0:T(8,128)S(1)}) custom-call(f32[64,4096]{1,0:T(8,128)S(1)} %bitcast.20, f32[64,4096]{1,0:T(8,128)} %collective-permute-done.3.refs_1_, f32[64,4096]{1,0:T(8,128)S(1)} %get-tuple-element.31.refs_2_, f32[8,128]{1,0:T(8,128)S(1)} %get-tuple-element.32.refs_3_, ...), custom_call_target="tpu_custom_call" | custom-call | flops 262144 | bytes 262144 | tf_op jit(solution)/shard_map/pallas_call | solution.py:138
  26.3 3.7 %collective-permute-done.2.refs_2_ = f32[32,4096]{1,0:T(8,128)} collective-permute-done((f32[32,4096]{1,0:T(8,128)}, f32[32,4096]{1,0:T(8,128)}, u32[]{:S(2)}, u32[]{:S(2)}) %collective-permute-start.2) | collective-permute-done | bytes 524320 | tf_op jit(solution)/shard_map/ppermute | solution.py:261
  30.0 1.8 %collective-permute-start.7 = (f32[32,4096]{1,0:T(8,128)}, f32[32,4096]{1,0:T(8,128)}, u32[]{:S(2)}, u32[]{:S(2)}) collective-permute-start(f32[32,4096]{1,0:T(8,128)} %collective-permute-done.2.refs_2_), channel_id=1, source_target_pairs={{0,4},{1,5},{2,30},{3,31},{4,8},{5,9},{6,2},{7,3},{8,12},{9,13},{1... | collective-permute-start | bytes 1572872 | tf_op jit(solution)/shard_map/ppermute | solution.py:261
  31.8 0.0 collective-permute-start.1
  31.8 0.5 collective-permute-start.4
  32.3 4.7 %shard_map.72 = (f32[64,4096]{1,0:T(8,128)S(1)}, f32[8,128]{1,0:T(8,128)S(1)}) custom-call(f32[64,4096]{1,0:T(8,128)S(1)} %bitcast.21, f32[32,4096]{1,0:T(8,128)} %collective-permute-done.refs_1_, f32[32,4096]{1,0:T(8,128)} %collective-permute-done.2.refs_2_, f32[64,4096]{1,0:T(8,128)S(1)} %get-tuple-element.35.refs_3_, ...), custom_call_target="tpu_custom_call" | custom-call | flops 262144 | bytes 262144 | tf_op jit(solution)/shard_map/pallas_call | solution.py:138
  37.0 0.0 copy-start.4
  37.0 1.0 copy-done.4
  38.0 9.5 %collective-permute-done.5.refs_1_ = f32[32,4096]{1,0:T(8,128)} collective-permute-done((f32[32,4096]{1,0:T(8,128)}, f32[32,4096]{1,0:T(8,128)}, u32[]{:S(2)}, u32[]{:S(2)}) %collective-permute-start.5) | collective-permute-done | bytes 524320 | tf_op jit(solution)/shard_map/ppermute | solution.py:261
  47.4 0.0 collective-permute-start.6
  47.4 9.9 %collective-permute-done.7.refs_2_ = f32[32,4096]{1,0:T(8,128)} collective-permute-done((f32[32,4096]{1,0:T(8,128)}, f32[32,4096]{1,0:T(8,128)}, u32[]{:S(2)}, u32[]{:S(2)}) %collective-permute-start.7) | collective-permute-done | bytes 524320 | tf_op jit(solution)/shard_map/ppermute | solution.py:261
  57.3 0.0 collective-permute-start.8
  57.3 1.2 %copy-done.5 = f32[64,4096]{1,0:T(8,128)S(1)} copy-done((f32[64,4096]{1,0:T(8,128)S(1)}, f32[64,4096]{1,0:T(8,128)}, u32[]{:S(2)}) %copy-start.5) | copy-done | bytes 1048600
  58.5 4.7 %shard_map.73 = (f32[64,4096]{1,0:T(8,128)S(1)}, f32[8,128]{1,0:T(8,128)S(1)}) custom-call(f32[64,4096]{1,0:T(8,128)S(1)} %bitcast.22, f32[32,4096]{1,0:T(8,128)} %collective-permute-done.5.refs_1_, f32[32,4096]{1,0:T(8,128)} %collective-permute-done.7.refs_2_, f32[64,4096]{1,0:T(8,128)S(1)} %copy-done.5, f32[8,128]{1,0:T(8,128)S(1)} %get-tuple-element.40.refs_4_, ...), custom_call_target="tpu_custom_call" | custom-call | flops 262144 | bytes 262144 | tf_op jit(solution)/shard_map/pallas_call | solution.py:138
  63.2 0.0 collective-permute-done.1.refs_1_
  63.2 0.0 collective-permute-done.4.refs_2_
  63.2 0.0 collective-permute-done.6.refs_3_
  63.2 0.0 collective-permute-done.8.refs_4_
  63.2 5.1 %shard_map.74 = (f32[2048,128]{1,0:T(8,128)S(1)}, f32[8,128]{1,0:T(8,128)S(1)}) custom-call(f32[64,4096]{1,0:T(8,128)S(1)} %bitcast.23, f32[32,4096]{1,0:T(8,128)} %collective-permute-done.1.refs_1_, f32[32,4096]{1,0:T(8,128)} %collective-permute-done.4.refs_2_, f32[32,4096]{1,0:T(8,128)} %collective-permute-done.6.refs_3_, ...), custom_call_target="tpu_custom_call" | custom-call | flops 262144 | bytes 262144 | tf_op jit(solution)/shard_map/pallas_call | solution.py:138
  68.3 0.0 copy-start.1
  68.3 1.0 copy-done.1
  69.3 0.0 all-to-all-done.1.columns
  69.3 6.5 %all-to-all-start = ((f32[32,64,128]{2,1,0:T(8,128)}), f32[32,64,128]{2,1,0:T(8,128)S(1)}, u32[]{:S(2)}, u32[]{:S(2)}) async-start(f32[32,64,128]{2,1,0:T(8,128)} %bitcast.24), calls=%async_computation | async-start | bytes 2097152 | tf_op jit(solution)/shard_map/all_to_all | solution.py:273
  75.8 0.1 shard_map.75
  75.9 1.8 %collective-permute-start.10 = (f32[4,64,128]{2,1,0:T(8,128)S(1)}, f32[4,64,128]{2,1,0:T(8,128)S(1)}, u32[]{:S(2)}, u32[]{:S(2)}) collective-permute-start(f32[4,64,128]{2,1,0:T(8,128)S(1)} %get-tuple-element.48), channel_id=1, source_target_pairs={{0,2},{1,3},{2,0},{3,1},{4,6},{5,7},{6,4},{7,5},{8,10},{9,11},{10,... | collective-permute-start | bytes 393224 | tf_op jit(solution)/shard_map/ppermute | solution.py:261
  77.7 0.0 collective-permute-start.11
  77.7 1.5 %collective-permute-start.12 = (f32[4,64,128]{2,1,0:T(8,128)S(1)}, f32[4,64,128]{2,1,0:T(8,128)S(1)}, u32[]{:S(2)}, u32[]{:S(2)}) collective-permute-start(f32[4,64,128]{2,1,0:T(8,128)S(1)} %get-tuple-element.50), channel_id=1, source_target_pairs={{0,4},{1,5},{2,6},{3,7},{4,0},{5,1},{6,2},{7,3},{8,12},{9,13},{10,... | collective-permute-start | bytes 393224 | tf_op jit(solution)/shard_map/ppermute | solution.py:261
  79.3 0.3 collective-permute-start.13
  79.5 2.6 %collective-permute-start.14 = (f32[4,64,128]{2,1,0:T(8,128)S(1)}, f32[4,64,128]{2,1,0:T(8,128)S(1)}, u32[]{:S(2)}, u32[]{:S(2)}) collective-permute-start(f32[4,64,128]{2,1,0:T(8,128)S(1)} %get-tuple-element.52), channel_id=1, source_target_pairs={{0,6},{1,7},{2,4},{3,5},{4,2},{5,3},{6,0},{7,1},{8,14},{9,15},{10,... | collective-permute-start | bytes 393224 | tf_op jit(solution)/shard_map/ppermute | solution.py:261
  82.1 8.3 %collective-permute-done.10.refs_2_ = f32[4,64,128]{2,1,0:T(8,128)S(1)} collective-permute-done((f32[4,64,128]{2,1,0:T(8,128)S(1)}, f32[4,64,128]{2,1,0:T(8,128)S(1)}, u32[]{:S(2)}, u32[]{:S(2)}) %collective-permute-start.10) | collective-permute-done | bytes 131104 | tf_op jit(solution)/shard_map/ppermute | solution.py:261
  90.4 0.0 collective-permute-start.15
  90.5 2.5 %collective-permute-done.11.refs_3_ = f32[4,64,128]{2,1,0:T(8,128)S(1)} collective-permute-done((f32[4,64,128]{2,1,0:T(8,128)S(1)}, f32[4,64,128]{2,1,0:T(8,128)S(1)}, u32[]{:S(2)}, u32[]{:S(2)}) %collective-permute-start.11) | collective-permute-done | bytes 131104 | tf_op jit(solution)/shard_map/ppermute | solution.py:261
  93.0 1.8 %collective-permute-start.9 = (f32[4,64,128]{2,1,0:T(8,128)S(1)}, f32[4,64,128]{2,1,0:T(8,128)S(1)}, u32[]{:S(2)}, u32[]{:S(2)}) collective-permute-start(f32[4,64,128]{2,1,0:T(8,128)S(1)} %get-tuple-element.47), channel_id=1, source_target_pairs={{0,1},{1,0},{2,3},{3,2},{4,5},{5,4},{6,7},{7,6},{8,9},{9,8},{10,11... | collective-permute-start | bytes 393224 | tf_op jit(solution)/shard_map/ppermute | solution.py:261
  94.7 0.0 collective-permute-done.12.refs_4_
  94.7 0.0 collective-permute-done.13.refs_5_
  94.7 3.6 %collective-permute-done.14.refs_6_ = f32[4,64,128]{2,1,0:T(8,128)S(1)} collective-permute-done((f32[4,64,128]{2,1,0:T(8,128)S(1)}, f32[4,64,128]{2,1,0:T(8,128)S(1)}, u32[]{:S(2)}, u32[]{:S(2)}) %collective-permute-start.14) | collective-permute-done | bytes 131104 | tf_op jit(solution)/shard_map/ppermute | solution.py:261
  98.3 3.5 %collective-permute-done.15.refs_7_ = f32[4,64,128]{2,1,0:T(8,128)S(1)} collective-permute-done((f32[4,64,128]{2,1,0:T(8,128)S(1)}, f32[4,64,128]{2,1,0:T(8,128)S(1)}, u32[]{:S(2)}, u32[]{:S(2)}) %collective-permute-start.15) | collective-permute-done | bytes 131104 | tf_op jit(solution)/shard_map/ppermute | solution.py:261
  101.9 0.0 collective-permute-done.9.refs_1_
  101.9 0.2 all-to-all-done.terms
  102.1 1.7 %shard_map.76 = f32[32,32]{1,0:T(8,128)} custom-call(s32[1]{0:T(128)} %bitcast.7.place, f32[32,64,128]{2,1,0:T(8,128)S(1)} %all-to-all-done.terms, f32[4,64,128]{2,1,0:T(8,128)S(1)} %get-tuple-element.46.refs_0_, f32[4,64,128]{2,1,0:T(8,128)S(1)} %collective-permute-done.9.refs_1_, f32[4,64,128]{2,1,0:T(8,128)S(1)} %collective-permute-done.10.refs_2_, ...), custom_call_target="tpu_custom_call" | custom-call | tf_op jit(solution)/shard_map/pallas_call | solution.py:249
  103.7 3.7 %all-to-all-start.2 = ((f32[32,1,32]{2,1,0:T(1,128)}), f32[32,1,32]{2,1,0:T(1,128)S(1)}, u32[]{:S(2)}, u32[]{:S(2)}) async-start(f32[32,1,32]{2,1,0:T(1,128)} %bitcast.10), calls=%async_computation.2 | async-start | bytes 32768 | tf_op jit(solution)/shard_map/all_to_all | solution.py:273
  107.4 0.0 copy-done.2
  107.5 0.6 copy.8
  108.1 1.2 %reshape.34 = f32[1,64,4096]{2,1,0:T(8,128)} reshape(f32[64,32,128]{2,1,0:T(8,128)S(1)} %copy.8) | data formatting | bytes 2097152 | tf_op jit(solution)/shard_map/reshape | solution.py:316
  109.2 5.4 %all-to-all-done.2 = f32[32,1,32]{2,1,0:T(1,128)S(1)} async-done(((f32[32,1,32]{2,1,0:T(1,128)}), f32[32,1,32]{2,1,0:T(1,128)S(1)}, u32[]{:S(2)}, u32[]{:S(2)}) %all-to-all-start.2) | async-done | bytes 4128 | tf_op jit(solution)/shard_map/all_to_all | solution.py:273
  114.6 0.6 reduce_sum.9
  (6 shorter events, 0.0 us)
Async XLA Ops:
  0.6 5.4 %copy-start = (f32[1,64,4096]{2,1,0:T(8,128)S(1)}, f32[1,64,4096]{2,1,0:T(8,128)}, u32[]{:S(2)}) copy-start(f32[1,64,4096]{2,1,0:T(8,128)} %param.5) | copy-start | bytes 3145732
  0.6 21.0 %collective-permute-start.3 = (f32[64,4096]{1,0:T(8,128)}, f32[64,4096]{1,0:T(8,128)}, u32[]{:S(2)}, u32[]{:S(2)}) collective-permute-start(f32[64,4096]{1,0:T(8,128)} %bitcast.17), channel_id=1, source_target_pairs={{0,1},{1,0},{2,3},{3,2},{4,5},{5,4},{6,7},{7,6},{8,9},{9,8},{10,11... | collective-permute-start | bytes 3145736 | tf_op jit(solution)/shard_map/ppermute | solution.py:261
  3.4 16.7 %collective-permute-start = (f32[32,4096]{1,0:T(8,128)}, f32[32,4096]{1,0:T(8,128)}, u32[]{:S(2)}, u32[]{:S(2)}) collective-permute-start(f32[32,4096]{1,0:T(8,128)} %get-tuple-element.55), channel_id=1, source_target_pairs={{0,2},{1,3},{2,0},{3,1},{4,6},{5,7},{6,4},{7,5},{8,10},{9,11},{10,... | collective-permute-start | bytes 1572872 | tf_op jit(solution)/shard_map/ppermute | solution.py:261
  6.0 24.1 %collective-permute-start.2 = (f32[32,4096]{1,0:T(8,128)}, f32[32,4096]{1,0:T(8,128)}, u32[]{:S(2)}, u32[]{:S(2)}) collective-permute-start(f32[32,4096]{1,0:T(8,128)} %get-tuple-element.54), channel_id=1, source_target_pairs={{0,2},{1,3},{2,0},{3,1},{4,6},{5,7},{6,4},{7,5},{8,10},{9,11},{10,... | collective-permute-start | bytes 1572872 | tf_op jit(solution)/shard_map/ppermute | solution.py:261
  7.1 5.5 %copy-start.8 = (f32[32]{0:T(128)S(1)}, f32[32]{0:T(128)}, u32[]{:S(2)}) copy-start(f32[32]{0:T(128)} %param.6) | copy-start | bytes 388
  7.1 62.2 %all-to-all-start.1 = ((f32[4,512,128]{2,1,0:T(8,128)}), f32[4,512,128]{2,1,0:T(8,128)S(1)}, u32[]{:S(2)}, u32[]{:S(2)}) async-start(f32[4,512,128]{2,1,0:T(8,128)} %bitcast.8), calls=%async_computation.1 | async-start | bytes 2097152 | tf_op jit(solution)/shard_map/all_to_all | solution.py:273
  12.6 1.2 %copy-start.6 = (s32[64,4096]{1,0:T(8,128)S(1)}, s32[64,4096]{1,0:T(8,128)}, u32[]{:S(2)}) copy-start(s32[64,4096]{1,0:T(8,128)} %index.1) | copy-start | bytes 3145732
  13.8 2.8 %copy-start.3 = (bf16[256,256]{1,0:T(8,128)(2,1)S(1)}, bf16[256,256]{1,0:T(8,128)(2,1)}, u32[]{:S(2)}) copy-start(bf16[256,256]{1,0:T(8,128)(2,1)} %constant.48.clone.refs_3_.refs_6_.refs_7_.refs_10_) | copy-start | bytes 393220
  13.8 2.8 %copy-start.7 = (bf16[64,192]{1,0:T(8,128)(2,1)S(1)}, bf16[64,192]{1,0:T(8,128)(2,1)}, u32[]{:S(2)}) copy-start(bf16[64,192]{1,0:T(8,128)(2,1)} %constant.47.clone.refs_2_.refs_5_.refs_6_.refs_9_) | copy-start | bytes 73732
  20.1 27.3 %collective-permute-start.5 = (f32[32,4096]{1,0:T(8,128)}, f32[32,4096]{1,0:T(8,128)}, u32[]{:S(2)}, u32[]{:S(2)}) collective-permute-start(f32[32,4096]{1,0:T(8,128)} %collective-permute-done.refs_1_), channel_id=1, source_target_pairs={{0,4},{1,5},{2,30},{3,31},{4,8},{5,9},{6,2},{7,3},{8,12},{9,13},{1... | collective-permute-start | bytes 1572872 | tf_op jit(solution)/shard_map/ppermute | solution.py:261
  30.0 27.3 %collective-permute-start.7 = (f32[32,4096]{1,0:T(8,128)}, f32[32,4096]{1,0:T(8,128)}, u32[]{:S(2)}, u32[]{:S(2)}) collective-permute-start(f32[32,4096]{1,0:T(8,128)} %collective-permute-done.2.refs_2_), channel_id=1, source_target_pairs={{0,4},{1,5},{2,30},{3,31},{4,8},{5,9},{6,2},{7,3},{8,12},{9,13},{1... | collective-permute-start | bytes 1572872 | tf_op jit(solution)/shard_map/ppermute | solution.py:261
  31.8 31.4 %collective-permute-start.1 = (f32[32,4096]{1,0:T(8,128)}, f32[32,4096]{1,0:T(8,128)}, u32[]{:S(2)}, u32[]{:S(2)}) collective-permute-start(f32[32,4096]{1,0:T(8,128)} %collective-permute-done.refs_1_), channel_id=1, source_target_pairs={{0,1},{1,0},{2,3},{3,2},{4,5},{5,4},{6,7},{7,6},{8,9},{9,8},{10,11... | collective-permute-start | bytes 1572872 | tf_op jit(solution)/shard_map/ppermute | solution.py:261
  31.8 31.4 %collective-permute-start.4 = (f32[32,4096]{1,0:T(8,128)}, f32[32,4096]{1,0:T(8,128)}, u32[]{:S(2)}, u32[]{:S(2)}) collective-permute-start(f32[32,4096]{1,0:T(8,128)} %collective-permute-done.2.refs_2_), channel_id=1, source_target_pairs={{0,1},{1,0},{2,3},{3,2},{4,5},{5,4},{6,7},{7,6},{8,9},{9,8},{10,11... | collective-permute-start | bytes 1572872 | tf_op jit(solution)/shard_map/ppermute | solution.py:261
  37.0 1.0 copy-start.4
  47.4 15.8 %collective-permute-start.6 = (f32[32,4096]{1,0:T(8,128)}, f32[32,4096]{1,0:T(8,128)}, u32[]{:S(2)}, u32[]{:S(2)}) collective-permute-start(f32[32,4096]{1,0:T(8,128)} %collective-permute-done.5.refs_1_), channel_id=1, source_target_pairs={{0,1},{1,0},{2,3},{3,2},{4,5},{5,4},{6,7},{7,6},{8,9},{9,8},{10,11... | collective-permute-start | bytes 1572872 | tf_op jit(solution)/shard_map/ppermute | solution.py:261
  57.3 5.9 %collective-permute-start.8 = (f32[32,4096]{1,0:T(8,128)}, f32[32,4096]{1,0:T(8,128)}, u32[]{:S(2)}, u32[]{:S(2)}) collective-permute-start(f32[32,4096]{1,0:T(8,128)} %collective-permute-done.7.refs_2_), channel_id=1, source_target_pairs={{0,1},{1,0},{2,3},{3,2},{4,5},{5,4},{6,7},{7,6},{8,9},{9,8},{10,11... | collective-permute-start | bytes 1572872 | tf_op jit(solution)/shard_map/ppermute | solution.py:261
  57.3 1.2 %copy-start.5 = (f32[64,4096]{1,0:T(8,128)S(1)}, f32[64,4096]{1,0:T(8,128)}, u32[]{:S(2)}) copy-start(f32[64,4096]{1,0:T(8,128)} %copy-done.4) | copy-start | bytes 3145732
  68.3 1.0 copy-start.1
  69.3 32.8 %all-to-all-start = ((f32[32,64,128]{2,1,0:T(8,128)}), f32[32,64,128]{2,1,0:T(8,128)S(1)}, u32[]{:S(2)}, u32[]{:S(2)}) async-start(f32[32,64,128]{2,1,0:T(8,128)} %bitcast.24), calls=%async_computation | async-start | bytes 2097152 | tf_op jit(solution)/shard_map/all_to_all | solution.py:273
  75.9 14.5 %collective-permute-start.10 = (f32[4,64,128]{2,1,0:T(8,128)S(1)}, f32[4,64,128]{2,1,0:T(8,128)S(1)}, u32[]{:S(2)}, u32[]{:S(2)}) collective-permute-start(f32[4,64,128]{2,1,0:T(8,128)S(1)} %get-tuple-element.48), channel_id=1, source_target_pairs={{0,2},{1,3},{2,0},{3,1},{4,6},{5,7},{6,4},{7,5},{8,10},{9,11},{10,... | collective-permute-start | bytes 393224 | tf_op jit(solution)/shard_map/ppermute | solution.py:261
  77.7 15.2 %collective-permute-start.11 = (f32[4,64,128]{2,1,0:T(8,128)S(1)}, f32[4,64,128]{2,1,0:T(8,128)S(1)}, u32[]{:S(2)}, u32[]{:S(2)}) collective-permute-start(f32[4,64,128]{2,1,0:T(8,128)S(1)} %get-tuple-element.49), channel_id=1, source_target_pairs={{0,3},{1,2},{2,1},{3,0},{4,7},{5,6},{6,5},{7,4},{8,11},{9,10},{10,... | collective-permute-start | bytes 393224 | tf_op jit(solution)/shard_map/ppermute | solution.py:261
  77.7 17.0 %collective-permute-start.12 = (f32[4,64,128]{2,1,0:T(8,128)S(1)}, f32[4,64,128]{2,1,0:T(8,128)S(1)}, u32[]{:S(2)}, u32[]{:S(2)}) collective-permute-start(f32[4,64,128]{2,1,0:T(8,128)S(1)} %get-tuple-element.50), channel_id=1, source_target_pairs={{0,4},{1,5},{2,6},{3,7},{4,0},{5,1},{6,2},{7,3},{8,12},{9,13},{10,... | collective-permute-start | bytes 393224 | tf_op jit(solution)/shard_map/ppermute | solution.py:261
  79.3 15.5 %collective-permute-start.13 = (f32[4,64,128]{2,1,0:T(8,128)S(1)}, f32[4,64,128]{2,1,0:T(8,128)S(1)}, u32[]{:S(2)}, u32[]{:S(2)}) collective-permute-start(f32[4,64,128]{2,1,0:T(8,128)S(1)} %get-tuple-element.51), channel_id=1, source_target_pairs={{0,5},{1,4},{2,7},{3,6},{4,1},{5,0},{6,3},{7,2},{8,13},{9,12},{10,... | collective-permute-start | bytes 393224 | tf_op jit(solution)/shard_map/ppermute | solution.py:261
  79.5 18.8 %collective-permute-start.14 = (f32[4,64,128]{2,1,0:T(8,128)S(1)}, f32[4,64,128]{2,1,0:T(8,128)S(1)}, u32[]{:S(2)}, u32[]{:S(2)}) collective-permute-start(f32[4,64,128]{2,1,0:T(8,128)S(1)} %get-tuple-element.52), channel_id=1, source_target_pairs={{0,6},{1,7},{2,4},{3,5},{4,2},{5,3},{6,0},{7,1},{8,14},{9,15},{10,... | collective-permute-start | bytes 393224 | tf_op jit(solution)/shard_map/ppermute | solution.py:261
  90.4 11.4 %collective-permute-start.15 = (f32[4,64,128]{2,1,0:T(8,128)S(1)}, f32[4,64,128]{2,1,0:T(8,128)S(1)}, u32[]{:S(2)}, u32[]{:S(2)}) collective-permute-start(f32[4,64,128]{2,1,0:T(8,128)S(1)} %get-tuple-element.53), channel_id=1, source_target_pairs={{0,7},{1,6},{2,5},{3,4},{4,3},{5,2},{6,1},{7,0},{8,15},{9,14},{10,... | collective-permute-start | bytes 393224 | tf_op jit(solution)/shard_map/ppermute | solution.py:261
  93.0 8.9 %collective-permute-start.9 = (f32[4,64,128]{2,1,0:T(8,128)S(1)}, f32[4,64,128]{2,1,0:T(8,128)S(1)}, u32[]{:S(2)}, u32[]{:S(2)}) collective-permute-start(f32[4,64,128]{2,1,0:T(8,128)S(1)} %get-tuple-element.47), channel_id=1, source_target_pairs={{0,1},{1,0},{2,3},{3,2},{4,5},{5,4},{6,7},{7,6},{8,9},{9,8},{10,11... | collective-permute-start | bytes 393224 | tf_op jit(solution)/shard_map/ppermute | solution.py:261
  102.1 5.4 %copy-start.2 = (f32[2048,128]{1,0:T(8,128)S(1)}, f32[2048,128]{1,0:T(8,128)}, u32[]{:S(2)}) copy-start(f32[2048,128]{1,0:T(8,128)} %copy-done.1) | copy-start | bytes 3145732
  103.7 10.9 %all-to-all-start.2 = ((f32[32,1,32]{2,1,0:T(1,128)}), f32[32,1,32]{2,1,0:T(1,128)S(1)}, u32[]{:S(2)}, u32[]{:S(2)}) async-start(f32[32,1,32]{2,1,0:T(1,128)} %bitcast.10), calls=%async_computation.2 | async-start | bytes 32768 | tf_op jit(solution)/shard_map/all_to_all | solution.py:273

commit v2 on v1

--- a/solution.py
+++ b/solution.py
@@ -179,36 +179,46 @@
     )(padded, shell_index)
 
 
-def tile_kernel(own, tiles):
-    tiles[...] = stacked(own[...])
-
-
-def tiled(own):
-    return pl.pallas_call(
-        tile_kernel,
-        out_shape=jax.ShapeDtypeStruct((own.size // LANES, LANES), f32),
-        in_specs=[VMEM],
-        out_specs=VMEM,
+def pieces_kernel(g, place, own, *outs):
+    tiles = outs[0].shape[0] // g
+    for k, out in enumerate(outs):
+        first = jnp.bitwise_xor(place[0], k) * tiles
+        for t in range(tiles):
+            cols = pl.ds(pl.multiple_of((first + t) * LANES, LANES), LANES)
+            out[t * g : (t + 1) * g, :] = own[:, cols]
+
+
+def cut_by_layer(own, place, layers):
+    g = own.shape[0]
+    rows = own.size // LANES // layers
+    return pl.pallas_call(
+        functools.partial(pieces_kernel, g),
+        out_shape=[jax.ShapeDtypeStruct((rows, LANES), f32)] * layers,
+        in_specs=[pl.BlockSpec(memory_space=pltpu.SMEM), VMEM],
+        out_specs=[VMEM] * layers,
         compiler_params=pltpu.CompilerParams(vmem_limit_bytes=8 * 2**20),
-    )(own)
-
-
-def regroup_kernel(place, columns, done, *outs):
+    )(place, own)
+
+
+def regroup_kernel(place, done, *refs):
+    outs = refs[-LAYER:]
     rows = outs[0].shape[1]
     for k, out in enumerate(outs):
-        first = pl.multiple_of(jnp.bitwise_xor(place[0], k) * rows, rows)
-        out[...] = columns[:, pl.ds(first, rows), :]
-
-
-def regroup(columns, place, done):
-    layers, rows = columns.shape[0], columns.shape[1] // LAYER
+        first = pl.multiple_of(jnp.bitwise_xor(place[1], k) * rows, rows)
+        for layer, piece in enumerate(refs[:-LAYER]):
+            out[layer] = piece[pl.ds(first, rows), :]
+
+
+def regroup(pieces, place, done):
+    rows = pieces[0].shape[0] // LAYER
     return pl.pallas_call(
         regroup_kernel,
-        out_shape=[jax.ShapeDtypeStruct((layers, rows, LANES), f32)] * LAYER,
-        in_specs=[pl.BlockSpec(memory_space=pltpu.SMEM), VMEM, pl.BlockSpec(memory_space=pl.ANY)],
+        out_shape=[jax.ShapeDtypeStruct((len(pieces), rows, LANES), f32)] * LAYER,
+        in_specs=[pl.BlockSpec(memory_space=pltpu.SMEM), pl.BlockSpec(memory_space=pl.ANY)]
+        + [VMEM] * len(pieces),
         out_specs=[VMEM] * LAYER,
         compiler_params=pltpu.CompilerParams(vmem_limit_bytes=8 * 2**20),
-    )(place, columns, done)
+    )(place, done, *pieces)
 
 
 def margin_kernel(scale, place, terms, *refs):
@@ -240,7 +250,7 @@
     by_distance = jnp.dot(summed, pick, precision=highest, preferred_element_type=f32)
     row = lax.broadcasted_iota(jnp.int32, (count, count), 0)
     col = lax.broadcasted_iota(jnp.int32, (count, count), 1)
-    order = (jnp.bitwise_xor(row, place[0]) == col).astype(f32)
+    order = (jnp.bitwise_xor(row, place[2]) == col).astype(f32)
     out[...] = scale * jnp.dot(order, by_distance, precision=highest, preferred_element_type=f32)
 
 
@@ -283,7 +293,7 @@
     consts = tables(g)
     own = orbitals.reshape(g, g * g)
     layers = count // LAYER
-    along = [[layer * LAYER + k for layer in range(layers)] for k in range(LAYER)]
+    place = jnp.stack([me // LAYER, me % LAYER, me]).astype(jnp.int32)
 
     def swap(value, distance=1):
         return permute(value, lambda d: d ^ distance, count)
@@ -291,13 +301,13 @@
     starts = [sum(CHUNKS[:k]) for k in range(len(CHUNKS))]
     near = [swap(own[start : start + size], 2) for start, size in zip(starts, CHUNKS)]
     peer = swap(own)
-    by_tile, kernel_values = after(tiled(own), kernel_values)
-    columns = exchange(by_tile.reshape(layers, -1, LANES), along)
+    pieces = list(cut_by_layer(own, place, layers))
+    pieces[:-1] = [pieces[0]] + [swap(pieces[k], k * LAYER) for k in range(1, layers - 1)]
 
     kern = lookup(kernel_values, shell_index)
     far = [None] * 2
     term, done = pair(own, [], None, kern, consts)
-    near[0], done = after(near[0], done)
+    near[0], pieces[1:-1], done = after(near[0], pieces[1:-1], done)
     far[0] = permute(near[0], far_target, count)
     term, done = pair(own, [peer], (term, done), kern, consts)
     near[1], done = after(near[1], done)
@@ -305,12 +315,13 @@
     near_cross = [swap(part) for part in near]
     use_near = (((me + 1) // 2) % 2).astype(jnp.int32).reshape(1)
     term, done = pair(own, near, (term, done), kern, consts)
-    far[1], done = after(far[1], done)
+    far[1], pieces[-1], done = after(far[1], pieces[-1], done)
+    pieces[-1] = swap(pieces[-1], (layers - 1) * LAYER)
     far_cross = [swap(part) for part in far]
     term, done = pair(own, far, (term, done), kern, consts)
     tiles, done = pair(own, near_cross, (term, done), kern, consts, far_cross, use_near, tiles=True)
-    place = (me % LAYER).astype(jnp.int32).reshape(1)
-    columns = list(regroup(columns, place, done))
+    tiles, pieces[-1] = after(tiles, pieces[-1])
+    columns = list(regroup(pieces, place, done))
     columns = [columns[0]] + [swap(columns[k], k) for k in range(1, LAYER)]
     spread_terms = exchange(tiles.reshape(count, -1, LANES))
     term = tiles.reshape(g * g // LANES, g, LANES).transpose(1, 0, 2).reshape(orbitals.shape)

time: 116 us -> 108 us (0.931)
  waiting for transfers between devices: 46.5 us -> 40 us
  starting transfers between devices: 30.7 us -> 28.7 us
  Pallas kernels: 28.1 us -> 29.8 us
  local copies, waits for them, and re-layouts: 8.4 us -> 7.2 us
    all_to_all x3 -> x2, starting transfers between devices: 15.7 us -> 9.52 us  [exchange(): lax.all_to_all(value, 'band', split_axis=0, concat_axis=0, tiled=True, ax...]
    ppermute x16 -> x19, waiting for transfers between devices: 41 us -> 35.6 us  [permute(): lax.ppermute(value, 'band', [(source, target(source) % count) for source...]
    ppermute x16 -> x19, starting transfers between devices: 15 us -> 19.1 us  [permute(): lax.ppermute(value, 'band', [(source, target(source) % count) for source...]
    unnamed x18 -> x22, local copies, waits for them, and re-layouts: 4.39 us -> 1.96 us
    pallas_call x2, Pallas kernels: 1.12 us -> 2.44 us  [the longest x1 1.41 us: cut_by_layer(): pl.pallas_call(functools.partial(pieces_kernel, g), out_shape=[jax.ShapeD...]
    transpose x1, local copies, waits for them, and re-layouts: 0.61 us -> 1.84 us  [local(): tiles.reshape(g * g // LANES, g, LANES).transpose(1, 0, 2)]
    all_to_all x3 -> x2, waiting for transfers between devices: 5.55 us -> 4.34 us  [exchange(): lax.all_to_all(value, 'band', split_axis=0, concat_axis=0, tiled=True, ax...]
  transfers between devices with their start and end apart: 19 -> 21, of which waited for: 9 -> 12; matrix products, arithmetic and copies ran while one was open for 3% -> 5% of each run, Pallas kernels for 23% -> 26%
where the time goes in v2:
time: 108 us; the launch traced here: 107 us
  waiting for transfers between devices  40 us (37%)
  Pallas kernels  29.8 us (28%)
  starting transfers between devices  28.7 us (27%)
  local copies, waits for them, and re-layouts  7.2 us (7%)
    ppermute x19, waiting for transfers between devices, permute(): lax.ppermute(value, 'band', [(source, target(source) % count) for source...  35.6 us
    pallas_call x5, Pallas kernels, pair(): pl.pallas_call(functools.partial(pair_kernel, g, len(right), len(other),...  22.3 us
    ppermute x19, starting transfers between devices, permute(): lax.ppermute(value, 'band', [(source, target(source) % count) for source...  19.1 us
    all_to_all x2, starting transfers between devices, exchange(): lax.all_to_all(value, 'band', split_axis=0, concat_axis=0, tiled=True, ax...  9.52 us
    all_to_all x2, waiting for transfers between devices, exchange(): lax.all_to_all(value, 'band', split_axis=0, concat_axis=0, tiled=True, ax...  4.34 us
    pallas_call x1, Pallas kernels, lookup(): pl.pallas_call(functools.partial(lookup_kernel, -1.0 / g ** 3), out_shape...  2.82 us
    slice x1, local copies, waits for them, and re-layouts, local(): own[start:start + size]  2.24 us
    pallas_call x1, Pallas kernels, partial_margin(): pl.pallas_call(functools.partial(margin_kernel, 1.0 / points), out_shape=...  2.22 us
  transfers between devices with their start and end apart: 21, of which 12 were waited for; matrix products, arithmetic and copies ran while one was open for 5% of the time, Pallas kernels for 26%

profile of v2, /device:TPU:0, one launch (start us, length us, event | category | flops | bytes accessed | tf_op | source)
XLA Modules:
  0.0 107.1 jit_solution(15911635201197314131)
XLA Ops:
  0.6 0.0 copy-start
  0.6 0.5 collective-permute-start.5
  1.2 2.2 %slice_bitcast_fusion = (f32[32,4096]{1,0:T(8,128)}, f32[32,4096]{1,0:T(8,128)}) fusion(f32[1,64,4096]{2,1,0:T(8,128)} %param.5), kind=kLoop, calls=%fused_computation | loop fusion | bytes 2097152 | tf_op jit(solution)/shard_map/slice | solution.py:302
  3.4 2.6 %collective-permute-start = (f32[32,4096]{1,0:T(8,128)}, f32[32,4096]{1,0:T(8,128)}, u32[]{:S(2)}, u32[]{:S(2)}) collective-permute-start(f32[32,4096]{1,0:T(8,128)} %get-tuple-element.69), channel_id=1, source_target_pairs={{0,2},{1,3},{2,0},{3,1},{4,6},{5,7},{6,4},{7,5},{8,10},{9,11},{10,... | collective-permute-start | bytes 1572872 | tf_op jit(solution)/shard_map/ppermute | solution.py:271
  6.0 0.0 collective-permute-start.4
  6.0 0.1 pad_add_fusion.place
  6.1 0.0 copy-done
  6.1 1.4 %shard_map.68 = (f32[512,128]{1,0:T(8,128)S(1)}, f32[512,128]{1,0:T(8,128)S(1)}, f32[512,128]{1,0:T(8,128)S(1)}, f32[512,128]{1,0:T(8,128)}) custom-call(s32[3]{0:T(128)S(1)} %pad_add_fusion.place, f32[64,4096]{1,0:T(8,128)S(1)} %bitcast.19), custom_call_target="tpu_custom_call" | custom-call | tf_op jit(solution)/shard_map/pallas_call | solution.py:194
  7.5 0.7 copy-done.4
  8.2 2.1 %collective-permute-start.1 = (f32[512,128]{1,0:T(8,128)S(1)}, f32[512,128]{1,0:T(8,128)S(1)}, u32[]{:S(2)}, u32[]{:S(2)}) collective-permute-start(f32[512,128]{1,0:T(8,128)S(1)} %get-tuple-element.35), channel_id=1, source_target_pairs={{0,8},{1,9},{2,10},{3,11},{4,12},{5,13},{6,14},{7,15},{8,0},{9,1},... | collective-permute-start | bytes 786440 | tf_op jit(solution)/shard_map/ppermute | solution.py:271
  10.3 2.6 %collective-permute-start.2 = (f32[512,128]{1,0:T(8,128)S(1)}, f32[512,128]{1,0:T(8,128)S(1)}, u32[]{:S(2)}, u32[]{:S(2)}) collective-permute-start(f32[512,128]{1,0:T(8,128)S(1)} %get-tuple-element.36), channel_id=1, source_target_pairs={{0,16},{1,17},{2,18},{3,19},{4,20},{5,21},{6,22},{7,23},{8,24},{9,... | collective-permute-start | bytes 786440 | tf_op jit(solution)/shard_map/ppermute | solution.py:271
  12.9 0.0 copy-done.10
  12.9 1.2 %copy-done.2 = s32[64,4096]{1,0:T(8,128)S(1)} copy-done((s32[64,4096]{1,0:T(8,128)S(1)}, s32[64,4096]{1,0:T(8,128)}, u32[]{:S(2)}) %copy-start.2) | copy-done | bytes 1048600
  14.1 2.8 %shard_map.69.refs_1_.refs_4_.refs_5_.refs_8_ = f32[2048,128]{1,0:T(8,128)S(1)} custom-call(f32[1,128]{1,0:T(1,128)S(1)} %pad_bitcast_fusion.values, s32[64,4096]{1,0:T(8,128)S(1)} %copy-done.2), custom_call_target="tpu_custom_call" | custom-call | tf_op jit(solution)/shard_map/pallas_call | solution.py:173
  16.9 0.0 copy-done.1
  16.9 0.0 copy-done.3
  16.9 3.4 %shard_map.70 = (f32[64,4096]{1,0:T(8,128)S(1)}, f32[8,128]{1,0:T(8,128)S(1)}) custom-call(f32[64,4096]{1,0:T(8,128)S(1)} %bitcast.20, f32[2048,128]{1,0:T(8,128)S(1)} %shard_map.69.refs_1_.refs_4_.refs_5_.refs_8_, bf16[64,192]{1,0:T(8,128)(2,1)S(1)} %copy-done.3, bf16[256,256]{1,0:T(8,128)(2,1)S(1)} %copy-done.1), custom_call_target="tpu_custom_call" | custom-call | flops 262144 | bytes 262144 | tf_op jit(solution)/shard_map/pallas_call | solution.py:138
  20.4 1.8 %collective-permute-done.1.refs_1_ = f32[512,128]{1,0:T(8,128)S(1)} collective-permute-done((f32[512,128]{1,0:T(8,128)S(1)}, f32[512,128]{1,0:T(8,128)S(1)}, u32[]{:S(2)}, u32[]{:S(2)}) %collective-permute-start.1) | collective-permute-done | bytes 262176 | tf_op jit(solution)/shard_map/ppermute | solution.py:271
  22.1 2.5 %collective-permute-done.2.refs_2_ = f32[512,128]{1,0:T(8,128)S(1)} collective-permute-done((f32[512,128]{1,0:T(8,128)S(1)}, f32[512,128]{1,0:T(8,128)S(1)}, u32[]{:S(2)}, u32[]{:S(2)}) %collective-permute-start.2) | collective-permute-done | bytes 262176 | tf_op jit(solution)/shard_map/ppermute | solution.py:271
  24.6 0.0 collective-permute-done.refs_1_
  24.6 1.5 %collective-permute-start.7 = (f32[32,4096]{1,0:T(8,128)}, f32[32,4096]{1,0:T(8,128)}, u32[]{:S(2)}, u32[]{:S(2)}) collective-permute-start(f32[32,4096]{1,0:T(8,128)} %collective-permute-done.refs_1_), channel_id=1, source_target_pairs={{0,4},{1,5},{2,30},{3,31},{4,8},{5,9},{6,2},{7,3},{8,12},{9,13},{1... | collective-permute-start | bytes 1572872 | tf_op jit(solution)/shard_map/ppermute | solution.py:271
  26.2 0.0 collective-permute-done.5.refs_1_
  26.2 3.5 %shard_map.71 = (f32[64,4096]{1,0:T(8,128)S(1)}, f32[8,128]{1,0:T(8,128)S(1)}) custom-call(f32[64,4096]{1,0:T(8,128)S(1)} %bitcast.21, f32[64,4096]{1,0:T(8,128)S(1)} %collective-permute-done.5.refs_1_, f32[64,4096]{1,0:T(8,128)S(1)} %get-tuple-element.39.refs_2_, f32[8,128]{1,0:T(8,128)S(1)} %get-tuple-element.40.refs_3_, ...), custom_call_target="tpu_custom_call" | custom-call | flops 262144 | bytes 262144 | tf_op jit(solution)/shard_map/pallas_call | solution.py:138
  29.7 0.0 copy-done.6
  29.7 0.3 collective-permute-done.4.refs_2_
  30.0 1.8 %collective-permute-start.9 = (f32[32,4096]{1,0:T(8,128)}, f32[32,4096]{1,0:T(8,128)}, u32[]{:S(2)}, u32[]{:S(2)}) collective-permute-start(f32[32,4096]{1,0:T(8,128)} %collective-permute-done.4.refs_2_), channel_id=1, source_target_pairs={{0,4},{1,5},{2,30},{3,31},{4,8},{5,9},{6,2},{7,3},{8,12},{9,13},{1... | collective-permute-start | bytes 1572872 | tf_op jit(solution)/shard_map/ppermute | solution.py:271
  31.8 0.0 collective-permute-start.3
  31.8 0.5 collective-permute-start.6
  32.3 4.7 %shard_map.72 = (f32[64,4096]{1,0:T(8,128)S(1)}, f32[8,128]{1,0:T(8,128)S(1)}) custom-call(f32[64,4096]{1,0:T(8,128)S(1)} %bitcast.22, f32[32,4096]{1,0:T(8,128)} %collective-permute-done.refs_1_, f32[32,4096]{1,0:T(8,128)} %collective-permute-done.4.refs_2_, f32[64,4096]{1,0:T(8,128)S(1)} %get-tuple-element.44.refs_3_, ...), custom_call_target="tpu_custom_call" | custom-call | flops 262144 | bytes 262144 | tf_op jit(solution)/shard_map/pallas_call | solution.py:138
  37.0 4.2 %collective-permute-done.7.refs_1_ = f32[32,4096]{1,0:T(8,128)} collective-permute-done((f32[32,4096]{1,0:T(8,128)}, f32[32,4096]{1,0:T(8,128)}, u32[]{:S(2)}, u32[]{:S(2)}) %collective-permute-start.7) | collective-permute-done | bytes 524320 | tf_op jit(solution)/shard_map/ppermute | solution.py:271
  41.2 0.0 collective-permute-start.8
  41.2 8.5 %collective-permute-done.9.refs_2_ = f32[32,4096]{1,0:T(8,128)} collective-permute-done((f32[32,4096]{1,0:T(8,128)}, f32[32,4096]{1,0:T(8,128)}, u32[]{:S(2)}, u32[]{:S(2)}) %collective-permute-start.9) | collective-permute-done | bytes 524320 | tf_op jit(solution)/shard_map/ppermute | solution.py:271
  49.7 0.0 collective-permute-start.10
  49.7 1.0 collective-permute-start.11
  50.7 4.6 %shard_map.73 = (f32[64,4096]{1,0:T(8,128)S(1)}, f32[8,128]{1,0:T(8,128)S(1)}) custom-call(f32[64,4096]{1,0:T(8,128)S(1)} %bitcast.23, f32[32,4096]{1,0:T(8,128)} %collective-permute-done.7.refs_1_, f32[32,4096]{1,0:T(8,128)} %collective-permute-done.9.refs_2_, f32[64,4096]{1,0:T(8,128)S(1)} %get-tuple-element.48.refs_3_, ...), custom_call_target="tpu_custom_call" | custom-call | flops 262144 | bytes 262144 | tf_op jit(solution)/shard_map/pallas_call | solution.py:138
  55.3 0.0 collective-permute-done.3.refs_1_
  55.3 0.0 collective-permute-done.6.refs_2_
  55.3 0.0 collective-permute-done.8.refs_3_
  55.3 0.0 collective-permute-done.10.refs_4_
  55.3 6.0 %shard_map.74 = (f32[2048,128]{1,0:T(8,128)}, f32[8,128]{1,0:T(8,128)S(1)}) custom-call(f32[64,4096]{1,0:T(8,128)S(1)} %bitcast.24, f32[32,4096]{1,0:T(8,128)} %collective-permute-done.3.refs_1_, f32[32,4096]{1,0:T(8,128)} %collective-permute-done.6.refs_2_, f32[32,4096]{1,0:T(8,128)} %collective-permute-done.8.refs_3_, ...), custom_call_target="tpu_custom_call" | custom-call | flops 262144 | bytes 262144 | tf_op jit(solution)/shard_map/pallas_call | solution.py:138
  61.4 0.0 collective-permute-done.11.refs_3_
  61.4 5.8 %all-to-all-start = ((f32[32,64,128]{2,1,0:T(8,128)}), f32[32,64,128]{2,1,0:T(8,128)S(1)}, u32[]{:S(2)}, u32[]{:S(2)}) async-start(f32[32,64,128]{2,1,0:T(8,128)} %bitcast.8), calls=%async_computation | async-start | bytes 2097152 | tf_op jit(solution)/shard_map/all_to_all | solution.py:283
  67.3 1.0 shard_map.75
  68.3 0.3 collective-permute-start.12
  68.6 1.7 %collective-permute-start.13 = (f32[4,64,128]{2,1,0:T(8,128)S(1)}, f32[4,64,128]{2,1,0:T(8,128)S(1)}, u32[]{:S(2)}, u32[]{:S(2)}) collective-permute-start(f32[4,64,128]{2,1,0:T(8,128)S(1)} %get-tuple-element.62), channel_id=1, source_target_pairs={{0,2},{1,3},{2,0},{3,1},{4,6},{5,7},{6,4},{7,5},{8,10},{9,11},{10,... | collective-permute-start | bytes 393224 | tf_op jit(solution)/shard_map/ppermute | solution.py:271
  70.3 0.0 collective-permute-start.14
  70.3 1.7 %collective-permute-start.15 = (f32[4,64,128]{2,1,0:T(8,128)S(1)}, f32[4,64,128]{2,1,0:T(8,128)S(1)}, u32[]{:S(2)}, u32[]{:S(2)}) collective-permute-start(f32[4,64,128]{2,1,0:T(8,128)S(1)} %get-tuple-element.64), channel_id=1, source_target_pairs={{0,4},{1,5},{2,6},{3,7},{4,0},{5,1},{6,2},{7,3},{8,12},{9,13},{10,... | collective-permute-start | bytes 393224 | tf_op jit(solution)/shard_map/ppermute | solution.py:271
  72.0 0.1 collective-permute-start.16
  72.1 0.0 collective-permute-done.12.refs_1_
  72.1 2.6 %collective-permute-start.17 = (f32[4,64,128]{2,1,0:T(8,128)S(1)}, f32[4,64,128]{2,1,0:T(8,128)S(1)}, u32[]{:S(2)}, u32[]{:S(2)}) collective-permute-start(f32[4,64,128]{2,1,0:T(8,128)S(1)} %get-tuple-element.66), channel_id=1, source_target_pairs={{0,6},{1,7},{2,4},{3,5},{4,2},{5,3},{6,0},{7,1},{8,14},{9,15},{10,... | collective-permute-start | bytes 393224 | tf_op jit(solution)/shard_map/ppermute | solution.py:271
  74.7 7.1 %collective-permute-done.13.refs_2_ = f32[4,64,128]{2,1,0:T(8,128)S(1)} collective-permute-done((f32[4,64,128]{2,1,0:T(8,128)S(1)}, f32[4,64,128]{2,1,0:T(8,128)S(1)}, u32[]{:S(2)}, u32[]{:S(2)}) %collective-permute-start.13) | collective-permute-done | bytes 131104 | tf_op jit(solution)/shard_map/ppermute | solution.py:271
  81.9 0.2 collective-permute-start.18
  82.0 2.4 %collective-permute-done.14.refs_3_ = f32[4,64,128]{2,1,0:T(8,128)S(1)} collective-permute-done((f32[4,64,128]{2,1,0:T(8,128)S(1)}, f32[4,64,128]{2,1,0:T(8,128)S(1)}, u32[]{:S(2)}, u32[]{:S(2)}) %collective-permute-start.14) | collective-permute-done | bytes 131104 | tf_op jit(solution)/shard_map/ppermute | solution.py:271
  84.4 0.0 collective-permute-done.15.refs_4_
  84.4 0.1 collective-permute-done.16.refs_5_
  84.5 5.2 %collective-permute-done.17.refs_6_ = f32[4,64,128]{2,1,0:T(8,128)S(1)} collective-permute-done((f32[4,64,128]{2,1,0:T(8,128)S(1)}, f32[4,64,128]{2,1,0:T(8,128)S(1)}, u32[]{:S(2)}, u32[]{:S(2)}) %collective-permute-start.17) | collective-permute-done | bytes 131104 | tf_op jit(solution)/shard_map/ppermute | solution.py:271
  89.7 3.5 %collective-permute-done.18.refs_7_ = f32[4,64,128]{2,1,0:T(8,128)S(1)} collective-permute-done((f32[4,64,128]{2,1,0:T(8,128)S(1)}, f32[4,64,128]{2,1,0:T(8,128)S(1)}, u32[]{:S(2)}, u32[]{:S(2)}) %collective-permute-start.18) | collective-permute-done | bytes 131104 | tf_op jit(solution)/shard_map/ppermute | solution.py:271
  93.3 0.2 all-to-all-done.terms
  93.5 2.2 %shard_map.76 = f32[32,32]{1,0:T(8,128)} custom-call(s32[3]{0:T(128)S(1)} %pad_add_fusion.place, f32[32,64,128]{2,1,0:T(8,128)S(1)} %all-to-all-done.terms, f32[4,64,128]{2,1,0:T(8,128)S(1)} %get-tuple-element.60.refs_0_, f32[4,64,128]{2,1,0:T(8,128)S(1)} %collective-permute-done.12.refs_1_, f32[4,64,128]{2,1,0:T(8,128)S(1)} %collective-permute-done.13.refs_2_, ...), custom_call_target="tpu_custom_call" | custom-call | tf_op jit(solution)/shard_map/pallas_call | solution.py:259
  95.7 3.7 %all-to-all-start.1 = ((f32[32,1,32]{2,1,0:T(1,128)}), f32[32,1,32]{2,1,0:T(1,128)S(1)}, u32[]{:S(2)}, u32[]{:S(2)}) async-start(f32[32,1,32]{2,1,0:T(1,128)} %bitcast.11), calls=%async_computation.1 | async-start | bytes 32768 | tf_op jit(solution)/shard_map/all_to_all | solution.py:283
  99.4 1.8 %copy.8 = f32[64,32,128]{2,1,0:T(8,128)S(1)} copy(f32[64,32,128]{2,0,1:T(8,128)} %bitcast.9) | data formatting | bytes 2097152 | tf_op jit(solution)/shard_map/transpose | solution.py:327
  101.3 1.2 %reshape.28 = f32[1,64,4096]{2,1,0:T(8,128)} reshape(f32[64,32,128]{2,1,0:T(8,128)S(1)} %copy.8) | data formatting | bytes 2097152 | tf_op jit(solution)/shard_map/reshape | solution.py:327
  102.4 4.1 %all-to-all-done.1 = f32[32,1,32]{2,1,0:T(1,128)S(1)} async-done(((f32[32,1,32]{2,1,0:T(1,128)}), f32[32,1,32]{2,1,0:T(1,128)S(1)}, u32[]{:S(2)}, u32[]{:S(2)}) %all-to-all-start.1) | async-done | bytes 4128 | tf_op jit(solution)/shard_map/all_to_all | solution.py:283
  106.6 0.6 reduce_sum.9
  (15 shorter events, 0.0 us)
Async XLA Ops:
  0.6 5.5 %copy-start = (f32[1,64,4096]{2,1,0:T(8,128)S(1)}, f32[1,64,4096]{2,1,0:T(8,128)}, u32[]{:S(2)}) copy-start(f32[1,64,4096]{2,1,0:T(8,128)} %param.5) | copy-start | bytes 3145732
  0.6 25.5 %collective-permute-start.5 = (f32[64,4096]{1,0:T(8,128)}, f32[64,4096]{1,0:T(8,128)S(1)}, u32[]{:S(2)}, u32[]{:S(2)}) collective-permute-start(f32[64,4096]{1,0:T(8,128)} %bitcast.18), channel_id=1, source_target_pairs={{0,1},{1,0},{2,3},{3,2},{4,5},{5,4},{6,7},{7,6},{8,9},{9,8},{10,11... | collective-permute-start | bytes 3145736 | tf_op jit(solution)/shard_map/ppermute | solution.py:271
  3.4 21.2 %collective-permute-start = (f32[32,4096]{1,0:T(8,128)}, f32[32,4096]{1,0:T(8,128)}, u32[]{:S(2)}, u32[]{:S(2)}) collective-permute-start(f32[32,4096]{1,0:T(8,128)} %get-tuple-element.69), channel_id=1, source_target_pairs={{0,2},{1,3},{2,0},{3,1},{4,6},{5,7},{6,4},{7,5},{8,10},{9,11},{10,... | collective-permute-start | bytes 1572872 | tf_op jit(solution)/shard_map/ppermute | solution.py:271
  6.0 24.1 %collective-permute-start.4 = (f32[32,4096]{1,0:T(8,128)}, f32[32,4096]{1,0:T(8,128)}, u32[]{:S(2)}, u32[]{:S(2)}) collective-permute-start(f32[32,4096]{1,0:T(8,128)} %get-tuple-element.68), channel_id=1, source_target_pairs={{0,2},{1,3},{2,0},{3,1},{4,6},{5,7},{6,4},{7,5},{8,10},{9,11},{10,... | collective-permute-start | bytes 1572872 | tf_op jit(solution)/shard_map/ppermute | solution.py:271
  7.5 0.7 copy-start.4
  8.2 4.7 %copy-start.10 = (f32[32]{0:T(128)S(1)}, f32[32]{0:T(128)}, u32[]{:S(2)}) copy-start(f32[32]{0:T(128)} %param.6) | copy-start | bytes 388
  8.2 13.9 %collective-permute-start.1 = (f32[512,128]{1,0:T(8,128)S(1)}, f32[512,128]{1,0:T(8,128)S(1)}, u32[]{:S(2)}, u32[]{:S(2)}) collective-permute-start(f32[512,128]{1,0:T(8,128)S(1)} %get-tuple-element.35), channel_id=1, source_target_pairs={{0,8},{1,9},{2,10},{3,11},{4,12},{5,13},{6,14},{7,15},{8,0},{9,1},... | collective-permute-start | bytes 786440 | tf_op jit(solution)/shard_map/ppermute | solution.py:271
  10.3 14.4 %collective-permute-start.2 = (f32[512,128]{1,0:T(8,128)S(1)}, f32[512,128]{1,0:T(8,128)S(1)}, u32[]{:S(2)}, u32[]{:S(2)}) collective-permute-start(f32[512,128]{1,0:T(8,128)S(1)} %get-tuple-element.36), channel_id=1, source_target_pairs={{0,16},{1,17},{2,18},{3,19},{4,20},{5,21},{6,22},{7,23},{8,24},{9,... | collective-permute-start | bytes 786440 | tf_op jit(solution)/shard_map/ppermute | solution.py:271
  12.9 1.2 %copy-start.2 = (s32[64,4096]{1,0:T(8,128)S(1)}, s32[64,4096]{1,0:T(8,128)}, u32[]{:S(2)}) copy-start(s32[64,4096]{1,0:T(8,128)} %index.1) | copy-start | bytes 3145732
  14.1 2.8 %copy-start.1 = (bf16[256,256]{1,0:T(8,128)(2,1)S(1)}, bf16[256,256]{1,0:T(8,128)(2,1)}, u32[]{:S(2)}) copy-start(bf16[256,256]{1,0:T(8,128)(2,1)} %constant.57.clone.refs_3_.refs_6_.refs_7_.refs_10_) | copy-start | bytes 393220
  14.1 2.8 %copy-start.3 = (bf16[64,192]{1,0:T(8,128)(2,1)S(1)}, bf16[64,192]{1,0:T(8,128)(2,1)}, u32[]{:S(2)}) copy-start(bf16[64,192]{1,0:T(8,128)(2,1)} %constant.56.clone.refs_2_.refs_5_.refs_6_.refs_9_) | copy-start | bytes 73732
  22.1 7.6 %copy-start.6 = (f32[512,128]{1,0:T(8,128)}, f32[512,128]{1,0:T(8,128)S(1)}, u32[]{:S(2)}) copy-start(f32[512,128]{1,0:T(8,128)S(1)} %collective-permute-done.1.refs_1_) | copy-start | bytes 786436
  24.6 5.1 %copy-start.8 = (f32[512,128]{1,0:T(8,128)}, f32[512,128]{1,0:T(8,128)S(1)}, u32[]{:S(2)}) copy-start(f32[512,128]{1,0:T(8,128)S(1)} %collective-permute-done.2.refs_2_) | copy-start | bytes 786436
  24.6 16.5 %collective-permute-start.7 = (f32[32,4096]{1,0:T(8,128)}, f32[32,4096]{1,0:T(8,128)}, u32[]{:S(2)}, u32[]{:S(2)}) collective-permute-start(f32[32,4096]{1,0:T(8,128)} %collective-permute-done.refs_1_), channel_id=1, source_target_pairs={{0,4},{1,5},{2,30},{3,31},{4,8},{5,9},{6,2},{7,3},{8,12},{9,13},{1... | collective-permute-start | bytes 1572872 | tf_op jit(solution)/shard_map/ppermute | solution.py:271
  30.0 19.7 %collective-permute-start.9 = (f32[32,4096]{1,0:T(8,128)}, f32[32,4096]{1,0:T(8,128)}, u32[]{:S(2)}, u32[]{:S(2)}) collective-permute-start(f32[32,4096]{1,0:T(8,128)} %collective-permute-done.4.refs_2_), channel_id=1, source_target_pairs={{0,4},{1,5},{2,30},{3,31},{4,8},{5,9},{6,2},{7,3},{8,12},{9,13},{1... | collective-permute-start | bytes 1572872 | tf_op jit(solution)/shard_map/ppermute | solution.py:271
  31.8 23.5 %collective-permute-start.3 = (f32[32,4096]{1,0:T(8,128)}, f32[32,4096]{1,0:T(8,128)}, u32[]{:S(2)}, u32[]{:S(2)}) collective-permute-start(f32[32,4096]{1,0:T(8,128)} %collective-permute-done.refs_1_), channel_id=1, source_target_pairs={{0,1},{1,0},{2,3},{3,2},{4,5},{5,4},{6,7},{7,6},{8,9},{9,8},{10,11... | collective-permute-start | bytes 1572872 | tf_op jit(solution)/shard_map/ppermute | solution.py:271
  31.8 23.5 %collective-permute-start.6 = (f32[32,4096]{1,0:T(8,128)}, f32[32,4096]{1,0:T(8,128)}, u32[]{:S(2)}, u32[]{:S(2)}) collective-permute-start(f32[32,4096]{1,0:T(8,128)} %collective-permute-done.4.refs_2_), channel_id=1, source_target_pairs={{0,1},{1,0},{2,3},{3,2},{4,5},{5,4},{6,7},{7,6},{8,9},{9,8},{10,11... | collective-permute-start | bytes 1572872 | tf_op jit(solution)/shard_map/ppermute | solution.py:271
  41.2 14.2 %collective-permute-start.8 = (f32[32,4096]{1,0:T(8,128)}, f32[32,4096]{1,0:T(8,128)}, u32[]{:S(2)}, u32[]{:S(2)}) collective-permute-start(f32[32,4096]{1,0:T(8,128)} %collective-permute-done.7.refs_1_), channel_id=1, source_target_pairs={{0,1},{1,0},{2,3},{3,2},{4,5},{5,4},{6,7},{7,6},{8,9},{9,8},{10,11... | collective-permute-start | bytes 1572872 | tf_op jit(solution)/shard_map/ppermute | solution.py:271
  49.7 5.6 %collective-permute-start.10 = (f32[32,4096]{1,0:T(8,128)}, f32[32,4096]{1,0:T(8,128)}, u32[]{:S(2)}, u32[]{:S(2)}) collective-permute-start(f32[32,4096]{1,0:T(8,128)} %collective-permute-done.9.refs_2_), channel_id=1, source_target_pairs={{0,1},{1,0},{2,3},{3,2},{4,5},{5,4},{6,7},{7,6},{8,9},{9,8},{10,11... | collective-permute-start | bytes 1572872 | tf_op jit(solution)/shard_map/ppermute | solution.py:271
  49.7 11.7 %collective-permute-start.11 = (f32[512,128]{1,0:T(8,128)}, f32[512,128]{1,0:T(8,128)}, u32[]{:S(2)}, u32[]{:S(2)}) collective-permute-start(f32[512,128]{1,0:T(8,128)} %get-tuple-element.53), channel_id=1, source_target_pairs={{0,24},{1,25},{2,26},{3,27},{4,28},{5,29},{6,30},{7,31},{8,16},{9,... | collective-permute-start | bytes 786440 | tf_op jit(solution)/shard_map/ppermute | solution.py:271
  61.4 5.9 %copy-start.5 = (f32[512,128]{1,0:T(8,128)S(1)}, f32[512,128]{1,0:T(8,128)}, u32[]{:S(2)}) copy-start(f32[512,128]{1,0:T(8,128)} %copy-done.4) | copy-start | bytes 786436
  61.4 5.9 %copy-start.7 = (f32[512,128]{1,0:T(8,128)S(1)}, f32[512,128]{1,0:T(8,128)}, u32[]{:S(2)}) copy-start(f32[512,128]{1,0:T(8,128)} %copy-done.6) | copy-start | bytes 786436
  61.4 5.9 %copy-start.9 = (f32[512,128]{1,0:T(8,128)S(1)}, f32[512,128]{1,0:T(8,128)}, u32[]{:S(2)}) copy-start(f32[512,128]{1,0:T(8,128)} %copy-done.8) | copy-start | bytes 786436
  61.4 32.1 %all-to-all-start = ((f32[32,64,128]{2,1,0:T(8,128)}), f32[32,64,128]{2,1,0:T(8,128)S(1)}, u32[]{:S(2)}, u32[]{:S(2)}) async-start(f32[32,64,128]{2,1,0:T(8,128)} %bitcast.8), calls=%async_computation | async-start | bytes 2097152 | tf_op jit(solution)/shard_map/all_to_all | solution.py:283
  68.3 3.8 %collective-permute-start.12 = (f32[4,64,128]{2,1,0:T(8,128)S(1)}, f32[4,64,128]{2,1,0:T(8,128)S(1)}, u32[]{:S(2)}, u32[]{:S(2)}) collective-permute-start(f32[4,64,128]{2,1,0:T(8,128)S(1)} %get-tuple-element.61), channel_id=1, source_target_pairs={{0,1},{1,0},{2,3},{3,2},{4,5},{5,4},{6,7},{7,6},{8,9},{9,8},{10,11... | collective-permute-start | bytes 393224 | tf_op jit(solution)/shard_map/ppermute | solution.py:271
  68.6 13.2 %collective-permute-start.13 = (f32[4,64,128]{2,1,0:T(8,128)S(1)}, f32[4,64,128]{2,1,0:T(8,128)S(1)}, u32[]{:S(2)}, u32[]{:S(2)}) collective-permute-start(f32[4,64,128]{2,1,0:T(8,128)S(1)} %get-tuple-element.62), channel_id=1, source_target_pairs={{0,2},{1,3},{2,0},{3,1},{4,6},{5,7},{6,4},{7,5},{8,10},{9,11},{10,... | collective-permute-start | bytes 393224 | tf_op jit(solution)/shard_map/ppermute | solution.py:271
  70.3 14.1 %collective-permute-start.14 = (f32[4,64,128]{2,1,0:T(8,128)S(1)}, f32[4,64,128]{2,1,0:T(8,128)S(1)}, u32[]{:S(2)}, u32[]{:S(2)}) collective-permute-start(f32[4,64,128]{2,1,0:T(8,128)S(1)} %get-tuple-element.63), channel_id=1, source_target_pairs={{0,3},{1,2},{2,1},{3,0},{4,7},{5,6},{6,5},{7,4},{8,11},{9,10},{10,... | collective-permute-start | bytes 393224 | tf_op jit(solution)/shard_map/ppermute | solution.py:271
  70.3 14.1 %collective-permute-start.15 = (f32[4,64,128]{2,1,0:T(8,128)S(1)}, f32[4,64,128]{2,1,0:T(8,128)S(1)}, u32[]{:S(2)}, u32[]{:S(2)}) collective-permute-start(f32[4,64,128]{2,1,0:T(8,128)S(1)} %get-tuple-element.64), channel_id=1, source_target_pairs={{0,4},{1,5},{2,6},{3,7},{4,0},{5,1},{6,2},{7,3},{8,12},{9,13},{10,... | collective-permute-start | bytes 393224 | tf_op jit(solution)/shard_map/ppermute | solution.py:271
  72.0 12.5 %collective-permute-start.16 = (f32[4,64,128]{2,1,0:T(8,128)S(1)}, f32[4,64,128]{2,1,0:T(8,128)S(1)}, u32[]{:S(2)}, u32[]{:S(2)}) collective-permute-start(f32[4,64,128]{2,1,0:T(8,128)S(1)} %get-tuple-element.65), channel_id=1, source_target_pairs={{0,5},{1,4},{2,7},{3,6},{4,1},{5,0},{6,3},{7,2},{8,13},{9,12},{10,... | collective-permute-start | bytes 393224 | tf_op jit(solution)/shard_map/ppermute | solution.py:271
  72.1 17.6 %collective-permute-start.17 = (f32[4,64,128]{2,1,0:T(8,128)S(1)}, f32[4,64,128]{2,1,0:T(8,128)S(1)}, u32[]{:S(2)}, u32[]{:S(2)}) collective-permute-start(f32[4,64,128]{2,1,0:T(8,128)S(1)} %get-tuple-element.66), channel_id=1, source_target_pairs={{0,6},{1,7},{2,4},{3,5},{4,2},{5,3},{6,0},{7,1},{8,14},{9,15},{10,... | collective-permute-start | bytes 393224 | tf_op jit(solution)/shard_map/ppermute | solution.py:271
  81.9 11.4 %collective-permute-start.18 = (f32[4,64,128]{2,1,0:T(8,128)S(1)}, f32[4,64,128]{2,1,0:T(8,128)S(1)}, u32[]{:S(2)}, u32[]{:S(2)}) collective-permute-start(f32[4,64,128]{2,1,0:T(8,128)S(1)} %get-tuple-element.67), channel_id=1, source_target_pairs={{0,7},{1,6},{2,5},{3,4},{4,3},{5,2},{6,1},{7,0},{8,15},{9,14},{10,... | collective-permute-start | bytes 393224 | tf_op jit(solution)/shard_map/ppermute | solution.py:271
  95.7 10.9 %all-to-all-start.1 = ((f32[32,1,32]{2,1,0:T(1,128)}), f32[32,1,32]{2,1,0:T(1,128)S(1)}, u32[]{:S(2)}, u32[]{:S(2)}) async-start(f32[32,1,32]{2,1,0:T(1,128)} %bitcast.11), calls=%async_computation.1 | async-start | bytes 32768 | tf_op jit(solution)/shard_map/all_to_all | solution.py:283

commit v3 on v2

--- a/solution.py
+++ b/solution.py
@@ -9,7 +9,7 @@
 from jax.experimental.pallas import tpu as pltpu
 from jax.sharding import PartitionSpec as P
 
-CHUNKS = (32, 32)
+CHUNKS = (1, 1)
 LAYER = 8
 LANES = 128
 SUBLANES = 8
@@ -37,6 +37,12 @@
     return hi, lo
 
 
+def three(value):
+    hi, lo = split(value)
+    last = (value - hi.astype(f32) - lo.astype(f32)).astype(bf16)
+    return [hi, lo, last]
+
+
 def rows_pass(table, value):
     hi, lo = split(value)
     stacked = jnp.concatenate([hi, lo, hi], axis=0)
@@ -78,31 +84,32 @@
     parts = [refs.pop(0) for _ in range(n_right + n_other)]
     flag = refs.pop(0) if n_other else None
     acc, _ = (refs.pop(0), refs.pop(0)) if has_acc else (None, None)
-    kern, rows_table, lanes_table, out, token, work, right, other, sems = refs
+    kern, rows_table, lanes_table, out, token, work, right, sems = refs
     half = g // 2
     count = g * g // LANES
     table = rows_table[...]
     wide = lanes_table[...]
 
-    copies = []
-    filled = 0
-    for k, part in enumerate(parts):
-        filled = 0 if k == n_right else filled
-        place = pl.ds(filled, part.shape[0])
-        whole = right if k < n_right else other
-        copies.append(pltpu.make_async_copy(part, whole.at[place, :], sems.at[k]))
-        filled += part.shape[0]
-    for copy in copies:
-        copy.start()
-    for copy in copies:
-        copy.wait()
+    def fetch(chosen):
+        copies = []
+        filled = 0
+        for k, part in enumerate(chosen):
+            place = pl.ds(filled, part.shape[0])
+            copies.append(pltpu.make_async_copy(part, right.at[place, :], sems.at[k]))
+            filled += part.shape[0]
+        for copy in copies:
+            copy.start()
+        for copy in copies:
+            copy.wait()
+
+    if n_other:
+        pl.when(flag[0] > 0)(functools.partial(fetch, parts[:n_right]))
+        pl.when(flag[0] <= 0)(functools.partial(fetch, parts[n_right:]))
+    else:
+        fetch(parts)
 
     def right_block():
-        if not parts:
-            return left[...]
-        if n_other:
-            return jnp.where(flag[0] > 0, right[...], other[...])
-        return right[...]
+        return right[...] if parts else left[...]
 
     value = stacked(rows_pass(table, left[...] * right_block()))
     work[...] = exchange_halves(lanes_pass(value, wide), g)
@@ -146,8 +153,7 @@
         scratch_shapes=[
             pltpu.VMEM((points // LANES, LANES), f32),
             pltpu.VMEM(left.shape if right else (SUBLANES, LANES), f32),
-            pltpu.VMEM(left.shape if other else (SUBLANES, LANES), f32),
-            pltpu.SemaphoreType.DMA((max(1, len(right) + len(other)),)),
+            pltpu.SemaphoreType.DMA((max(1, len(right), len(other)),)),
         ],
         compiler_params=pltpu.CompilerParams(vmem_limit_bytes=10 * 2**20),
         cost_estimate=pl.CostEstimate(flops=points, bytes_accessed=points, transcendentals=0),
@@ -179,7 +185,13 @@
     )(padded, shell_index)
 
 
-def pieces_kernel(g, place, own, *outs):
+def pieces_kernel(place, own, *refs):
+    parts, outs = refs[: len(CHUNKS)], refs[len(CHUNKS) :]
+    g = own.shape[0]
+    start = 0
+    for part in parts:
+        part[...] = own[start : start + part.shape[0], :]
+        start += part.shape[0]
     tiles = outs[0].shape[0] // g
     for k, out in enumerate(outs):
         first = jnp.bitwise_xor(place[0], k) * tiles
@@ -188,16 +200,18 @@
             out[t * g : (t + 1) * g, :] = own[:, cols]
 
 
-def cut_by_layer(own, place, layers):
+def cut(own, place, layers):
     g = own.shape[0]
     rows = own.size // LANES // layers
-    return pl.pallas_call(
-        functools.partial(pieces_kernel, g),
-        out_shape=[jax.ShapeDtypeStruct((rows, LANES), f32)] * layers,
+    shapes = [(g * size // sum(CHUNKS), own.shape[1]) for size in CHUNKS] + [(rows, LANES)] * layers
+    outs = pl.pallas_call(
+        pieces_kernel,
+        out_shape=[jax.ShapeDtypeStruct(shape, f32) for shape in shapes],
         in_specs=[pl.BlockSpec(memory_space=pltpu.SMEM), VMEM],
-        out_specs=[VMEM] * layers,
+        out_specs=[VMEM] * len(shapes),
         compiler_params=pltpu.CompilerParams(vmem_limit_bytes=8 * 2**20),
     )(place, own)
+    return outs[: len(CHUNKS)], list(outs[len(CHUNKS) :])
 
 
 def regroup_kernel(place, done, *refs):
@@ -245,13 +259,20 @@
     summed = jnp.sum(kept.reshape(count, SUBLANES, size), axis=1)
     pick_row = lax.broadcasted_iota(jnp.int32, (size, count), 0) // SUBLANES
     pick_col = lax.broadcasted_iota(jnp.int32, (size, count), 1)
-    pick = (pick_row == pick_col).astype(f32)
-    highest = lax.Precision.HIGHEST
-    by_distance = jnp.dot(summed, pick, precision=highest, preferred_element_type=f32)
+    pick = (pick_row == pick_col).astype(f32).astype(bf16)
+    by_distance = jnp.dot(
+        jnp.concatenate(three(summed), axis=1),
+        jnp.concatenate([pick] * 3, axis=0),
+        preferred_element_type=f32,
+    )
     row = lax.broadcasted_iota(jnp.int32, (count, count), 0)
     col = lax.broadcasted_iota(jnp.int32, (count, count), 1)
-    order = (jnp.bitwise_xor(row, place[2]) == col).astype(f32)
-    out[...] = scale * jnp.dot(order, by_distance, precision=highest, preferred_element_type=f32)
+    order = (jnp.bitwise_xor(row, place[2]) == col).astype(f32).astype(bf16)
+    out[...] = scale * jnp.dot(
+        jnp.concatenate([order] * 3, axis=1),
+        jnp.concatenate(three(by_distance), axis=0),
+        preferred_element_type=f32,
+    )
 
 
 def partial_margin(orbitals, terms, place, points):
@@ -298,10 +319,9 @@
     def swap(value, distance=1):
         return permute(value, lambda d: d ^ distance, count)
 
-    starts = [sum(CHUNKS[:k]) for k in range(len(CHUNKS))]
-    near = [swap(own[start : start + size], 2) for start, size in zip(starts, CHUNKS)]
+    parts, pieces = cut(own, place, layers)
+    near = [swap(part, 2) for part in parts]
     peer = swap(own)
-    pieces = list(cut_by_layer(own, place, layers))
     pieces[:-1] = [pieces[0]] + [swap(pieces[k], k * LAYER) for k in range(1, layers - 1)]
 
     kern = lookup(kernel_values, shell_index)

time: 108 us -> 107 us (level)
  local copies, waits for them, and re-layouts: 7.2 us -> 4.97 us
  waiting for transfers between devices: 40 us -> 41.3 us
    slice x1 -> x0, local copies, waits for them, and re-layouts: 2.24 us -> none  [local(): own[start:start + size]]
    ppermute x19, waiting for transfers between devices: 35.6 us -> 36.9 us  [permute(): lax.ppermute(value, 'band', [(source, target(source) % count) for source...]
  transfers between devices with their start and end apart: 21 -> 21, of which waited for: 12 -> 12; matrix products, arithmetic and copies ran while one was open for 5% -> 3% of each run, Pallas kernels for 26% -> 26%
where the time goes in v3:
time: 107 us; the launch traced here: 106 us
  waiting for transfers between devices  41.3 us (39%)
  Pallas kernels  29.4 us (27%)
  starting transfers between devices  29 us (27%)
  local copies, waits for them, and re-layouts  4.97 us (5%)
    ppermute x19, waiting for transfers between devices, permute(): lax.ppermute(value, 'band', [(source, target(source) % count) for source...  36.9 us
    pallas_call x5, Pallas kernels, pair(): pl.pallas_call(functools.partial(pair_kernel, g, len(right), len(other),...  21.9 us
    ppermute x19, starting transfers between devices, permute(): lax.ppermute(value, 'band', [(source, target(source) % count) for source...  19 us
    all_to_all x2, starting transfers between devices, exchange(): lax.all_to_all(value, 'band', split_axis=0, concat_axis=0, tiled=True, ax...  9.94 us
    all_to_all x2, waiting for transfers between devices, exchange(): lax.all_to_all(value, 'band', split_axis=0, concat_axis=0, tiled=True, ax...  4.34 us
    pallas_call x1, Pallas kernels, lookup(): pl.pallas_call(functools.partial(lookup_kernel, -1.0 / g ** 3), out_shape...  2.82 us
    pallas_call x1, Pallas kernels, partial_margin(): pl.pallas_call(functools.partial(margin_kernel, 1.0 / points), out_shape=...  2.19 us
  transfers between devices with their start and end apart: 21, of which 12 were waited for; matrix products, arithmetic and copies ran while one was open for 3% of the time, Pallas kernels for 26%

profile of v3, /device:TPU:0, one launch (start us, length us, event | category | flops | bytes accessed | tf_op | source)
XLA Modules:
  0.0 106.1 jit_solution(13270300085723529656)
XLA Ops:
  0.6 0.5 collective-permute-start.5
  1.1 0.1 pad_add_fusion.place
  1.2 1.2 %copy-done = f32[1,64,4096]{2,1,0:T(8,128)S(1)} copy-done((f32[1,64,4096]{2,1,0:T(8,128)S(1)}, f32[1,64,4096]{2,1,0:T(8,128)}, u32[]{:S(2)}) %copy-start) | copy-done | bytes 1048600
  2.5 1.5 %shard_map.68 = (f32[32,4096]{1,0:T(8,128)S(1)}, f32[32,4096]{1,0:T(8,128)S(1)}, f32[512,128]{1,0:T(8,128)S(1)}, f32[512,128]{1,0:T(8,128)S(1)}, f32[512,128]{1,0:T(8,128)S(1)}, /*index=5*/f32[512,128]{1,0:T(8,128)}) custom-call(s32[3]{0:T(128)S(1)} %pad_add_fusion.place, f32[64,4096]{1,0:T(8,128)S(1)} %bitcast.15), custom_call_target="tpu_custom_call" | custom-call | tf_op jit(solution)/shard_map/pallas_call | solution.py:207
  3.9 0.7 copy-done.5
  4.6 2.5 %collective-permute-start = (f32[32,4096]{1,0:T(8,128)S(1)}, f32[32,4096]{1,0:T(8,128)}, u32[]{:S(2)}, u32[]{:S(2)}) collective-permute-start(f32[32,4096]{1,0:T(8,128)S(1)} %get-tuple-element.37), channel_id=1, source_target_pairs={{0,2},{1,3},{2,0},{3,1},{4,6},{5,7},{6,4},{7,5},{8,10},{9,11},{10,... | collective-permute-start | bytes 1572872 | tf_op jit(solution)/shard_map/ppermute | solution.py:292
  7.1 0.0 collective-permute-start.4
  7.2 2.1 %collective-permute-start.1 = (f32[512,128]{1,0:T(8,128)S(1)}, f32[512,128]{1,0:T(8,128)S(1)}, u32[]{:S(2)}, u32[]{:S(2)}) collective-permute-start(f32[512,128]{1,0:T(8,128)S(1)} %get-tuple-element.38), channel_id=1, source_target_pairs={{0,8},{1,9},{2,10},{3,11},{4,12},{5,13},{6,14},{7,15},{8,0},{9,1},... | collective-permute-start | bytes 786440 | tf_op jit(solution)/shard_map/ppermute | solution.py:292
  9.2 2.6 %collective-permute-start.2 = (f32[512,128]{1,0:T(8,128)S(1)}, f32[512,128]{1,0:T(8,128)S(1)}, u32[]{:S(2)}, u32[]{:S(2)}) collective-permute-start(f32[512,128]{1,0:T(8,128)S(1)} %get-tuple-element.39), channel_id=1, source_target_pairs={{0,16},{1,17},{2,18},{3,19},{4,20},{5,21},{6,22},{7,23},{8,24},{9,... | collective-permute-start | bytes 786440 | tf_op jit(solution)/shard_map/ppermute | solution.py:292
  11.8 0.0 copy-done.11
  11.8 0.0 copy-start.1
  11.9 0.0 copy-start.2
  11.9 0.0 copy-start.4
  11.9 2.8 %shard_map.69.refs_1_.refs_4_.refs_5_.refs_8_ = f32[2048,128]{1,0:T(8,128)S(1)} custom-call(f32[1,128]{1,0:T(1,128)S(1)} %pad_bitcast_fusion.values, s32[64,4096]{1,0:T(8,128)S(1)} %copy-done.3), custom_call_target="tpu_custom_call" | custom-call | tf_op jit(solution)/shard_map/pallas_call | solution.py:179
  14.7 0.0 copy-done.1
  14.7 0.0 copy-done.2
  14.7 0.0 copy-done.4
  14.7 3.4 %shard_map.70 = (f32[64,4096]{1,0:T(8,128)S(1)}, f32[8,128]{1,0:T(8,128)S(1)}) custom-call(f32[64,4096]{1,0:T(8,128)S(1)} %bitcast.16, f32[2048,128]{1,0:T(8,128)S(1)} %shard_map.69.refs_1_.refs_4_.refs_5_.refs_8_, bf16[64,192]{1,0:T(8,128)(2,1)S(1)} %copy-done.4, bf16[256,256]{1,0:T(8,128)(2,1)S(1)} %copy-done.2), custom_call_target="tpu_custom_call" | custom-call | flops 262144 | bytes 262144 | tf_op jit(solution)/shard_map/pallas_call | solution.py:145
  18.2 3.0 %collective-permute-done.1.refs_1_ = f32[512,128]{1,0:T(8,128)S(1)} collective-permute-done((f32[512,128]{1,0:T(8,128)S(1)}, f32[512,128]{1,0:T(8,128)S(1)}, u32[]{:S(2)}, u32[]{:S(2)}) %collective-permute-start.1) | collective-permute-done | bytes 262176 | tf_op jit(solution)/shard_map/ppermute | solution.py:292
  21.1 2.5 %collective-permute-done.2.refs_2_ = f32[512,128]{1,0:T(8,128)S(1)} collective-permute-done((f32[512,128]{1,0:T(8,128)S(1)}, f32[512,128]{1,0:T(8,128)S(1)}, u32[]{:S(2)}, u32[]{:S(2)}) %collective-permute-start.2) | collective-permute-done | bytes 262176 | tf_op jit(solution)/shard_map/ppermute | solution.py:292
  23.7 0.0 collective-permute-done.refs_1_
  23.7 1.5 %collective-permute-start.7 = (f32[32,4096]{1,0:T(8,128)}, f32[32,4096]{1,0:T(8,128)}, u32[]{:S(2)}, u32[]{:S(2)}) collective-permute-start(f32[32,4096]{1,0:T(8,128)} %collective-permute-done.refs_1_), channel_id=1, source_target_pairs={{0,4},{1,5},{2,30},{3,31},{4,8},{5,9},{6,2},{7,3},{8,12},{9,13},{1... | collective-permute-start | bytes 1572872 | tf_op jit(solution)/shard_map/ppermute | solution.py:292
  25.2 0.0 collective-permute-done.5.refs_1_
  25.2 3.6 %shard_map.71 = (f32[64,4096]{1,0:T(8,128)S(1)}, f32[8,128]{1,0:T(8,128)S(1)}) custom-call(f32[64,4096]{1,0:T(8,128)S(1)} %bitcast.17, f32[64,4096]{1,0:T(8,128)S(1)} %collective-permute-done.5.refs_1_, f32[64,4096]{1,0:T(8,128)S(1)} %get-tuple-element.43.refs_2_, f32[8,128]{1,0:T(8,128)S(1)} %get-tuple-element.44.refs_3_, ...), custom_call_target="tpu_custom_call" | custom-call | flops 262144 | bytes 262144 | tf_op jit(solution)/shard_map/pallas_call | solution.py:145
  28.8 2.3 %collective-permute-done.4.refs_2_ = f32[32,4096]{1,0:T(8,128)} collective-permute-done((f32[32,4096]{1,0:T(8,128)S(1)}, f32[32,4096]{1,0:T(8,128)}, u32[]{:S(2)}, u32[]{:S(2)}) %collective-permute-start.4) | collective-permute-done | bytes 524320 | tf_op jit(solution)/shard_map/ppermute | solution.py:292
  31.0 1.8 %collective-permute-start.9 = (f32[32,4096]{1,0:T(8,128)}, f32[32,4096]{1,0:T(8,128)}, u32[]{:S(2)}, u32[]{:S(2)}) collective-permute-start(f32[32,4096]{1,0:T(8,128)} %collective-permute-done.4.refs_2_), channel_id=1, source_target_pairs={{0,4},{1,5},{2,30},{3,31},{4,8},{5,9},{6,2},{7,3},{8,12},{9,13},{1... | collective-permute-start | bytes 1572872 | tf_op jit(solution)/shard_map/ppermute | solution.py:292
  32.8 0.0 collective-permute-start.3
  32.8 0.5 collective-permute-start.6
  33.3 4.7 %shard_map.72 = (f32[64,4096]{1,0:T(8,128)S(1)}, f32[8,128]{1,0:T(8,128)S(1)}) custom-call(f32[64,4096]{1,0:T(8,128)S(1)} %bitcast.18, f32[32,4096]{1,0:T(8,128)} %collective-permute-done.refs_1_, f32[32,4096]{1,0:T(8,128)} %collective-permute-done.4.refs_2_, f32[64,4096]{1,0:T(8,128)S(1)} %get-tuple-element.48.refs_3_, ...), custom_call_target="tpu_custom_call" | custom-call | flops 262144 | bytes 262144 | tf_op jit(solution)/shard_map/pallas_call | solution.py:145
  38.0 0.3 collective-permute-done.7.refs_1_
  38.3 0.0 collective-permute-start.8
  38.3 10.5 %collective-permute-done.9.refs_2_ = f32[32,4096]{1,0:T(8,128)} collective-permute-done((f32[32,4096]{1,0:T(8,128)}, f32[32,4096]{1,0:T(8,128)}, u32[]{:S(2)}, u32[]{:S(2)}) %collective-permute-start.9) | collective-permute-done | bytes 524320 | tf_op jit(solution)/shard_map/ppermute | solution.py:292
  48.7 0.0 collective-permute-start.10
  48.8 0.9 collective-permute-start.11
  49.7 4.6 %shard_map.73 = (f32[64,4096]{1,0:T(8,128)S(1)}, f32[8,128]{1,0:T(8,128)S(1)}) custom-call(f32[64,4096]{1,0:T(8,128)S(1)} %bitcast.19, f32[32,4096]{1,0:T(8,128)} %collective-permute-done.7.refs_1_, f32[32,4096]{1,0:T(8,128)} %collective-permute-done.9.refs_2_, f32[64,4096]{1,0:T(8,128)S(1)} %get-tuple-element.52.refs_3_, ...), custom_call_target="tpu_custom_call" | custom-call | flops 262144 | bytes 262144 | tf_op jit(solution)/shard_map/pallas_call | solution.py:145
  54.3 0.0 collective-permute-done.3.refs_1_
  54.3 0.0 collective-permute-done.6.refs_2_
  54.3 0.0 collective-permute-done.8.refs_3_
  54.4 0.0 collective-permute-done.10.refs_4_
  54.4 5.6 %shard_map.74 = (f32[2048,128]{1,0:T(8,128)}, f32[8,128]{1,0:T(8,128)S(1)}) custom-call(f32[64,4096]{1,0:T(8,128)S(1)} %bitcast.20, f32[32,4096]{1,0:T(8,128)} %collective-permute-done.3.refs_1_, f32[32,4096]{1,0:T(8,128)} %collective-permute-done.6.refs_2_, f32[32,4096]{1,0:T(8,128)} %collective-permute-done.8.refs_3_, ...), custom_call_target="tpu_custom_call" | custom-call | flops 262144 | bytes 262144 | tf_op jit(solution)/shard_map/pallas_call | solution.py:145
  60.0 0.0 collective-permute-done.11.refs_3_
  60.1 6.2 %all-to-all-start = ((f32[32,64,128]{2,1,0:T(8,128)}), f32[32,64,128]{2,1,0:T(8,128)S(1)}, u32[]{:S(2)}, u32[]{:S(2)}) async-start(f32[32,64,128]{2,1,0:T(8,128)} %bitcast.6), calls=%async_computation | async-start | bytes 2097152 | tf_op jit(solution)/shard_map/all_to_all | solution.py:304
  66.3 1.0 shard_map.75
  67.4 0.3 collective-permute-start.12
  67.7 1.7 %collective-permute-start.13 = (f32[4,64,128]{2,1,0:T(8,128)S(1)}, f32[4,64,128]{2,1,0:T(8,128)S(1)}, u32[]{:S(2)}, u32[]{:S(2)}) collective-permute-start(f32[4,64,128]{2,1,0:T(8,128)S(1)} %get-tuple-element.66), channel_id=1, source_target_pairs={{0,2},{1,3},{2,0},{3,1},{4,6},{5,7},{6,4},{7,5},{8,10},{9,11},{10,... | collective-permute-start | bytes 393224 | tf_op jit(solution)/shard_map/ppermute | solution.py:292
  69.4 0.0 collective-permute-start.14
  69.4 1.7 %collective-permute-start.15 = (f32[4,64,128]{2,1,0:T(8,128)S(1)}, f32[4,64,128]{2,1,0:T(8,128)S(1)}, u32[]{:S(2)}, u32[]{:S(2)}) collective-permute-start(f32[4,64,128]{2,1,0:T(8,128)S(1)} %get-tuple-element.68), channel_id=1, source_target_pairs={{0,4},{1,5},{2,6},{3,7},{4,0},{5,1},{6,2},{7,3},{8,12},{9,13},{10,... | collective-permute-start | bytes 393224 | tf_op jit(solution)/shard_map/ppermute | solution.py:292
  71.1 0.1 collective-permute-start.16
  71.2 0.0 collective-permute-done.12.refs_1_
  71.2 2.6 %collective-permute-start.17 = (f32[4,64,128]{2,1,0:T(8,128)S(1)}, f32[4,64,128]{2,1,0:T(8,128)S(1)}, u32[]{:S(2)}, u32[]{:S(2)}) collective-permute-start(f32[4,64,128]{2,1,0:T(8,128)S(1)} %get-tuple-element.70), channel_id=1, source_target_pairs={{0,6},{1,7},{2,4},{3,5},{4,2},{5,3},{6,0},{7,1},{8,14},{9,15},{10,... | collective-permute-start | bytes 393224 | tf_op jit(solution)/shard_map/ppermute | solution.py:292
  73.8 7.1 %collective-permute-done.13.refs_2_ = f32[4,64,128]{2,1,0:T(8,128)S(1)} collective-permute-done((f32[4,64,128]{2,1,0:T(8,128)S(1)}, f32[4,64,128]{2,1,0:T(8,128)S(1)}, u32[]{:S(2)}, u32[]{:S(2)}) %collective-permute-start.13) | collective-permute-done | bytes 131104 | tf_op jit(solution)/shard_map/ppermute | solution.py:292
  80.9 0.2 collective-permute-start.18
  81.1 2.4 %collective-permute-done.14.refs_3_ = f32[4,64,128]{2,1,0:T(8,128)S(1)} collective-permute-done((f32[4,64,128]{2,1,0:T(8,128)S(1)}, f32[4,64,128]{2,1,0:T(8,128)S(1)}, u32[]{:S(2)}, u32[]{:S(2)}) %collective-permute-start.14) | collective-permute-done | bytes 131104 | tf_op jit(solution)/shard_map/ppermute | solution.py:292
  83.4 0.0 collective-permute-done.15.refs_4_
  83.5 0.1 collective-permute-done.16.refs_5_
  83.6 5.2 %collective-permute-done.17.refs_6_ = f32[4,64,128]{2,1,0:T(8,128)S(1)} collective-permute-done((f32[4,64,128]{2,1,0:T(8,128)S(1)}, f32[4,64,128]{2,1,0:T(8,128)S(1)}, u32[]{:S(2)}, u32[]{:S(2)}) %collective-permute-start.17) | collective-permute-done | bytes 131104 | tf_op jit(solution)/shard_map/ppermute | solution.py:292
  88.8 3.5 %collective-permute-done.18.refs_7_ = f32[4,64,128]{2,1,0:T(8,128)S(1)} collective-permute-done((f32[4,64,128]{2,1,0:T(8,128)S(1)}, f32[4,64,128]{2,1,0:T(8,128)S(1)}, u32[]{:S(2)}, u32[]{:S(2)}) %collective-permute-start.18) | collective-permute-done | bytes 131104 | tf_op jit(solution)/shard_map/ppermute | solution.py:292
  92.3 0.2 all-to-all-done.terms
  92.5 2.2 %shard_map.76 = f32[32,32]{1,0:T(8,128)} custom-call(s32[3]{0:T(128)S(1)} %pad_add_fusion.place, f32[32,64,128]{2,1,0:T(8,128)S(1)} %all-to-all-done.terms, f32[4,64,128]{2,1,0:T(8,128)S(1)} %get-tuple-element.64.refs_0_, f32[4,64,128]{2,1,0:T(8,128)S(1)} %collective-permute-done.12.refs_1_, f32[4,64,128]{2,1,0:T(8,128)S(1)} %collective-permute-done.13.refs_2_, ...), custom_call_target="tpu_custom_call" | custom-call | tf_op jit(solution)/shard_map/pallas_call | solution.py:280
  94.7 3.7 %all-to-all-start.1 = ((f32[32,1,32]{2,1,0:T(1,128)}), f32[32,1,32]{2,1,0:T(1,128)S(1)}, u32[]{:S(2)}, u32[]{:S(2)}) async-start(f32[32,1,32]{2,1,0:T(1,128)} %bitcast.9), calls=%async_computation.1 | async-start | bytes 32768 | tf_op jit(solution)/shard_map/all_to_all | solution.py:304
  98.4 1.8 %copy.8 = f32[64,32,128]{2,1,0:T(8,128)S(1)} copy(f32[64,32,128]{2,0,1:T(8,128)} %bitcast.7) | data formatting | bytes 2097152 | tf_op jit(solution)/shard_map/transpose | solution.py:347
  100.3 1.2 %reshape.26 = f32[1,64,4096]{2,1,0:T(8,128)} reshape(f32[64,32,128]{2,1,0:T(8,128)S(1)} %copy.8) | data formatting | bytes 2097152 | tf_op jit(solution)/shard_map/reshape | solution.py:347
  101.4 4.1 %all-to-all-done.1 = f32[32,1,32]{2,1,0:T(1,128)S(1)} async-done(((f32[32,1,32]{2,1,0:T(1,128)}), f32[32,1,32]{2,1,0:T(1,128)S(1)}, u32[]{:S(2)}, u32[]{:S(2)}) %all-to-all-start.1) | async-done | bytes 4128 | tf_op jit(solution)/shard_map/all_to_all | solution.py:304
  105.6 0.6 reduce_sum.9
  (16 shorter events, 0.0 us)
Async XLA Ops:
  0.6 24.6 %collective-permute-start.5 = (f32[64,4096]{1,0:T(8,128)}, f32[64,4096]{1,0:T(8,128)S(1)}, u32[]{:S(2)}, u32[]{:S(2)}) collective-permute-start(f32[64,4096]{1,0:T(8,128)} %bitcast.14), channel_id=1, source_target_pairs={{0,1},{1,0},{2,3},{3,2},{4,5},{5,4},{6,7},{7,6},{8,9},{9,8},{10,11... | collective-permute-start | bytes 3145736 | tf_op jit(solution)/shard_map/ppermute | solution.py:292
  1.2 1.2 %copy-start = (f32[1,64,4096]{2,1,0:T(8,128)S(1)}, f32[1,64,4096]{2,1,0:T(8,128)}, u32[]{:S(2)}) copy-start(f32[1,64,4096]{2,1,0:T(8,128)} %param.5) | copy-start | bytes 3145732
  2.4 9.4 %copy-start.3 = (s32[64,4096]{1,0:T(8,128)S(1)}, s32[64,4096]{1,0:T(8,128)}, u32[]{:S(2)}) copy-start(s32[64,4096]{1,0:T(8,128)} %index.1) | copy-start | bytes 3145732
  3.9 0.7 copy-start.5
  4.6 19.0 %collective-permute-start = (f32[32,4096]{1,0:T(8,128)S(1)}, f32[32,4096]{1,0:T(8,128)}, u32[]{:S(2)}, u32[]{:S(2)}) collective-permute-start(f32[32,4096]{1,0:T(8,128)S(1)} %get-tuple-element.37), channel_id=1, source_target_pairs={{0,2},{1,3},{2,0},{3,1},{4,6},{5,7},{6,4},{7,5},{8,10},{9,11},{10,... | collective-permute-start | bytes 1572872 | tf_op jit(solution)/shard_map/ppermute | solution.py:292
  7.1 23.9 %collective-permute-start.4 = (f32[32,4096]{1,0:T(8,128)S(1)}, f32[32,4096]{1,0:T(8,128)}, u32[]{:S(2)}, u32[]{:S(2)}) collective-permute-start(f32[32,4096]{1,0:T(8,128)S(1)} %get-tuple-element.42), channel_id=1, source_target_pairs={{0,2},{1,3},{2,0},{3,1},{4,6},{5,7},{6,4},{7,5},{8,10},{9,11},{10,... | collective-permute-start | bytes 1572872 | tf_op jit(solution)/shard_map/ppermute | solution.py:292
  7.2 4.7 %copy-start.11 = (f32[32]{0:T(128)S(1)}, f32[32]{0:T(128)}, u32[]{:S(2)}) copy-start(f32[32]{0:T(128)} %param.6) | copy-start | bytes 388
  7.2 14.0 %collective-permute-start.1 = (f32[512,128]{1,0:T(8,128)S(1)}, f32[512,128]{1,0:T(8,128)S(1)}, u32[]{:S(2)}, u32[]{:S(2)}) collective-permute-start(f32[512,128]{1,0:T(8,128)S(1)} %get-tuple-element.38), channel_id=1, source_target_pairs={{0,8},{1,9},{2,10},{3,11},{4,12},{5,13},{6,14},{7,15},{8,0},{9,1},... | collective-permute-start | bytes 786440 | tf_op jit(solution)/shard_map/ppermute | solution.py:292
  9.2 14.4 %collective-permute-start.2 = (f32[512,128]{1,0:T(8,128)S(1)}, f32[512,128]{1,0:T(8,128)S(1)}, u32[]{:S(2)}, u32[]{:S(2)}) collective-permute-start(f32[512,128]{1,0:T(8,128)S(1)} %get-tuple-element.39), channel_id=1, source_target_pairs={{0,16},{1,17},{2,18},{3,19},{4,20},{5,21},{6,22},{7,23},{8,24},{9,... | collective-permute-start | bytes 786440 | tf_op jit(solution)/shard_map/ppermute | solution.py:292
  11.8 2.9 %copy-start.1 = (f32[1,64,4096]{2,1,0:T(8,128)S(1)}, f32[1,64,4096]{2,1,0:T(8,128)}, u32[]{:S(2)}) copy-start(f32[1,64,4096]{2,1,0:T(8,128)} %param.5) | copy-start | bytes 3145732
  11.9 2.9 %copy-start.2 = (bf16[256,256]{1,0:T(8,128)(2,1)S(1)}, bf16[256,256]{1,0:T(8,128)(2,1)}, u32[]{:S(2)}) copy-start(bf16[256,256]{1,0:T(8,128)(2,1)} %constant.57.clone.refs_3_.refs_6_.refs_7_.refs_10_) | copy-start | bytes 393220
  11.9 2.9 %copy-start.4 = (bf16[64,192]{1,0:T(8,128)(2,1)S(1)}, bf16[64,192]{1,0:T(8,128)(2,1)}, u32[]{:S(2)}) copy-start(bf16[64,192]{1,0:T(8,128)(2,1)} %constant.56.clone.refs_2_.refs_5_.refs_6_.refs_9_) | copy-start | bytes 73732
  21.1 7.6 %copy-start.7 = (f32[512,128]{1,0:T(8,128)}, f32[512,128]{1,0:T(8,128)S(1)}, u32[]{:S(2)}) copy-start(f32[512,128]{1,0:T(8,128)S(1)} %collective-permute-done.1.refs_1_) | copy-start | bytes 786436
  23.7 5.1 %copy-start.9 = (f32[512,128]{1,0:T(8,128)}, f32[512,128]{1,0:T(8,128)S(1)}, u32[]{:S(2)}) copy-start(f32[512,128]{1,0:T(8,128)S(1)} %collective-permute-done.2.refs_2_) | copy-start | bytes 786436
  23.7 14.6 %collective-permute-start.7 = (f32[32,4096]{1,0:T(8,128)}, f32[32,4096]{1,0:T(8,128)}, u32[]{:S(2)}, u32[]{:S(2)}) collective-permute-start(f32[32,4096]{1,0:T(8,128)} %collective-permute-done.refs_1_), channel_id=1, source_target_pairs={{0,4},{1,5},{2,30},{3,31},{4,8},{5,9},{6,2},{7,3},{8,12},{9,13},{1... | collective-permute-start | bytes 1572872 | tf_op jit(solution)/shard_map/ppermute | solution.py:292
  31.0 17.7 %collective-permute-start.9 = (f32[32,4096]{1,0:T(8,128)}, f32[32,4096]{1,0:T(8,128)}, u32[]{:S(2)}, u32[]{:S(2)}) collective-permute-start(f32[32,4096]{1,0:T(8,128)} %collective-permute-done.4.refs_2_), channel_id=1, source_target_pairs={{0,4},{1,5},{2,30},{3,31},{4,8},{5,9},{6,2},{7,3},{8,12},{9,13},{1... | collective-permute-start | bytes 1572872 | tf_op jit(solution)/shard_map/ppermute | solution.py:292
  32.8 21.5 %collective-permute-start.3 = (f32[32,4096]{1,0:T(8,128)}, f32[32,4096]{1,0:T(8,128)}, u32[]{:S(2)}, u32[]{:S(2)}) collective-permute-start(f32[32,4096]{1,0:T(8,128)} %collective-permute-done.refs_1_), channel_id=1, source_target_pairs={{0,1},{1,0},{2,3},{3,2},{4,5},{5,4},{6,7},{7,6},{8,9},{9,8},{10,11... | collective-permute-start | bytes 1572872 | tf_op jit(solution)/shard_map/ppermute | solution.py:292
  32.8 21.5 %collective-permute-start.6 = (f32[32,4096]{1,0:T(8,128)}, f32[32,4096]{1,0:T(8,128)}, u32[]{:S(2)}, u32[]{:S(2)}) collective-permute-start(f32[32,4096]{1,0:T(8,128)} %collective-permute-done.4.refs_2_), channel_id=1, source_target_pairs={{0,1},{1,0},{2,3},{3,2},{4,5},{5,4},{6,7},{7,6},{8,9},{9,8},{10,11... | collective-permute-start | bytes 1572872 | tf_op jit(solution)/shard_map/ppermute | solution.py:292
  38.3 16.1 %collective-permute-start.8 = (f32[32,4096]{1,0:T(8,128)}, f32[32,4096]{1,0:T(8,128)}, u32[]{:S(2)}, u32[]{:S(2)}) collective-permute-start(f32[32,4096]{1,0:T(8,128)} %collective-permute-done.7.refs_1_), channel_id=1, source_target_pairs={{0,1},{1,0},{2,3},{3,2},{4,5},{5,4},{6,7},{7,6},{8,9},{9,8},{10,11... | collective-permute-start | bytes 1572872 | tf_op jit(solution)/shard_map/ppermute | solution.py:292
  48.7 5.6 %collective-permute-start.10 = (f32[32,4096]{1,0:T(8,128)}, f32[32,4096]{1,0:T(8,128)}, u32[]{:S(2)}, u32[]{:S(2)}) collective-permute-start(f32[32,4096]{1,0:T(8,128)} %collective-permute-done.9.refs_2_), channel_id=1, source_target_pairs={{0,1},{1,0},{2,3},{3,2},{4,5},{5,4},{6,7},{7,6},{8,9},{9,8},{10,11... | collective-permute-start | bytes 1572872 | tf_op jit(solution)/shard_map/ppermute | solution.py:292
  48.8 11.3 %collective-permute-start.11 = (f32[512,128]{1,0:T(8,128)}, f32[512,128]{1,0:T(8,128)}, u32[]{:S(2)}, u32[]{:S(2)}) collective-permute-start(f32[512,128]{1,0:T(8,128)} %get-tuple-element.57), channel_id=1, source_target_pairs={{0,24},{1,25},{2,26},{3,27},{4,28},{5,29},{6,30},{7,31},{8,16},{9,... | collective-permute-start | bytes 786440 | tf_op jit(solution)/shard_map/ppermute | solution.py:292
  60.0 6.3 %copy-start.6 = (f32[512,128]{1,0:T(8,128)S(1)}, f32[512,128]{1,0:T(8,128)}, u32[]{:S(2)}) copy-start(f32[512,128]{1,0:T(8,128)} %copy-done.5) | copy-start | bytes 786436
  60.0 6.3 %copy-start.8 = (f32[512,128]{1,0:T(8,128)S(1)}, f32[512,128]{1,0:T(8,128)}, u32[]{:S(2)}) copy-start(f32[512,128]{1,0:T(8,128)} %copy-done.7) | copy-start | bytes 786436
  60.0 6.3 %copy-start.10 = (f32[512,128]{1,0:T(8,128)S(1)}, f32[512,128]{1,0:T(8,128)}, u32[]{:S(2)}) copy-start(f32[512,128]{1,0:T(8,128)} %copy-done.9) | copy-start | bytes 786436
  60.1 32.5 %all-to-all-start = ((f32[32,64,128]{2,1,0:T(8,128)}), f32[32,64,128]{2,1,0:T(8,128)S(1)}, u32[]{:S(2)}, u32[]{:S(2)}) async-start(f32[32,64,128]{2,1,0:T(8,128)} %bitcast.6), calls=%async_computation | async-start | bytes 2097152 | tf_op jit(solution)/shard_map/all_to_all | solution.py:304
  67.4 3.8 %collective-permute-start.12 = (f32[4,64,128]{2,1,0:T(8,128)S(1)}, f32[4,64,128]{2,1,0:T(8,128)S(1)}, u32[]{:S(2)}, u32[]{:S(2)}) collective-permute-start(f32[4,64,128]{2,1,0:T(8,128)S(1)} %get-tuple-element.65), channel_id=1, source_target_pairs={{0,1},{1,0},{2,3},{3,2},{4,5},{5,4},{6,7},{7,6},{8,9},{9,8},{10,11... | collective-permute-start | bytes 393224 | tf_op jit(solution)/shard_map/ppermute | solution.py:292
  67.7 13.2 %collective-permute-start.13 = (f32[4,64,128]{2,1,0:T(8,128)S(1)}, f32[4,64,128]{2,1,0:T(8,128)S(1)}, u32[]{:S(2)}, u32[]{:S(2)}) collective-permute-start(f32[4,64,128]{2,1,0:T(8,128)S(1)} %get-tuple-element.66), channel_id=1, source_target_pairs={{0,2},{1,3},{2,0},{3,1},{4,6},{5,7},{6,4},{7,5},{8,10},{9,11},{10,... | collective-permute-start | bytes 393224 | tf_op jit(solution)/shard_map/ppermute | solution.py:292
  69.4 14.1 %collective-permute-start.14 = (f32[4,64,128]{2,1,0:T(8,128)S(1)}, f32[4,64,128]{2,1,0:T(8,128)S(1)}, u32[]{:S(2)}, u32[]{:S(2)}) collective-permute-start(f32[4,64,128]{2,1,0:T(8,128)S(1)} %get-tuple-element.67), channel_id=1, source_target_pairs={{0,3},{1,2},{2,1},{3,0},{4,7},{5,6},{6,5},{7,4},{8,11},{9,10},{10,... | collective-permute-start | bytes 393224 | tf_op jit(solution)/shard_map/ppermute | solution.py:292
  69.4 14.1 %collective-permute-start.15 = (f32[4,64,128]{2,1,0:T(8,128)S(1)}, f32[4,64,128]{2,1,0:T(8,128)S(1)}, u32[]{:S(2)}, u32[]{:S(2)}) collective-permute-start(f32[4,64,128]{2,1,0:T(8,128)S(1)} %get-tuple-element.68), channel_id=1, source_target_pairs={{0,4},{1,5},{2,6},{3,7},{4,0},{5,1},{6,2},{7,3},{8,12},{9,13},{10,... | collective-permute-start | bytes 393224 | tf_op jit(solution)/shard_map/ppermute | solution.py:292
  71.1 12.5 %collective-permute-start.16 = (f32[4,64,128]{2,1,0:T(8,128)S(1)}, f32[4,64,128]{2,1,0:T(8,128)S(1)}, u32[]{:S(2)}, u32[]{:S(2)}) collective-permute-start(f32[4,64,128]{2,1,0:T(8,128)S(1)} %get-tuple-element.69), channel_id=1, source_target_pairs={{0,5},{1,4},{2,7},{3,6},{4,1},{5,0},{6,3},{7,2},{8,13},{9,12},{10,... | collective-permute-start | bytes 393224 | tf_op jit(solution)/shard_map/ppermute | solution.py:292
  71.2 17.6 %collective-permute-start.17 = (f32[4,64,128]{2,1,0:T(8,128)S(1)}, f32[4,64,128]{2,1,0:T(8,128)S(1)}, u32[]{:S(2)}, u32[]{:S(2)}) collective-permute-start(f32[4,64,128]{2,1,0:T(8,128)S(1)} %get-tuple-element.70), channel_id=1, source_target_pairs={{0,6},{1,7},{2,4},{3,5},{4,2},{5,3},{6,0},{7,1},{8,14},{9,15},{10,... | collective-permute-start | bytes 393224 | tf_op jit(solution)/shard_map/ppermute | solution.py:292
  80.9 11.4 %collective-permute-start.18 = (f32[4,64,128]{2,1,0:T(8,128)S(1)}, f32[4,64,128]{2,1,0:T(8,128)S(1)}, u32[]{:S(2)}, u32[]{:S(2)}) collective-permute-start(f32[4,64,128]{2,1,0:T(8,128)S(1)} %get-tuple-element.71), channel_id=1, source_target_pairs={{0,7},{1,6},{2,5},{3,4},{4,3},{5,2},{6,1},{7,0},{8,15},{9,14},{10,... | collective-permute-start | bytes 393224 | tf_op jit(solution)/shard_map/ppermute | solution.py:292
  94.7 10.9 %all-to-all-start.1 = ((f32[32,1,32]{2,1,0:T(1,128)}), f32[32,1,32]{2,1,0:T(1,128)S(1)}, u32[]{:S(2)}, u32[]{:S(2)}) async-start(f32[32,1,32]{2,1,0:T(1,128)} %bitcast.9), calls=%async_computation.1 | async-start | bytes 32768 | tf_op jit(solution)/shard_map/all_to_all | solution.py:304

commit v4 on v3

--- a/solution.py
+++ b/solution.py
@@ -194,7 +194,7 @@
         start += part.shape[0]
     tiles = outs[0].shape[0] // g
     for k, out in enumerate(outs):
-        first = jnp.bitwise_xor(place[0], k) * tiles
+        first = jnp.bitwise_xor(place[0], k + 1) * tiles
         for t in range(tiles):
             cols = pl.ds(pl.multiple_of((first + t) * LANES, LANES), LANES)
             out[t * g : (t + 1) * g, :] = own[:, cols]
@@ -203,7 +203,8 @@
 def cut(own, place, layers):
     g = own.shape[0]
     rows = own.size // LANES // layers
-    shapes = [(g * size // sum(CHUNKS), own.shape[1]) for size in CHUNKS] + [(rows, LANES)] * layers
+    shapes = [(g * size // sum(CHUNKS), own.shape[1]) for size in CHUNKS]
+    shapes += [(rows, LANES)] * (layers - 1)
     outs = pl.pallas_call(
         pieces_kernel,
         out_shape=[jax.ShapeDtypeStruct(shape, f32) for shape in shapes],
@@ -214,25 +215,29 @@
     return outs[: len(CHUNKS)], list(outs[len(CHUNKS) :])
 
 
-def regroup_kernel(place, done, *refs):
-    outs = refs[-LAYER:]
+def regroup_kernel(place, done, own, *refs):
+    outs, pieces = refs[-LAYER:], refs[:-LAYER]
+    g = own.shape[0]
     rows = outs[0].shape[1]
     for k, out in enumerate(outs):
         first = pl.multiple_of(jnp.bitwise_xor(place[1], k) * rows, rows)
-        for layer, piece in enumerate(refs[:-LAYER]):
-            out[layer] = piece[pl.ds(first, rows), :]
-
-
-def regroup(pieces, place, done):
+        start = place[0] * (LAYER * rows) + first
+        tile = pl.ds(pl.multiple_of(start // g * LANES, LANES), LANES)
+        out[0] = own[pl.ds(pl.multiple_of(start % g, rows), rows), tile]
+        for n, piece in enumerate(pieces):
+            out[n + 1] = piece[pl.ds(first, rows), :]
+
+
+def regroup(own, pieces, place, done):
     rows = pieces[0].shape[0] // LAYER
     return pl.pallas_call(
         regroup_kernel,
-        out_shape=[jax.ShapeDtypeStruct((len(pieces), rows, LANES), f32)] * LAYER,
+        out_shape=[jax.ShapeDtypeStruct((1 + len(pieces), rows, LANES), f32)] * LAYER,
         in_specs=[pl.BlockSpec(memory_space=pltpu.SMEM), pl.BlockSpec(memory_space=pl.ANY)]
-        + [VMEM] * len(pieces),
+        + [VMEM] * (1 + len(pieces)),
         out_specs=[VMEM] * LAYER,
         compiler_params=pltpu.CompilerParams(vmem_limit_bytes=8 * 2**20),
-    )(place, done, *pieces)
+    )(place, done, own, *pieces)
 
 
 def margin_kernel(scale, place, terms, *refs):
@@ -322,15 +327,16 @@
     parts, pieces = cut(own, place, layers)
     near = [swap(part, 2) for part in parts]
     peer = swap(own)
-    pieces[:-1] = [pieces[0]] + [swap(pieces[k], k * LAYER) for k in range(1, layers - 1)]
+    pieces[:-1] = [swap(piece, (k + 1) * LAYER) for k, piece in enumerate(pieces[:-1])]
 
     kern = lookup(kernel_values, shell_index)
     far = [None] * 2
     term, done = pair(own, [], None, kern, consts)
-    near[0], pieces[1:-1], done = after(near[0], pieces[1:-1], done)
+    half = layers // 2 - 1
+    near[0], pieces[:half], done = after(near[0], pieces[:half], done)
     far[0] = permute(near[0], far_target, count)
     term, done = pair(own, [peer], (term, done), kern, consts)
-    near[1], done = after(near[1], done)
+    near[1], pieces[half:-1], done = after(near[1], pieces[half:-1], done)
     far[1] = permute(near[1], far_target, count)
     near_cross = [swap(part) for part in near]
     use_near = (((me + 1) // 2) % 2).astype(jnp.int32).reshape(1)
@@ -341,7 +347,7 @@
     term, done = pair(own, far, (term, done), kern, consts)
     tiles, done = pair(own, near_cross, (term, done), kern, consts, far_cross, use_near, tiles=True)
     tiles, pieces[-1] = after(tiles, pieces[-1])
-    columns = list(regroup(pieces, place, done))
+    columns = list(regroup(own, pieces, place, done))
     columns = [columns[0]] + [swap(columns[k], k) for k in range(1, LAYER)]
     spread_terms = exchange(tiles.reshape(count, -1, LANES))
     term = tiles.reshape(g * g // LANES, g, LANES).transpose(1, 0, 2).reshape(orbitals.shape)

time: 107 us -> 105 us (0.981)
  transfers between devices with their start and end apart: 21 -> 21, of which waited for: 12 -> 11; matrix products, arithmetic and copies ran while one was open for 3% -> 3% of each run, Pallas kernels for 26% -> 26%
where the time goes in v4:
time: 105 us
  waiting for transfers between devices  41 us (39%)
  Pallas kernels  29.4 us (28%)
  starting transfers between devices  28.4 us (27%)
  local copies, waits for them, and re-layouts  4.27 us (4%)
    ppermute x19, waiting for transfers between devices, permute(): lax.ppermute(value, 'band', [(source, target(source) % count) for source...  36.7 us
    pallas_call x5, Pallas kernels, pair(): pl.pallas_call(functools.partial(pair_kernel, g, len(right), len(other),...  21.9 us
    ppermute x19, starting transfers between devices, permute(): lax.ppermute(value, 'band', [(source, target(source) % count) for source...  19.3 us
    all_to_all x2, starting transfers between devices, exchange(): lax.all_to_all(value, 'band', split_axis=0, concat_axis=0, tiled=True, ax...  9.15 us
    all_to_all x2, waiting for transfers between devices, exchange(): lax.all_to_all(value, 'band', split_axis=0, concat_axis=0, tiled=True, ax...  4.33 us
    pallas_call x1, Pallas kernels, lookup(): pl.pallas_call(functools.partial(lookup_kernel, -1.0 / g ** 3), out_shape...  2.82 us
    pallas_call x1, Pallas kernels, partial_margin(): pl.pallas_call(functools.partial(margin_kernel, 1.0 / points), out_shape=...  2.19 us
  transfers between devices with their start and end apart: 21, of which 11 were waited for; matrix products, arithmetic and copies ran while one was open for 3% of the time, Pallas kernels for 26%

profile of v4, /device:TPU:0, one launch (start us, length us, event | category | flops | bytes accessed | tf_op | source)
XLA Modules:
  0.0 104.6 jit_solution(10871316711305166113)
XLA Ops:
  0.6 0.5 collective-permute-start.5
  1.1 0.1 pad_add_fusion.place
  1.2 1.2 %copy-done = f32[1,64,4096]{2,1,0:T(8,128)S(1)} copy-done((f32[1,64,4096]{2,1,0:T(8,128)S(1)}, f32[1,64,4096]{2,1,0:T(8,128)}, u32[]{:S(2)}) %copy-start) | copy-done | bytes 1048600
  2.5 1.4 %shard_map.68 = (f32[32,4096]{1,0:T(8,128)S(1)}, f32[32,4096]{1,0:T(8,128)S(1)}, f32[512,128]{1,0:T(8,128)S(1)}, f32[512,128]{1,0:T(8,128)S(1)}, f32[512,128]{1,0:T(8,128)}) custom-call(s32[3]{0:T(128)S(1)} %pad_add_fusion.place, f32[64,4096]{1,0:T(8,128)S(1)} %bitcast.15), custom_call_target="tpu_custom_call" | custom-call | tf_op jit(solution)/shard_map/pallas_call | solution.py:208
  3.9 2.5 %collective-permute-start = (f32[32,4096]{1,0:T(8,128)S(1)}, f32[32,4096]{1,0:T(8,128)}, u32[]{:S(2)}, u32[]{:S(2)}) collective-permute-start(f32[32,4096]{1,0:T(8,128)S(1)} %get-tuple-element.36), channel_id=1, source_target_pairs={{0,2},{1,3},{2,0},{3,1},{4,6},{5,7},{6,4},{7,5},{8,10},{9,11},{10,... | collective-permute-start | bytes 1572872 | tf_op jit(solution)/shard_map/ppermute | solution.py:297
  6.4 0.0 collective-permute-start.3
  6.4 2.1 %collective-permute-start.1 = (f32[512,128]{1,0:T(8,128)S(1)}, f32[512,128]{1,0:T(8,128)S(1)}, u32[]{:S(2)}, u32[]{:S(2)}) collective-permute-start(f32[512,128]{1,0:T(8,128)S(1)} %get-tuple-element.37), channel_id=1, source_target_pairs={{0,8},{1,9},{2,10},{3,11},{4,12},{5,13},{6,14},{7,15},{8,0},{9,1},... | collective-permute-start | bytes 786440 | tf_op jit(solution)/shard_map/ppermute | solution.py:297
  8.5 2.6 %collective-permute-start.4 = (f32[512,128]{1,0:T(8,128)S(1)}, f32[512,128]{1,0:T(8,128)S(1)}, u32[]{:S(2)}, u32[]{:S(2)}) collective-permute-start(f32[512,128]{1,0:T(8,128)S(1)} %get-tuple-element.41), channel_id=1, source_target_pairs={{0,16},{1,17},{2,18},{3,19},{4,20},{5,21},{6,22},{7,23},{8,24},{9,... | collective-permute-start | bytes 786440 | tf_op jit(solution)/shard_map/ppermute | solution.py:297
  11.1 0.0 copy-done.9
  11.1 0.0 copy-done.3
  11.1 0.0 copy-start.1
  11.1 0.0 copy-start.2
  11.1 0.0 copy-start.4
  11.1 2.8 %shard_map.69.refs_1_.refs_4_.refs_5_.refs_8_ = f32[2048,128]{1,0:T(8,128)S(1)} custom-call(f32[1,128]{1,0:T(1,128)S(1)} %pad_bitcast_fusion.values, s32[64,4096]{1,0:T(8,128)S(1)} %copy-done.3), custom_call_target="tpu_custom_call" | custom-call | tf_op jit(solution)/shard_map/pallas_call | solution.py:179
  14.0 3.4 %shard_map.70 = (f32[64,4096]{1,0:T(8,128)S(1)}, f32[8,128]{1,0:T(8,128)S(1)}) custom-call(f32[64,4096]{1,0:T(8,128)S(1)} %bitcast.16, f32[2048,128]{1,0:T(8,128)S(1)} %shard_map.69.refs_1_.refs_4_.refs_5_.refs_8_, bf16[64,192]{1,0:T(8,128)(2,1)S(1)} %copy-done.4, bf16[256,256]{1,0:T(8,128)(2,1)S(1)} %copy-done.2), custom_call_target="tpu_custom_call" | custom-call | flops 262144 | bytes 262144 | tf_op jit(solution)/shard_map/pallas_call | solution.py:145
  17.4 3.0 %collective-permute-done.1.refs_0_ = f32[512,128]{1,0:T(8,128)S(1)} collective-permute-done((f32[512,128]{1,0:T(8,128)S(1)}, f32[512,128]{1,0:T(8,128)S(1)}, u32[]{:S(2)}, u32[]{:S(2)}) %collective-permute-start.1) | collective-permute-done | bytes 262176 | tf_op jit(solution)/shard_map/ppermute | solution.py:297
  20.4 0.0 collective-permute-done.refs_1_
  20.4 1.7 %collective-permute-start.7 = (f32[32,4096]{1,0:T(8,128)}, f32[32,4096]{1,0:T(8,128)}, u32[]{:S(2)}, u32[]{:S(2)}) collective-permute-start(f32[32,4096]{1,0:T(8,128)} %collective-permute-done.refs_1_), channel_id=1, source_target_pairs={{0,4},{1,5},{2,30},{3,31},{4,8},{5,9},{6,2},{7,3},{8,12},{9,13},{1... | collective-permute-start | bytes 1572872 | tf_op jit(solution)/shard_map/ppermute | solution.py:297
  22.1 0.0 collective-permute-done.5.refs_1_
  22.1 3.5 %shard_map.71 = (f32[64,4096]{1,0:T(8,128)S(1)}, f32[8,128]{1,0:T(8,128)S(1)}) custom-call(f32[64,4096]{1,0:T(8,128)S(1)} %bitcast.17, f32[64,4096]{1,0:T(8,128)S(1)} %collective-permute-done.5.refs_1_, f32[64,4096]{1,0:T(8,128)S(1)} %get-tuple-element.42.refs_2_, f32[8,128]{1,0:T(8,128)S(1)} %get-tuple-element.43.refs_3_, ...), custom_call_target="tpu_custom_call" | custom-call | flops 262144 | bytes 262144 | tf_op jit(solution)/shard_map/pallas_call | solution.py:145
  25.7 0.0 collective-permute-done.4.refs_1_
  25.7 0.0 copy-start.7
  25.7 4.6 %collective-permute-done.3.refs_2_ = f32[32,4096]{1,0:T(8,128)} collective-permute-done((f32[32,4096]{1,0:T(8,128)S(1)}, f32[32,4096]{1,0:T(8,128)}, u32[]{:S(2)}, u32[]{:S(2)}) %collective-permute-start.3) | collective-permute-done | bytes 524320 | tf_op jit(solution)/shard_map/ppermute | solution.py:297
  30.3 1.8 %collective-permute-start.9 = (f32[32,4096]{1,0:T(8,128)}, f32[32,4096]{1,0:T(8,128)}, u32[]{:S(2)}, u32[]{:S(2)}) collective-permute-start(f32[32,4096]{1,0:T(8,128)} %collective-permute-done.3.refs_2_), channel_id=1, source_target_pairs={{0,4},{1,5},{2,30},{3,31},{4,8},{5,9},{6,2},{7,3},{8,12},{9,13},{1... | collective-permute-start | bytes 1572872 | tf_op jit(solution)/shard_map/ppermute | solution.py:297
  32.1 0.0 collective-permute-start.2
  32.1 0.5 collective-permute-start.6
  32.6 4.7 %shard_map.72 = (f32[64,4096]{1,0:T(8,128)S(1)}, f32[8,128]{1,0:T(8,128)S(1)}) custom-call(f32[64,4096]{1,0:T(8,128)S(1)} %bitcast.18, f32[32,4096]{1,0:T(8,128)} %collective-permute-done.refs_1_, f32[32,4096]{1,0:T(8,128)} %collective-permute-done.3.refs_2_, f32[64,4096]{1,0:T(8,128)S(1)} %get-tuple-element.47.refs_3_, ...), custom_call_target="tpu_custom_call" | custom-call | flops 262144 | bytes 262144 | tf_op jit(solution)/shard_map/pallas_call | solution.py:145
  37.3 0.1 collective-permute-done.7.refs_1_
  37.4 0.0 collective-permute-start.8
  37.4 10.5 %collective-permute-done.9.refs_2_ = f32[32,4096]{1,0:T(8,128)} collective-permute-done((f32[32,4096]{1,0:T(8,128)}, f32[32,4096]{1,0:T(8,128)}, u32[]{:S(2)}, u32[]{:S(2)}) %collective-permute-start.9) | collective-permute-done | bytes 524320 | tf_op jit(solution)/shard_map/ppermute | solution.py:297
  47.9 0.0 collective-permute-start.10
  48.0 1.0 collective-permute-start.11
  48.9 4.6 %shard_map.73 = (f32[64,4096]{1,0:T(8,128)S(1)}, f32[8,128]{1,0:T(8,128)S(1)}) custom-call(f32[64,4096]{1,0:T(8,128)S(1)} %bitcast.19, f32[32,4096]{1,0:T(8,128)} %collective-permute-done.7.refs_1_, f32[32,4096]{1,0:T(8,128)} %collective-permute-done.9.refs_2_, f32[64,4096]{1,0:T(8,128)S(1)} %get-tuple-element.51.refs_3_, ...), custom_call_target="tpu_custom_call" | custom-call | flops 262144 | bytes 262144 | tf_op jit(solution)/shard_map/pallas_call | solution.py:145
  53.6 0.0 collective-permute-done.2.refs_1_
  53.6 0.0 collective-permute-done.6.refs_2_
  53.6 0.0 collective-permute-done.8.refs_3_
  53.6 0.0 collective-permute-done.10.refs_4_
  53.6 5.6 %shard_map.74 = (f32[2048,128]{1,0:T(8,128)}, f32[8,128]{1,0:T(8,128)S(1)}) custom-call(f32[64,4096]{1,0:T(8,128)S(1)} %bitcast.20, f32[32,4096]{1,0:T(8,128)} %collective-permute-done.2.refs_1_, f32[32,4096]{1,0:T(8,128)} %collective-permute-done.6.refs_2_, f32[32,4096]{1,0:T(8,128)} %collective-permute-done.8.refs_3_, ...), custom_call_target="tpu_custom_call" | custom-call | flops 262144 | bytes 262144 | tf_op jit(solution)/shard_map/pallas_call | solution.py:145
  59.3 0.0 collective-permute-done.11.refs_2_
  59.3 5.4 %all-to-all-start = ((f32[32,64,128]{2,1,0:T(8,128)}), f32[32,64,128]{2,1,0:T(8,128)S(1)}, u32[]{:S(2)}, u32[]{:S(2)}) async-start(f32[32,64,128]{2,1,0:T(8,128)} %bitcast.6), calls=%async_computation | async-start | bytes 2097152 | tf_op jit(solution)/shard_map/all_to_all | solution.py:309
  64.8 0.0 copy-done.6
  64.8 0.0 copy-done.8
  64.8 1.1 %shard_map.75 = (f32[4,64,128]{2,1,0:T(8,128)S(1)}, f32[4,64,128]{2,1,0:T(8,128)S(1)}, f32[4,64,128]{2,1,0:T(8,128)S(1)}, f32[4,64,128]{2,1,0:T(8,128)S(1)}, f32...) custom-call(s32[3]{0:T(128)S(1)} %pad_add_fusion.place, ...), custom_call_target="tpu_custom_call" | custom-call | tf_op jit(solution)/shard_map/pallas_call | solution.py:233
  65.9 0.3 collective-permute-start.12
  66.2 1.7 %collective-permute-start.13 = (f32[4,64,128]{2,1,0:T(8,128)S(1)}, f32[4,64,128]{2,1,0:T(8,128)S(1)}, u32[]{:S(2)}, u32[]{:S(2)}) collective-permute-start(f32[4,64,128]{2,1,0:T(8,128)S(1)} %get-tuple-element.64), channel_id=1, source_target_pairs={{0,2},{1,3},{2,0},{3,1},{4,6},{5,7},{6,4},{7,5},{8,10},{9,11},{10,... | collective-permute-start | bytes 393224 | tf_op jit(solution)/shard_map/ppermute | solution.py:297
  67.9 0.0 collective-permute-start.14
  67.9 1.7 %collective-permute-start.15 = (f32[4,64,128]{2,1,0:T(8,128)S(1)}, f32[4,64,128]{2,1,0:T(8,128)S(1)}, u32[]{:S(2)}, u32[]{:S(2)}) collective-permute-start(f32[4,64,128]{2,1,0:T(8,128)S(1)} %get-tuple-element.66), channel_id=1, source_target_pairs={{0,4},{1,5},{2,6},{3,7},{4,0},{5,1},{6,2},{7,3},{8,12},{9,13},{10,... | collective-permute-start | bytes 393224 | tf_op jit(solution)/shard_map/ppermute | solution.py:297
  69.6 0.1 collective-permute-start.16
  69.7 0.0 collective-permute-done.12.refs_1_
  69.7 2.6 %collective-permute-start.17 = (f32[4,64,128]{2,1,0:T(8,128)S(1)}, f32[4,64,128]{2,1,0:T(8,128)S(1)}, u32[]{:S(2)}, u32[]{:S(2)}) collective-permute-start(f32[4,64,128]{2,1,0:T(8,128)S(1)} %get-tuple-element.68), channel_id=1, source_target_pairs={{0,6},{1,7},{2,4},{3,5},{4,2},{5,3},{6,0},{7,1},{8,14},{9,15},{10,... | collective-permute-start | bytes 393224 | tf_op jit(solution)/shard_map/ppermute | solution.py:297
  72.3 7.1 %collective-permute-done.13.refs_2_ = f32[4,64,128]{2,1,0:T(8,128)S(1)} collective-permute-done((f32[4,64,128]{2,1,0:T(8,128)S(1)}, f32[4,64,128]{2,1,0:T(8,128)S(1)}, u32[]{:S(2)}, u32[]{:S(2)}) %collective-permute-start.13) | collective-permute-done | bytes 131104 | tf_op jit(solution)/shard_map/ppermute | solution.py:297
  79.4 0.2 collective-permute-start.18
  79.6 2.4 %collective-permute-done.14.refs_3_ = f32[4,64,128]{2,1,0:T(8,128)S(1)} collective-permute-done((f32[4,64,128]{2,1,0:T(8,128)S(1)}, f32[4,64,128]{2,1,0:T(8,128)S(1)}, u32[]{:S(2)}, u32[]{:S(2)}) %collective-permute-start.14) | collective-permute-done | bytes 131104 | tf_op jit(solution)/shard_map/ppermute | solution.py:297
  81.9 0.0 collective-permute-done.15.refs_4_
  81.9 0.1 collective-permute-done.16.refs_5_
  82.1 5.2 %collective-permute-done.17.refs_6_ = f32[4,64,128]{2,1,0:T(8,128)S(1)} collective-permute-done((f32[4,64,128]{2,1,0:T(8,128)S(1)}, f32[4,64,128]{2,1,0:T(8,128)S(1)}, u32[]{:S(2)}, u32[]{:S(2)}) %collective-permute-start.17) | collective-permute-done | bytes 131104 | tf_op jit(solution)/shard_map/ppermute | solution.py:297
  87.3 3.5 %collective-permute-done.18.refs_7_ = f32[4,64,128]{2,1,0:T(8,128)S(1)} collective-permute-done((f32[4,64,128]{2,1,0:T(8,128)S(1)}, f32[4,64,128]{2,1,0:T(8,128)S(1)}, u32[]{:S(2)}, u32[]{:S(2)}) %collective-permute-start.18) | collective-permute-done | bytes 131104 | tf_op jit(solution)/shard_map/ppermute | solution.py:297
  90.8 0.2 all-to-all-done.terms
  91.0 2.2 %shard_map.76 = f32[32,32]{1,0:T(8,128)} custom-call(s32[3]{0:T(128)S(1)} %pad_add_fusion.place, f32[32,64,128]{2,1,0:T(8,128)S(1)} %all-to-all-done.terms, f32[4,64,128]{2,1,0:T(8,128)S(1)} %get-tuple-element.62.refs_0_, f32[4,64,128]{2,1,0:T(8,128)S(1)} %collective-permute-done.12.refs_1_, f32[4,64,128]{2,1,0:T(8,128)S(1)} %collective-permute-done.13.refs_2_, ...), custom_call_target="tpu_custom_call" | custom-call | tf_op jit(solution)/shard_map/pallas_call | solution.py:285
  93.2 3.7 %all-to-all-start.1 = ((f32[32,1,32]{2,1,0:T(1,128)}), f32[32,1,32]{2,1,0:T(1,128)S(1)}, u32[]{:S(2)}, u32[]{:S(2)}) async-start(f32[32,1,32]{2,1,0:T(1,128)} %bitcast.9), calls=%async_computation.1 | async-start | bytes 32768 | tf_op jit(solution)/shard_map/all_to_all | solution.py:309
  96.9 1.8 %copy.8 = f32[64,32,128]{2,1,0:T(8,128)S(1)} copy(f32[64,32,128]{2,0,1:T(8,128)} %bitcast.7) | data formatting | bytes 2097152 | tf_op jit(solution)/shard_map/transpose | solution.py:353
  98.8 1.2 %reshape.26 = f32[1,64,4096]{2,1,0:T(8,128)} reshape(f32[64,32,128]{2,1,0:T(8,128)S(1)} %copy.8) | data formatting | bytes 2097152 | tf_op jit(solution)/shard_map/reshape | solution.py:353
  99.9 4.1 %all-to-all-done.1 = f32[32,1,32]{2,1,0:T(1,128)S(1)} async-done(((f32[32,1,32]{2,1,0:T(1,128)}), f32[32,1,32]{2,1,0:T(1,128)S(1)}, u32[]{:S(2)}, u32[]{:S(2)}) %all-to-all-start.1) | async-done | bytes 4128 | tf_op jit(solution)/shard_map/all_to_all | solution.py:309
  104.1 0.6 reduce_sum.9
  (12 shorter events, 0.0 us)
Async XLA Ops:
  0.6 21.5 %collective-permute-start.5 = (f32[64,4096]{1,0:T(8,128)}, f32[64,4096]{1,0:T(8,128)S(1)}, u32[]{:S(2)}, u32[]{:S(2)}) collective-permute-start(f32[64,4096]{1,0:T(8,128)} %bitcast.14), channel_id=1, source_target_pairs={{0,1},{1,0},{2,3},{3,2},{4,5},{5,4},{6,7},{7,6},{8,9},{9,8},{10,11... | collective-permute-start | bytes 3145736 | tf_op jit(solution)/shard_map/ppermute | solution.py:297
  1.2 1.2 %copy-start = (f32[1,64,4096]{2,1,0:T(8,128)S(1)}, f32[1,64,4096]{2,1,0:T(8,128)}, u32[]{:S(2)}) copy-start(f32[1,64,4096]{2,1,0:T(8,128)} %param.5) | copy-start | bytes 3145732
  2.4 8.7 %copy-start.3 = (s32[64,4096]{1,0:T(8,128)S(1)}, s32[64,4096]{1,0:T(8,128)}, u32[]{:S(2)}) copy-start(s32[64,4096]{1,0:T(8,128)} %index.1) | copy-start | bytes 3145732
  3.9 16.5 %collective-permute-start = (f32[32,4096]{1,0:T(8,128)S(1)}, f32[32,4096]{1,0:T(8,128)}, u32[]{:S(2)}, u32[]{:S(2)}) collective-permute-start(f32[32,4096]{1,0:T(8,128)S(1)} %get-tuple-element.36), channel_id=1, source_target_pairs={{0,2},{1,3},{2,0},{3,1},{4,6},{5,7},{6,4},{7,5},{8,10},{9,11},{10,... | collective-permute-start | bytes 1572872 | tf_op jit(solution)/shard_map/ppermute | solution.py:297
  6.4 23.9 %collective-permute-start.3 = (f32[32,4096]{1,0:T(8,128)S(1)}, f32[32,4096]{1,0:T(8,128)}, u32[]{:S(2)}, u32[]{:S(2)}) collective-permute-start(f32[32,4096]{1,0:T(8,128)S(1)} %get-tuple-element.40), channel_id=1, source_target_pairs={{0,2},{1,3},{2,0},{3,1},{4,6},{5,7},{6,4},{7,5},{8,10},{9,11},{10,... | collective-permute-start | bytes 1572872 | tf_op jit(solution)/shard_map/ppermute | solution.py:297
  6.4 4.7 %copy-start.9 = (f32[32]{0:T(128)S(1)}, f32[32]{0:T(128)}, u32[]{:S(2)}) copy-start(f32[32]{0:T(128)} %param.6) | copy-start | bytes 388
  6.4 14.0 %collective-permute-start.1 = (f32[512,128]{1,0:T(8,128)S(1)}, f32[512,128]{1,0:T(8,128)S(1)}, u32[]{:S(2)}, u32[]{:S(2)}) collective-permute-start(f32[512,128]{1,0:T(8,128)S(1)} %get-tuple-element.37), channel_id=1, source_target_pairs={{0,8},{1,9},{2,10},{3,11},{4,12},{5,13},{6,14},{7,15},{8,0},{9,1},... | collective-permute-start | bytes 786440 | tf_op jit(solution)/shard_map/ppermute | solution.py:297
  8.5 17.1 %collective-permute-start.4 = (f32[512,128]{1,0:T(8,128)S(1)}, f32[512,128]{1,0:T(8,128)S(1)}, u32[]{:S(2)}, u32[]{:S(2)}) collective-permute-start(f32[512,128]{1,0:T(8,128)S(1)} %get-tuple-element.41), channel_id=1, source_target_pairs={{0,16},{1,17},{2,18},{3,19},{4,20},{5,21},{6,22},{7,23},{8,24},{9,... | collective-permute-start | bytes 786440 | tf_op jit(solution)/shard_map/ppermute | solution.py:297
  11.1 2.9 %copy-start.1 = (f32[1,64,4096]{2,1,0:T(8,128)S(1)}, f32[1,64,4096]{2,1,0:T(8,128)}, u32[]{:S(2)}) copy-start(f32[1,64,4096]{2,1,0:T(8,128)} %param.5) | copy-start | bytes 3145732
  11.1 2.9 %copy-start.2 = (bf16[256,256]{1,0:T(8,128)(2,1)S(1)}, bf16[256,256]{1,0:T(8,128)(2,1)}, u32[]{:S(2)}) copy-start(bf16[256,256]{1,0:T(8,128)(2,1)} %constant.57.clone.refs_3_.refs_6_.refs_7_.refs_10_) | copy-start | bytes 393220
  11.1 2.9 %copy-start.4 = (bf16[64,192]{1,0:T(8,128)(2,1)S(1)}, bf16[64,192]{1,0:T(8,128)(2,1)}, u32[]{:S(2)}) copy-start(bf16[64,192]{1,0:T(8,128)(2,1)} %constant.56.clone.refs_2_.refs_5_.refs_6_.refs_9_) | copy-start | bytes 73732
  20.4 5.3 %copy-start.5 = (f32[512,128]{1,0:T(8,128)}, f32[512,128]{1,0:T(8,128)S(1)}, u32[]{:S(2)}) copy-start(f32[512,128]{1,0:T(8,128)S(1)} %collective-permute-done.1.refs_0_) | copy-start | bytes 786436
  20.4 17.0 %collective-permute-start.7 = (f32[32,4096]{1,0:T(8,128)}, f32[32,4096]{1,0:T(8,128)}, u32[]{:S(2)}, u32[]{:S(2)}) collective-permute-start(f32[32,4096]{1,0:T(8,128)} %collective-permute-done.refs_1_), channel_id=1, source_target_pairs={{0,4},{1,5},{2,30},{3,31},{4,8},{5,9},{6,2},{7,3},{8,12},{9,13},{1... | collective-permute-start | bytes 1572872 | tf_op jit(solution)/shard_map/ppermute | solution.py:297
  25.7 11.6 %copy-start.7 = (f32[512,128]{1,0:T(8,128)}, f32[512,128]{1,0:T(8,128)S(1)}, u32[]{:S(2)}) copy-start(f32[512,128]{1,0:T(8,128)S(1)} %collective-permute-done.4.refs_1_) | copy-start | bytes 786436
  30.3 17.7 %collective-permute-start.9 = (f32[32,4096]{1,0:T(8,128)}, f32[32,4096]{1,0:T(8,128)}, u32[]{:S(2)}, u32[]{:S(2)}) collective-permute-start(f32[32,4096]{1,0:T(8,128)} %collective-permute-done.3.refs_2_), channel_id=1, source_target_pairs={{0,4},{1,5},{2,30},{3,31},{4,8},{5,9},{6,2},{7,3},{8,12},{9,13},{1... | collective-permute-start | bytes 1572872 | tf_op jit(solution)/shard_map/ppermute | solution.py:297
  32.1 21.5 %collective-permute-start.2 = (f32[32,4096]{1,0:T(8,128)}, f32[32,4096]{1,0:T(8,128)}, u32[]{:S(2)}, u32[]{:S(2)}) collective-permute-start(f32[32,4096]{1,0:T(8,128)} %collective-permute-done.refs_1_), channel_id=1, source_target_pairs={{0,1},{1,0},{2,3},{3,2},{4,5},{5,4},{6,7},{7,6},{8,9},{9,8},{10,11... | collective-permute-start | bytes 1572872 | tf_op jit(solution)/shard_map/ppermute | solution.py:297
  32.1 21.5 %collective-permute-start.6 = (f32[32,4096]{1,0:T(8,128)}, f32[32,4096]{1,0:T(8,128)}, u32[]{:S(2)}, u32[]{:S(2)}) collective-permute-start(f32[32,4096]{1,0:T(8,128)} %collective-permute-done.3.refs_2_), channel_id=1, source_target_pairs={{0,1},{1,0},{2,3},{3,2},{4,5},{5,4},{6,7},{7,6},{8,9},{9,8},{10,11... | collective-permute-start | bytes 1572872 | tf_op jit(solution)/shard_map/ppermute | solution.py:297
  37.4 16.2 %collective-permute-start.8 = (f32[32,4096]{1,0:T(8,128)}, f32[32,4096]{1,0:T(8,128)}, u32[]{:S(2)}, u32[]{:S(2)}) collective-permute-start(f32[32,4096]{1,0:T(8,128)} %collective-permute-done.7.refs_1_), channel_id=1, source_target_pairs={{0,1},{1,0},{2,3},{3,2},{4,5},{5,4},{6,7},{7,6},{8,9},{9,8},{10,11... | collective-permute-start | bytes 1572872 | tf_op jit(solution)/shard_map/ppermute | solution.py:297
  47.9 5.7 %collective-permute-start.10 = (f32[32,4096]{1,0:T(8,128)}, f32[32,4096]{1,0:T(8,128)}, u32[]{:S(2)}, u32[]{:S(2)}) collective-permute-start(f32[32,4096]{1,0:T(8,128)} %collective-permute-done.9.refs_2_), channel_id=1, source_target_pairs={{0,1},{1,0},{2,3},{3,2},{4,5},{5,4},{6,7},{7,6},{8,9},{9,8},{10,11... | collective-permute-start | bytes 1572872 | tf_op jit(solution)/shard_map/ppermute | solution.py:297
  48.0 11.3 %collective-permute-start.11 = (f32[512,128]{1,0:T(8,128)}, f32[512,128]{1,0:T(8,128)}, u32[]{:S(2)}, u32[]{:S(2)}) collective-permute-start(f32[512,128]{1,0:T(8,128)} %get-tuple-element.56), channel_id=1, source_target_pairs={{0,24},{1,25},{2,26},{3,27},{4,28},{5,29},{6,30},{7,31},{8,16},{9,... | collective-permute-start | bytes 786440 | tf_op jit(solution)/shard_map/ppermute | solution.py:297
  59.3 5.5 %copy-start.6 = (f32[512,128]{1,0:T(8,128)S(1)}, f32[512,128]{1,0:T(8,128)}, u32[]{:S(2)}) copy-start(f32[512,128]{1,0:T(8,128)} %copy-done.5) | copy-start | bytes 786436
  59.3 5.5 %copy-start.8 = (f32[512,128]{1,0:T(8,128)S(1)}, f32[512,128]{1,0:T(8,128)}, u32[]{:S(2)}) copy-start(f32[512,128]{1,0:T(8,128)} %copy-done.7) | copy-start | bytes 786436
  59.3 31.7 %all-to-all-start = ((f32[32,64,128]{2,1,0:T(8,128)}), f32[32,64,128]{2,1,0:T(8,128)S(1)}, u32[]{:S(2)}, u32[]{:S(2)}) async-start(f32[32,64,128]{2,1,0:T(8,128)} %bitcast.6), calls=%async_computation | async-start | bytes 2097152 | tf_op jit(solution)/shard_map/all_to_all | solution.py:309
  65.9 3.8 %collective-permute-start.12 = (f32[4,64,128]{2,1,0:T(8,128)S(1)}, f32[4,64,128]{2,1,0:T(8,128)S(1)}, u32[]{:S(2)}, u32[]{:S(2)}) collective-permute-start(f32[4,64,128]{2,1,0:T(8,128)S(1)} %get-tuple-element.63), channel_id=1, source_target_pairs={{0,1},{1,0},{2,3},{3,2},{4,5},{5,4},{6,7},{7,6},{8,9},{9,8},{10,11... | collective-permute-start | bytes 393224 | tf_op jit(solution)/shard_map/ppermute | solution.py:297
  66.2 13.2 %collective-permute-start.13 = (f32[4,64,128]{2,1,0:T(8,128)S(1)}, f32[4,64,128]{2,1,0:T(8,128)S(1)}, u32[]{:S(2)}, u32[]{:S(2)}) collective-permute-start(f32[4,64,128]{2,1,0:T(8,128)S(1)} %get-tuple-element.64), channel_id=1, source_target_pairs={{0,2},{1,3},{2,0},{3,1},{4,6},{5,7},{6,4},{7,5},{8,10},{9,11},{10,... | collective-permute-start | bytes 393224 | tf_op jit(solution)/shard_map/ppermute | solution.py:297
  67.9 14.1 %collective-permute-start.14 = (f32[4,64,128]{2,1,0:T(8,128)S(1)}, f32[4,64,128]{2,1,0:T(8,128)S(1)}, u32[]{:S(2)}, u32[]{:S(2)}) collective-permute-start(f32[4,64,128]{2,1,0:T(8,128)S(1)} %get-tuple-element.65), channel_id=1, source_target_pairs={{0,3},{1,2},{2,1},{3,0},{4,7},{5,6},{6,5},{7,4},{8,11},{9,10},{10,... | collective-permute-start | bytes 393224 | tf_op jit(solution)/shard_map/ppermute | solution.py:297
  67.9 14.1 %collective-permute-start.15 = (f32[4,64,128]{2,1,0:T(8,128)S(1)}, f32[4,64,128]{2,1,0:T(8,128)S(1)}, u32[]{:S(2)}, u32[]{:S(2)}) collective-permute-start(f32[4,64,128]{2,1,0:T(8,128)S(1)} %get-tuple-element.66), channel_id=1, source_target_pairs={{0,4},{1,5},{2,6},{3,7},{4,0},{5,1},{6,2},{7,3},{8,12},{9,13},{10,... | collective-permute-start | bytes 393224 | tf_op jit(solution)/shard_map/ppermute | solution.py:297
  69.6 12.5 %collective-permute-start.16 = (f32[4,64,128]{2,1,0:T(8,128)S(1)}, f32[4,64,128]{2,1,0:T(8,128)S(1)}, u32[]{:S(2)}, u32[]{:S(2)}) collective-permute-start(f32[4,64,128]{2,1,0:T(8,128)S(1)} %get-tuple-element.67), channel_id=1, source_target_pairs={{0,5},{1,4},{2,7},{3,6},{4,1},{5,0},{6,3},{7,2},{8,13},{9,12},{10,... | collective-permute-start | bytes 393224 | tf_op jit(solution)/shard_map/ppermute | solution.py:297
  69.7 17.6 %collective-permute-start.17 = (f32[4,64,128]{2,1,0:T(8,128)S(1)}, f32[4,64,128]{2,1,0:T(8,128)S(1)}, u32[]{:S(2)}, u32[]{:S(2)}) collective-permute-start(f32[4,64,128]{2,1,0:T(8,128)S(1)} %get-tuple-element.68), channel_id=1, source_target_pairs={{0,6},{1,7},{2,4},{3,5},{4,2},{5,3},{6,0},{7,1},{8,14},{9,15},{10,... | collective-permute-start | bytes 393224 | tf_op jit(solution)/shard_map/ppermute | solution.py:297
  79.4 11.4 %collective-permute-start.18 = (f32[4,64,128]{2,1,0:T(8,128)S(1)}, f32[4,64,128]{2,1,0:T(8,128)S(1)}, u32[]{:S(2)}, u32[]{:S(2)}) collective-permute-start(f32[4,64,128]{2,1,0:T(8,128)S(1)} %get-tuple-element.69), channel_id=1, source_target_pairs={{0,7},{1,6},{2,5},{3,4},{4,3},{5,2},{6,1},{7,0},{8,15},{9,14},{10,... | collective-permute-start | bytes 393224 | tf_op jit(solution)/shard_map/ppermute | solution.py:297
  93.2 10.8 %all-to-all-start.1 = ((f32[32,1,32]{2,1,0:T(1,128)}), f32[32,1,32]{2,1,0:T(1,128)S(1)}, u32[]{:S(2)}, u32[]{:S(2)}) async-start(f32[32,1,32]{2,1,0:T(1,128)} %bitcast.9), calls=%async_computation.1 | async-start | bytes 32768 | tf_op jit(solution)/shard_map/all_to_all | solution.py:309

commit v5 on v4

--- a/solution.py
+++ b/solution.py
@@ -186,18 +186,27 @@
 
 
 def pieces_kernel(place, own, *refs):
-    parts, outs = refs[: len(CHUNKS)], refs[len(CHUNKS) :]
+    parts, outs, sems = refs[: len(CHUNKS)], refs[len(CHUNKS) : -1], refs[-1]
     g = own.shape[0]
+    moves = []
     start = 0
     for part in parts:
-        part[...] = own[start : start + part.shape[0], :]
+        moves.append((own.at[pl.ds(start, part.shape[0]), :], part))
         start += part.shape[0]
     tiles = outs[0].shape[0] // g
     for k, out in enumerate(outs):
         first = jnp.bitwise_xor(place[0], k + 1) * tiles
         for t in range(tiles):
             cols = pl.ds(pl.multiple_of((first + t) * LANES, LANES), LANES)
-            out[t * g : (t + 1) * g, :] = own[:, cols]
+            moves.append((own.at[:, cols], out.at[pl.ds(t * g, g), :]))
+    copies = [
+        pltpu.make_async_copy(source, target, sems.at[n])
+        for n, (source, target) in enumerate(moves)
+    ]
+    for copy in copies:
+        copy.start()
+    for copy in copies:
+        copy.wait()
 
 
 def cut(own, place, layers):
@@ -208,8 +217,14 @@
     outs = pl.pallas_call(
         pieces_kernel,
         out_shape=[jax.ShapeDtypeStruct(shape, f32) for shape in shapes],
-        in_specs=[pl.BlockSpec(memory_space=pltpu.SMEM), VMEM],
+        in_specs=[
+            pl.BlockSpec(memory_space=pltpu.SMEM),
+            pl.BlockSpec(memory_space=pltpu.HBM),
+        ],
         out_specs=[VMEM] * len(shapes),
+        scratch_shapes=[
+            pltpu.SemaphoreType.DMA((len(CHUNKS) + (layers - 1) * (rows // g),))
+        ],
         compiler_params=pltpu.CompilerParams(vmem_limit_bytes=8 * 2**20),
     )(place, own)
     return outs[: len(CHUNKS)], list(outs[len(CHUNKS) :])

time: 105 us -> 105 us (level)
  no operation moved by 1% of the time
where the time goes in v5:
time: 105 us
  waiting for transfers between devices  41 us (39%)
  Pallas kernels  29.8 us (28%)
  starting transfers between devices  28.5 us (27%)
  local copies, waits for them, and re-layouts  4.27 us (4%)
    ppermute x19, waiting for transfers between devices, permute(): lax.ppermute(value, 'band', [(source, target(source) % count) for source...  36.7 us
    pallas_call x5, Pallas kernels, pair(): pl.pallas_call(functools.partial(pair_kernel, g, len(right), len(other),...  21.9 us
    ppermute x19, starting transfers between devices, permute(): lax.ppermute(value, 'band', [(source, target(source) % count) for source...  19.4 us
    all_to_all x2, starting transfers between devices, exchange(): lax.all_to_all(value, 'band', split_axis=0, concat_axis=0, tiled=True, ax...  9.14 us
    all_to_all x2, waiting for transfers between devices, exchange(): lax.all_to_all(value, 'band', split_axis=0, concat_axis=0, tiled=True, ax...  4.33 us
    pallas_call x1, Pallas kernels, lookup(): pl.pallas_call(functools.partial(lookup_kernel, -1.0 / g ** 3), out_shape...  2.82 us
    pallas_call x1, Pallas kernels, partial_margin(): pl.pallas_call(functools.partial(margin_kernel, 1.0 / points), out_shape=...  2.19 us
  transfers between devices with their start and end apart: 21, of which 11 were waited for; matrix products, arithmetic and copies ran while one was open for 3% of the time, Pallas kernels for 26%

profile of v5, /device:TPU:0, one launch (start us, length us, event | category | flops | bytes accessed | tf_op | source)
XLA Modules:
  0.0 105.1 jit_solution(12068000537721285310)
XLA Ops:
  0.6 0.5 collective-permute-start.5
  1.1 0.1 pad_add_fusion.place
  1.2 1.2 %copy-done = f32[1,64,4096]{2,1,0:T(8,128)S(1)} copy-done((f32[1,64,4096]{2,1,0:T(8,128)S(1)}, f32[1,64,4096]{2,1,0:T(8,128)}, u32[]{:S(2)}) %copy-start) | copy-done | bytes 1048600
  2.5 1.8 %shard_map.68 = (f32[32,4096]{1,0:T(8,128)S(1)}, f32[32,4096]{1,0:T(8,128)S(1)}, f32[512,128]{1,0:T(8,128)S(1)}, f32[512,128]{1,0:T(8,128)S(1)}, f32[512,128]{1,0:T(8,128)}) custom-call(s32[3]{0:T(128)S(1)} %pad_add_fusion.place, f32[64,4096]{1,0:T(8,128)S(1)} %bitcast.15), custom_call_target="tpu_custom_call" | custom-call | tf_op jit(solution)/shard_map/pallas_call | solution.py:217
  4.2 2.6 %collective-permute-start = (f32[32,4096]{1,0:T(8,128)S(1)}, f32[32,4096]{1,0:T(8,128)}, u32[]{:S(2)}, u32[]{:S(2)}) collective-permute-start(f32[32,4096]{1,0:T(8,128)S(1)} %get-tuple-element.36), channel_id=1, source_target_pairs={{0,2},{1,3},{2,0},{3,1},{4,6},{5,7},{6,4},{7,5},{8,10},{9,11},{10,... | collective-permute-start | bytes 1572872 | tf_op jit(solution)/shard_map/ppermute | solution.py:312
  6.8 0.1 collective-permute-start.3
  7.0 2.0 %collective-permute-start.1 = (f32[512,128]{1,0:T(8,128)S(1)}, f32[512,128]{1,0:T(8,128)S(1)}, u32[]{:S(2)}, u32[]{:S(2)}) collective-permute-start(f32[512,128]{1,0:T(8,128)S(1)} %get-tuple-element.37), channel_id=1, source_target_pairs={{0,8},{1,9},{2,10},{3,11},{4,12},{5,13},{6,14},{7,15},{8,0},{9,1},... | collective-permute-start | bytes 786440 | tf_op jit(solution)/shard_map/ppermute | solution.py:312
  9.0 2.6 %collective-permute-start.4 = (f32[512,128]{1,0:T(8,128)S(1)}, f32[512,128]{1,0:T(8,128)S(1)}, u32[]{:S(2)}, u32[]{:S(2)}) collective-permute-start(f32[512,128]{1,0:T(8,128)S(1)} %get-tuple-element.41), channel_id=1, source_target_pairs={{0,16},{1,17},{2,18},{3,19},{4,20},{5,21},{6,22},{7,23},{8,24},{9,... | collective-permute-start | bytes 786440 | tf_op jit(solution)/shard_map/ppermute | solution.py:312
  11.5 0.0 copy-done.9
  11.5 0.0 copy-done.3
  11.6 0.0 copy-start.1
  11.6 0.0 copy-start.2
  11.6 0.0 copy-start.4
  11.6 2.8 %shard_map.69.refs_1_.refs_4_.refs_5_.refs_8_ = f32[2048,128]{1,0:T(8,128)S(1)} custom-call(f32[1,128]{1,0:T(1,128)S(1)} %pad_bitcast_fusion.values, s32[64,4096]{1,0:T(8,128)S(1)} %copy-done.3), custom_call_target="tpu_custom_call" | custom-call | tf_op jit(solution)/shard_map/pallas_call | solution.py:179
  14.4 3.4 %shard_map.70 = (f32[64,4096]{1,0:T(8,128)S(1)}, f32[8,128]{1,0:T(8,128)S(1)}) custom-call(f32[64,4096]{1,0:T(8,128)S(1)} %bitcast.16, f32[2048,128]{1,0:T(8,128)S(1)} %shard_map.69.refs_1_.refs_4_.refs_5_.refs_8_, bf16[64,192]{1,0:T(8,128)(2,1)S(1)} %copy-done.4, bf16[256,256]{1,0:T(8,128)(2,1)S(1)} %copy-done.2), custom_call_target="tpu_custom_call" | custom-call | flops 262144 | bytes 262144 | tf_op jit(solution)/shard_map/pallas_call | solution.py:145
  17.9 3.0 %collective-permute-done.1.refs_0_ = f32[512,128]{1,0:T(8,128)S(1)} collective-permute-done((f32[512,128]{1,0:T(8,128)S(1)}, f32[512,128]{1,0:T(8,128)S(1)}, u32[]{:S(2)}, u32[]{:S(2)}) %collective-permute-start.1) | collective-permute-done | bytes 262176 | tf_op jit(solution)/shard_map/ppermute | solution.py:312
  20.8 0.0 collective-permute-done.refs_1_
  20.8 1.7 %collective-permute-start.7 = (f32[32,4096]{1,0:T(8,128)}, f32[32,4096]{1,0:T(8,128)}, u32[]{:S(2)}, u32[]{:S(2)}) collective-permute-start(f32[32,4096]{1,0:T(8,128)} %collective-permute-done.refs_1_), channel_id=1, source_target_pairs={{0,4},{1,5},{2,30},{3,31},{4,8},{5,9},{6,2},{7,3},{8,12},{9,13},{1... | collective-permute-start | bytes 1572872 | tf_op jit(solution)/shard_map/ppermute | solution.py:312
  22.5 0.0 collective-permute-done.5.refs_1_
  22.5 3.6 %shard_map.71 = (f32[64,4096]{1,0:T(8,128)S(1)}, f32[8,128]{1,0:T(8,128)S(1)}) custom-call(f32[64,4096]{1,0:T(8,128)S(1)} %bitcast.17, f32[64,4096]{1,0:T(8,128)S(1)} %collective-permute-done.5.refs_1_, f32[64,4096]{1,0:T(8,128)S(1)} %get-tuple-element.42.refs_2_, f32[8,128]{1,0:T(8,128)S(1)} %get-tuple-element.43.refs_3_, ...), custom_call_target="tpu_custom_call" | custom-call | flops 262144 | bytes 262144 | tf_op jit(solution)/shard_map/pallas_call | solution.py:145
  26.1 0.0 collective-permute-done.4.refs_1_
  26.1 0.0 copy-start.7
  26.1 4.6 %collective-permute-done.3.refs_2_ = f32[32,4096]{1,0:T(8,128)} collective-permute-done((f32[32,4096]{1,0:T(8,128)S(1)}, f32[32,4096]{1,0:T(8,128)}, u32[]{:S(2)}, u32[]{:S(2)}) %collective-permute-start.3) | collective-permute-done | bytes 524320 | tf_op jit(solution)/shard_map/ppermute | solution.py:312
  30.7 1.8 %collective-permute-start.9 = (f32[32,4096]{1,0:T(8,128)}, f32[32,4096]{1,0:T(8,128)}, u32[]{:S(2)}, u32[]{:S(2)}) collective-permute-start(f32[32,4096]{1,0:T(8,128)} %collective-permute-done.3.refs_2_), channel_id=1, source_target_pairs={{0,4},{1,5},{2,30},{3,31},{4,8},{5,9},{6,2},{7,3},{8,12},{9,13},{1... | collective-permute-start | bytes 1572872 | tf_op jit(solution)/shard_map/ppermute | solution.py:312
  32.5 0.0 collective-permute-start.2
  32.5 0.5 collective-permute-start.6
  33.0 4.7 %shard_map.72 = (f32[64,4096]{1,0:T(8,128)S(1)}, f32[8,128]{1,0:T(8,128)S(1)}) custom-call(f32[64,4096]{1,0:T(8,128)S(1)} %bitcast.18, f32[32,4096]{1,0:T(8,128)} %collective-permute-done.refs_1_, f32[32,4096]{1,0:T(8,128)} %collective-permute-done.3.refs_2_, f32[64,4096]{1,0:T(8,128)S(1)} %get-tuple-element.47.refs_3_, ...), custom_call_target="tpu_custom_call" | custom-call | flops 262144 | bytes 262144 | tf_op jit(solution)/shard_map/pallas_call | solution.py:145
  37.7 0.1 collective-permute-done.7.refs_1_
  37.8 0.0 collective-permute-start.8
  37.8 10.6 %collective-permute-done.9.refs_2_ = f32[32,4096]{1,0:T(8,128)} collective-permute-done((f32[32,4096]{1,0:T(8,128)}, f32[32,4096]{1,0:T(8,128)}, u32[]{:S(2)}, u32[]{:S(2)}) %collective-permute-start.9) | collective-permute-done | bytes 524320 | tf_op jit(solution)/shard_map/ppermute | solution.py:312
  48.4 0.0 collective-permute-start.10
  48.4 1.0 collective-permute-start.11
  49.4 4.7 %shard_map.73 = (f32[64,4096]{1,0:T(8,128)S(1)}, f32[8,128]{1,0:T(8,128)S(1)}) custom-call(f32[64,4096]{1,0:T(8,128)S(1)} %bitcast.19, f32[32,4096]{1,0:T(8,128)} %collective-permute-done.7.refs_1_, f32[32,4096]{1,0:T(8,128)} %collective-permute-done.9.refs_2_, f32[64,4096]{1,0:T(8,128)S(1)} %get-tuple-element.51.refs_3_, ...), custom_call_target="tpu_custom_call" | custom-call | flops 262144 | bytes 262144 | tf_op jit(solution)/shard_map/pallas_call | solution.py:145
  54.1 0.0 collective-permute-done.2.refs_1_
  54.1 0.0 collective-permute-done.6.refs_2_
  54.1 0.0 collective-permute-done.8.refs_3_
  54.1 0.0 collective-permute-done.10.refs_4_
  54.1 5.6 %shard_map.74 = (f32[2048,128]{1,0:T(8,128)}, f32[8,128]{1,0:T(8,128)S(1)}) custom-call(f32[64,4096]{1,0:T(8,128)S(1)} %bitcast.20, f32[32,4096]{1,0:T(8,128)} %collective-permute-done.2.refs_1_, f32[32,4096]{1,0:T(8,128)} %collective-permute-done.6.refs_2_, f32[32,4096]{1,0:T(8,128)} %collective-permute-done.8.refs_3_, ...), custom_call_target="tpu_custom_call" | custom-call | flops 262144 | bytes 262144 | tf_op jit(solution)/shard_map/pallas_call | solution.py:145
  59.7 0.0 collective-permute-done.11.refs_2_
  59.8 0.0 copy-start.6
  59.8 0.0 copy-start.8
  59.8 5.4 %all-to-all-start = ((f32[32,64,128]{2,1,0:T(8,128)}), f32[32,64,128]{2,1,0:T(8,128)S(1)}, u32[]{:S(2)}, u32[]{:S(2)}) async-start(f32[32,64,128]{2,1,0:T(8,128)} %bitcast.6), calls=%async_computation | async-start | bytes 2097152 | tf_op jit(solution)/shard_map/all_to_all | solution.py:324
  65.2 1.1 %shard_map.75 = (f32[4,64,128]{2,1,0:T(8,128)S(1)}, f32[4,64,128]{2,1,0:T(8,128)S(1)}, f32[4,64,128]{2,1,0:T(8,128)S(1)}, f32[4,64,128]{2,1,0:T(8,128)S(1)}, f32...) custom-call(s32[3]{0:T(128)S(1)} %pad_add_fusion.place, ...), custom_call_target="tpu_custom_call" | custom-call | tf_op jit(solution)/shard_map/pallas_call | solution.py:248
  66.3 0.3 collective-permute-start.12
  66.6 1.7 %collective-permute-start.13 = (f32[4,64,128]{2,1,0:T(8,128)S(1)}, f32[4,64,128]{2,1,0:T(8,128)S(1)}, u32[]{:S(2)}, u32[]{:S(2)}) collective-permute-start(f32[4,64,128]{2,1,0:T(8,128)S(1)} %get-tuple-element.64), channel_id=1, source_target_pairs={{0,2},{1,3},{2,0},{3,1},{4,6},{5,7},{6,4},{7,5},{8,10},{9,11},{10,... | collective-permute-start | bytes 393224 | tf_op jit(solution)/shard_map/ppermute | solution.py:312
  68.3 0.0 collective-permute-start.14
  68.3 1.7 %collective-permute-start.15 = (f32[4,64,128]{2,1,0:T(8,128)S(1)}, f32[4,64,128]{2,1,0:T(8,128)S(1)}, u32[]{:S(2)}, u32[]{:S(2)}) collective-permute-start(f32[4,64,128]{2,1,0:T(8,128)S(1)} %get-tuple-element.66), channel_id=1, source_target_pairs={{0,4},{1,5},{2,6},{3,7},{4,0},{5,1},{6,2},{7,3},{8,12},{9,13},{10,... | collective-permute-start | bytes 393224 | tf_op jit(solution)/shard_map/ppermute | solution.py:312
  70.0 0.1 collective-permute-start.16
  70.1 0.0 collective-permute-done.12.refs_1_
  70.1 2.6 %collective-permute-start.17 = (f32[4,64,128]{2,1,0:T(8,128)S(1)}, f32[4,64,128]{2,1,0:T(8,128)S(1)}, u32[]{:S(2)}, u32[]{:S(2)}) collective-permute-start(f32[4,64,128]{2,1,0:T(8,128)S(1)} %get-tuple-element.68), channel_id=1, source_target_pairs={{0,6},{1,7},{2,4},{3,5},{4,2},{5,3},{6,0},{7,1},{8,14},{9,15},{10,... | collective-permute-start | bytes 393224 | tf_op jit(solution)/shard_map/ppermute | solution.py:312
  72.7 7.1 %collective-permute-done.13.refs_2_ = f32[4,64,128]{2,1,0:T(8,128)S(1)} collective-permute-done((f32[4,64,128]{2,1,0:T(8,128)S(1)}, f32[4,64,128]{2,1,0:T(8,128)S(1)}, u32[]{:S(2)}, u32[]{:S(2)}) %collective-permute-start.13) | collective-permute-done | bytes 131104 | tf_op jit(solution)/shard_map/ppermute | solution.py:312
  79.8 0.2 collective-permute-start.18
  80.0 2.4 %collective-permute-done.14.refs_3_ = f32[4,64,128]{2,1,0:T(8,128)S(1)} collective-permute-done((f32[4,64,128]{2,1,0:T(8,128)S(1)}, f32[4,64,128]{2,1,0:T(8,128)S(1)}, u32[]{:S(2)}, u32[]{:S(2)}) %collective-permute-start.14) | collective-permute-done | bytes 131104 | tf_op jit(solution)/shard_map/ppermute | solution.py:312
  82.4 0.0 collective-permute-done.15.refs_4_
  82.4 0.1 collective-permute-done.16.refs_5_
  82.5 5.2 %collective-permute-done.17.refs_6_ = f32[4,64,128]{2,1,0:T(8,128)S(1)} collective-permute-done((f32[4,64,128]{2,1,0:T(8,128)S(1)}, f32[4,64,128]{2,1,0:T(8,128)S(1)}, u32[]{:S(2)}, u32[]{:S(2)}) %collective-permute-start.17) | collective-permute-done | bytes 131104 | tf_op jit(solution)/shard_map/ppermute | solution.py:312
  87.7 3.5 %collective-permute-done.18.refs_7_ = f32[4,64,128]{2,1,0:T(8,128)S(1)} collective-permute-done((f32[4,64,128]{2,1,0:T(8,128)S(1)}, f32[4,64,128]{2,1,0:T(8,128)S(1)}, u32[]{:S(2)}, u32[]{:S(2)}) %collective-permute-start.18) | collective-permute-done | bytes 131104 | tf_op jit(solution)/shard_map/ppermute | solution.py:312
  91.3 0.2 all-to-all-done.terms
  91.5 2.2 %shard_map.76 = f32[32,32]{1,0:T(8,128)} custom-call(s32[3]{0:T(128)S(1)} %pad_add_fusion.place, f32[32,64,128]{2,1,0:T(8,128)S(1)} %all-to-all-done.terms, f32[4,64,128]{2,1,0:T(8,128)S(1)} %get-tuple-element.62.refs_0_, f32[4,64,128]{2,1,0:T(8,128)S(1)} %collective-permute-done.12.refs_1_, f32[4,64,128]{2,1,0:T(8,128)S(1)} %collective-permute-done.13.refs_2_, ...), custom_call_target="tpu_custom_call" | custom-call | tf_op jit(solution)/shard_map/pallas_call | solution.py:300
  93.7 3.7 %all-to-all-start.1 = ((f32[32,1,32]{2,1,0:T(1,128)}), f32[32,1,32]{2,1,0:T(1,128)S(1)}, u32[]{:S(2)}, u32[]{:S(2)}) async-start(f32[32,1,32]{2,1,0:T(1,128)} %bitcast.9), calls=%async_computation.1 | async-start | bytes 32768 | tf_op jit(solution)/shard_map/all_to_all | solution.py:324
  97.4 1.8 %copy.8 = f32[64,32,128]{2,1,0:T(8,128)S(1)} copy(f32[64,32,128]{2,0,1:T(8,128)} %bitcast.7) | data formatting | bytes 2097152 | tf_op jit(solution)/shard_map/transpose | solution.py:368
  99.2 1.2 %reshape.26 = f32[1,64,4096]{2,1,0:T(8,128)} reshape(f32[64,32,128]{2,1,0:T(8,128)S(1)} %copy.8) | data formatting | bytes 2097152 | tf_op jit(solution)/shard_map/reshape | solution.py:368
  100.4 4.1 %all-to-all-done.1 = f32[32,1,32]{2,1,0:T(1,128)S(1)} async-done(((f32[32,1,32]{2,1,0:T(1,128)}), f32[32,1,32]{2,1,0:T(1,128)S(1)}, u32[]{:S(2)}, u32[]{:S(2)}) %all-to-all-start.1) | async-done | bytes 4128 | tf_op jit(solution)/shard_map/all_to_all | solution.py:324
  104.5 0.6 reduce_sum.9
  (12 shorter events, 0.0 us)
Async XLA Ops:
  0.6 21.9 %collective-permute-start.5 = (f32[64,4096]{1,0:T(8,128)}, f32[64,4096]{1,0:T(8,128)S(1)}, u32[]{:S(2)}, u32[]{:S(2)}) collective-permute-start(f32[64,4096]{1,0:T(8,128)} %bitcast.14), channel_id=1, source_target_pairs={{0,1},{1,0},{2,3},{3,2},{4,5},{5,4},{6,7},{7,6},{8,9},{9,8},{10,11... | collective-permute-start | bytes 3145736 | tf_op jit(solution)/shard_map/ppermute | solution.py:312
  1.2 1.2 %copy-start = (f32[1,64,4096]{2,1,0:T(8,128)S(1)}, f32[1,64,4096]{2,1,0:T(8,128)}, u32[]{:S(2)}) copy-start(f32[1,64,4096]{2,1,0:T(8,128)} %param.5) | copy-start | bytes 3145732
  2.4 9.1 %copy-start.3 = (s32[64,4096]{1,0:T(8,128)S(1)}, s32[64,4096]{1,0:T(8,128)}, u32[]{:S(2)}) copy-start(s32[64,4096]{1,0:T(8,128)} %index.1) | copy-start | bytes 3145732
  4.2 16.6 %collective-permute-start = (f32[32,4096]{1,0:T(8,128)S(1)}, f32[32,4096]{1,0:T(8,128)}, u32[]{:S(2)}, u32[]{:S(2)}) collective-permute-start(f32[32,4096]{1,0:T(8,128)S(1)} %get-tuple-element.36), channel_id=1, source_target_pairs={{0,2},{1,3},{2,0},{3,1},{4,6},{5,7},{6,4},{7,5},{8,10},{9,11},{10,... | collective-permute-start | bytes 1572872 | tf_op jit(solution)/shard_map/ppermute | solution.py:312
  6.8 23.9 %collective-permute-start.3 = (f32[32,4096]{1,0:T(8,128)S(1)}, f32[32,4096]{1,0:T(8,128)}, u32[]{:S(2)}, u32[]{:S(2)}) collective-permute-start(f32[32,4096]{1,0:T(8,128)S(1)} %get-tuple-element.40), channel_id=1, source_target_pairs={{0,2},{1,3},{2,0},{3,1},{4,6},{5,7},{6,4},{7,5},{8,10},{9,11},{10,... | collective-permute-start | bytes 1572872 | tf_op jit(solution)/shard_map/ppermute | solution.py:312
  6.9 4.6 %copy-start.9 = (f32[32]{0:T(128)S(1)}, f32[32]{0:T(128)}, u32[]{:S(2)}) copy-start(f32[32]{0:T(128)} %param.6) | copy-start | bytes 388
  7.0 13.9 %collective-permute-start.1 = (f32[512,128]{1,0:T(8,128)S(1)}, f32[512,128]{1,0:T(8,128)S(1)}, u32[]{:S(2)}, u32[]{:S(2)}) collective-permute-start(f32[512,128]{1,0:T(8,128)S(1)} %get-tuple-element.37), channel_id=1, source_target_pairs={{0,8},{1,9},{2,10},{3,11},{4,12},{5,13},{6,14},{7,15},{8,0},{9,1},... | collective-permute-start | bytes 786440 | tf_op jit(solution)/shard_map/ppermute | solution.py:312
  9.0 17.2 %collective-permute-start.4 = (f32[512,128]{1,0:T(8,128)S(1)}, f32[512,128]{1,0:T(8,128)S(1)}, u32[]{:S(2)}, u32[]{:S(2)}) collective-permute-start(f32[512,128]{1,0:T(8,128)S(1)} %get-tuple-element.41), channel_id=1, source_target_pairs={{0,16},{1,17},{2,18},{3,19},{4,20},{5,21},{6,22},{7,23},{8,24},{9,... | collective-permute-start | bytes 786440 | tf_op jit(solution)/shard_map/ppermute | solution.py:312
  11.6 2.9 %copy-start.1 = (f32[1,64,4096]{2,1,0:T(8,128)S(1)}, f32[1,64,4096]{2,1,0:T(8,128)}, u32[]{:S(2)}) copy-start(f32[1,64,4096]{2,1,0:T(8,128)} %param.5) | copy-start | bytes 3145732
  11.6 2.9 %copy-start.2 = (bf16[256,256]{1,0:T(8,128)(2,1)S(1)}, bf16[256,256]{1,0:T(8,128)(2,1)}, u32[]{:S(2)}) copy-start(bf16[256,256]{1,0:T(8,128)(2,1)} %constant.57.clone.refs_3_.refs_6_.refs_7_.refs_10_) | copy-start | bytes 393220
  11.6 2.9 %copy-start.4 = (bf16[64,192]{1,0:T(8,128)(2,1)S(1)}, bf16[64,192]{1,0:T(8,128)(2,1)}, u32[]{:S(2)}) copy-start(bf16[64,192]{1,0:T(8,128)(2,1)} %constant.56.clone.refs_2_.refs_5_.refs_6_.refs_9_) | copy-start | bytes 73732
  20.8 5.3 %copy-start.5 = (f32[512,128]{1,0:T(8,128)}, f32[512,128]{1,0:T(8,128)S(1)}, u32[]{:S(2)}) copy-start(f32[512,128]{1,0:T(8,128)S(1)} %collective-permute-done.1.refs_0_) | copy-start | bytes 786436
  20.8 17.0 %collective-permute-start.7 = (f32[32,4096]{1,0:T(8,128)}, f32[32,4096]{1,0:T(8,128)}, u32[]{:S(2)}, u32[]{:S(2)}) collective-permute-start(f32[32,4096]{1,0:T(8,128)} %collective-permute-done.refs_1_), channel_id=1, source_target_pairs={{0,4},{1,5},{2,30},{3,31},{4,8},{5,9},{6,2},{7,3},{8,12},{9,13},{1... | collective-permute-start | bytes 1572872 | tf_op jit(solution)/shard_map/ppermute | solution.py:312
  26.1 11.6 %copy-start.7 = (f32[512,128]{1,0:T(8,128)}, f32[512,128]{1,0:T(8,128)S(1)}, u32[]{:S(2)}) copy-start(f32[512,128]{1,0:T(8,128)S(1)} %collective-permute-done.4.refs_1_) | copy-start | bytes 786436
  30.7 17.6 %collective-permute-start.9 = (f32[32,4096]{1,0:T(8,128)}, f32[32,4096]{1,0:T(8,128)}, u32[]{:S(2)}, u32[]{:S(2)}) collective-permute-start(f32[32,4096]{1,0:T(8,128)} %collective-permute-done.3.refs_2_), channel_id=1, source_target_pairs={{0,4},{1,5},{2,30},{3,31},{4,8},{5,9},{6,2},{7,3},{8,12},{9,13},{1... | collective-permute-start | bytes 1572872 | tf_op jit(solution)/shard_map/ppermute | solution.py:312
  32.5 21.5 %collective-permute-start.2 = (f32[32,4096]{1,0:T(8,128)}, f32[32,4096]{1,0:T(8,128)}, u32[]{:S(2)}, u32[]{:S(2)}) collective-permute-start(f32[32,4096]{1,0:T(8,128)} %collective-permute-done.refs_1_), channel_id=1, source_target_pairs={{0,1},{1,0},{2,3},{3,2},{4,5},{5,4},{6,7},{7,6},{8,9},{9,8},{10,11... | collective-permute-start | bytes 1572872 | tf_op jit(solution)/shard_map/ppermute | solution.py:312
  32.5 21.6 %collective-permute-start.6 = (f32[32,4096]{1,0:T(8,128)}, f32[32,4096]{1,0:T(8,128)}, u32[]{:S(2)}, u32[]{:S(2)}) collective-permute-start(f32[32,4096]{1,0:T(8,128)} %collective-permute-done.3.refs_2_), channel_id=1, source_target_pairs={{0,1},{1,0},{2,3},{3,2},{4,5},{5,4},{6,7},{7,6},{8,9},{9,8},{10,11... | collective-permute-start | bytes 1572872 | tf_op jit(solution)/shard_map/ppermute | solution.py:312
  37.8 16.3 %collective-permute-start.8 = (f32[32,4096]{1,0:T(8,128)}, f32[32,4096]{1,0:T(8,128)}, u32[]{:S(2)}, u32[]{:S(2)}) collective-permute-start(f32[32,4096]{1,0:T(8,128)} %collective-permute-done.7.refs_1_), channel_id=1, source_target_pairs={{0,1},{1,0},{2,3},{3,2},{4,5},{5,4},{6,7},{7,6},{8,9},{9,8},{10,11... | collective-permute-start | bytes 1572872 | tf_op jit(solution)/shard_map/ppermute | solution.py:312
  48.4 5.7 %collective-permute-start.10 = (f32[32,4096]{1,0:T(8,128)}, f32[32,4096]{1,0:T(8,128)}, u32[]{:S(2)}, u32[]{:S(2)}) collective-permute-start(f32[32,4096]{1,0:T(8,128)} %collective-permute-done.9.refs_2_), channel_id=1, source_target_pairs={{0,1},{1,0},{2,3},{3,2},{4,5},{5,4},{6,7},{7,6},{8,9},{9,8},{10,11... | collective-permute-start | bytes 1572872 | tf_op jit(solution)/shard_map/ppermute | solution.py:312
  48.4 11.4 %collective-permute-start.11 = (f32[512,128]{1,0:T(8,128)}, f32[512,128]{1,0:T(8,128)}, u32[]{:S(2)}, u32[]{:S(2)}) collective-permute-start(f32[512,128]{1,0:T(8,128)} %get-tuple-element.56), channel_id=1, source_target_pairs={{0,24},{1,25},{2,26},{3,27},{4,28},{5,29},{6,30},{7,31},{8,16},{9,... | collective-permute-start | bytes 786440 | tf_op jit(solution)/shard_map/ppermute | solution.py:312
  59.8 5.5 %copy-start.6 = (f32[512,128]{1,0:T(8,128)S(1)}, f32[512,128]{1,0:T(8,128)}, u32[]{:S(2)}) copy-start(f32[512,128]{1,0:T(8,128)} %copy-done.5) | copy-start | bytes 786436
  59.8 5.5 %copy-start.8 = (f32[512,128]{1,0:T(8,128)S(1)}, f32[512,128]{1,0:T(8,128)}, u32[]{:S(2)}) copy-start(f32[512,128]{1,0:T(8,128)} %copy-done.7) | copy-start | bytes 786436
  59.8 31.7 %all-to-all-start = ((f32[32,64,128]{2,1,0:T(8,128)}), f32[32,64,128]{2,1,0:T(8,128)S(1)}, u32[]{:S(2)}, u32[]{:S(2)}) async-start(f32[32,64,128]{2,1,0:T(8,128)} %bitcast.6), calls=%async_computation | async-start | bytes 2097152 | tf_op jit(solution)/shard_map/all_to_all | solution.py:324
  66.3 3.8 %collective-permute-start.12 = (f32[4,64,128]{2,1,0:T(8,128)S(1)}, f32[4,64,128]{2,1,0:T(8,128)S(1)}, u32[]{:S(2)}, u32[]{:S(2)}) collective-permute-start(f32[4,64,128]{2,1,0:T(8,128)S(1)} %get-tuple-element.63), channel_id=1, source_target_pairs={{0,1},{1,0},{2,3},{3,2},{4,5},{5,4},{6,7},{7,6},{8,9},{9,8},{10,11... | collective-permute-start | bytes 393224 | tf_op jit(solution)/shard_map/ppermute | solution.py:312
  66.6 13.2 %collective-permute-start.13 = (f32[4,64,128]{2,1,0:T(8,128)S(1)}, f32[4,64,128]{2,1,0:T(8,128)S(1)}, u32[]{:S(2)}, u32[]{:S(2)}) collective-permute-start(f32[4,64,128]{2,1,0:T(8,128)S(1)} %get-tuple-element.64), channel_id=1, source_target_pairs={{0,2},{1,3},{2,0},{3,1},{4,6},{5,7},{6,4},{7,5},{8,10},{9,11},{10,... | collective-permute-start | bytes 393224 | tf_op jit(solution)/shard_map/ppermute | solution.py:312
  68.3 14.1 %collective-permute-start.14 = (f32[4,64,128]{2,1,0:T(8,128)S(1)}, f32[4,64,128]{2,1,0:T(8,128)S(1)}, u32[]{:S(2)}, u32[]{:S(2)}) collective-permute-start(f32[4,64,128]{2,1,0:T(8,128)S(1)} %get-tuple-element.65), channel_id=1, source_target_pairs={{0,3},{1,2},{2,1},{3,0},{4,7},{5,6},{6,5},{7,4},{8,11},{9,10},{10,... | collective-permute-start | bytes 393224 | tf_op jit(solution)/shard_map/ppermute | solution.py:312
  68.3 14.1 %collective-permute-start.15 = (f32[4,64,128]{2,1,0:T(8,128)S(1)}, f32[4,64,128]{2,1,0:T(8,128)S(1)}, u32[]{:S(2)}, u32[]{:S(2)}) collective-permute-start(f32[4,64,128]{2,1,0:T(8,128)S(1)} %get-tuple-element.66), channel_id=1, source_target_pairs={{0,4},{1,5},{2,6},{3,7},{4,0},{5,1},{6,2},{7,3},{8,12},{9,13},{10,... | collective-permute-start | bytes 393224 | tf_op jit(solution)/shard_map/ppermute | solution.py:312
  70.0 12.5 %collective-permute-start.16 = (f32[4,64,128]{2,1,0:T(8,128)S(1)}, f32[4,64,128]{2,1,0:T(8,128)S(1)}, u32[]{:S(2)}, u32[]{:S(2)}) collective-permute-start(f32[4,64,128]{2,1,0:T(8,128)S(1)} %get-tuple-element.67), channel_id=1, source_target_pairs={{0,5},{1,4},{2,7},{3,6},{4,1},{5,0},{6,3},{7,2},{8,13},{9,12},{10,... | collective-permute-start | bytes 393224 | tf_op jit(solution)/shard_map/ppermute | solution.py:312
  70.1 17.6 %collective-permute-start.17 = (f32[4,64,128]{2,1,0:T(8,128)S(1)}, f32[4,64,128]{2,1,0:T(8,128)S(1)}, u32[]{:S(2)}, u32[]{:S(2)}) collective-permute-start(f32[4,64,128]{2,1,0:T(8,128)S(1)} %get-tuple-element.68), channel_id=1, source_target_pairs={{0,6},{1,7},{2,4},{3,5},{4,2},{5,3},{6,0},{7,1},{8,14},{9,15},{10,... | collective-permute-start | bytes 393224 | tf_op jit(solution)/shard_map/ppermute | solution.py:312
  79.8 11.4 %collective-permute-start.18 = (f32[4,64,128]{2,1,0:T(8,128)S(1)}, f32[4,64,128]{2,1,0:T(8,128)S(1)}, u32[]{:S(2)}, u32[]{:S(2)}) collective-permute-start(f32[4,64,128]{2,1,0:T(8,128)S(1)} %get-tuple-element.69), channel_id=1, source_target_pairs={{0,7},{1,6},{2,5},{3,4},{4,3},{5,2},{6,1},{7,0},{8,15},{9,14},{10,... | collective-permute-start | bytes 393224 | tf_op jit(solution)/shard_map/ppermute | solution.py:312
  93.7 10.8 %all-to-all-start.1 = ((f32[32,1,32]{2,1,0:T(1,128)}), f32[32,1,32]{2,1,0:T(1,128)S(1)}, u32[]{:S(2)}, u32[]{:S(2)}) async-start(f32[32,1,32]{2,1,0:T(1,128)} %bitcast.9), calls=%async_computation.1 | async-start | bytes 32768 | tf_op jit(solution)/shard_map/all_to_all | solution.py:324
